TPU v7x, 128 devices: a whole 4x4x4 slice. The times are simulated.
128 devices in a mesh: seq: 32 (over y, z, core), head: 4 (over x).
Axes of the slice: x: 4, y: 4, z: 4, core: 2. Of those that a mesh axis runs over, the one named last changes fastest.
Arguments:
- tokens: bfloat16 [32768, 2048], P(('seq', 'head')), may hold values from -6 to 6
- in_weight: bfloat16 [2048, 16, 160], P(None, 'head'), may hold values from -0.125 to 0.125
- conv_kernel: float32 [3, 16, 160], P(None, 'head'), may hold values from -2.4 to 2.4
- grad_out: bfloat16 [32768, 2048], P('seq', 'head'), may hold values from -6 to 6
Outputs:
- attended: bfloat16 [32768, 2048], P('seq', 'head')
- grad_input: bfloat16 [32768, 2048], P(('seq', 'head'))
- grad_weight: float32 [2048, 16, 160], P('seq', 'head')
All inputs are finite; a program needn't handle non-finite values.
Results may differ from a plain program's by a relative error of at most 0.009.
Values may be sent and summed in bfloat16 or wider, within the bound.
A program may use at most 192 MiB of HBM per device.

v0:
```python
import math

import jax
import jax.numpy as jnp
from jax import lax
from jax.sharding import PartitionSpec as P

F = 16
E = 128
BLK = 256
FEAT = 273
CHAN = 160


exact_mode = lax.Precision.HIGHEST


def passed_along(block, axis, distance):
    devices = range(lax.axis_size(axis))
    route = [(i - distance, i) for i in devices if i - distance in devices]
    return lax.ppermute(block, axis, route)


def carried_in(part, axis, combine, identity, reverse):
    count = lax.axis_size(axis)
    place = lax.axis_index(axis)
    ahead = count - 1 - place if reverse else place
    gathered = jax.tree.map(lambda a: lax.all_gather(a, axis), part)
    state = jax.tree.map(lambda a, e: jnp.zeros_like(a) + jnp.asarray(e, a.dtype), part, identity)

    def one(step, state):
        source = count - 1 - step if reverse else step
        return combine(
            state, jax.tree.map(lambda a: lax.dynamic_index_in_dim(a, source, 0, False), gathered)
        )

    return lax.fori_loop(0, ahead, one, state)


def features(vector):
    leading = vector.shape[:-1]
    square = (vector[..., :, None] * vector[..., None, :]).reshape(leading + (F * F,))
    constant = jnp.ones(leading + (1,), vector.dtype)
    return jnp.concatenate(
        [constant, vector * F ** (-0.25), square * (1.0 / math.sqrt(2.0 * F))], -1
    )


def feature_grad(vector, grad_phi):
    linear = grad_phi[..., 1 : 1 + F]
    square = grad_phi[..., 1 + F :].reshape(vector.shape[:-1] + (F, F))
    symmetric = square + jnp.swapaxes(square, -1, -2)
    return linear * F ** (-0.25) + jnp.einsum(
        "...ij,...j->...i", symmetric, vector, precision=exact_mode
    ) * (1.0 / math.sqrt(2.0 * F))


def add_pair(earlier, later_part):
    return (earlier[0] + later_part[0], earlier[1] + later_part[1])


def before(pieces):
    running = jnp.cumsum(pieces, 0)
    return jnp.concatenate([jnp.zeros_like(pieces[:1]), running[:-1]], 0)


def after(pieces):
    return jnp.flip(before(jnp.flip(pieces, 0)), 0)


def local(tokens, in_weight, conv_kernel, grad_out):
    f32 = jnp.float32
    bf16 = jnp.bfloat16
    head_count = in_weight.shape[1]
    gathered = lax.all_gather(tokens, "head", axis=0, tiled=True)
    row_count = gathered.shape[0]
    blocks = row_count // BLK
    projected = jnp.einsum("td,dhc->thc", gathered, in_weight, preferred_element_type=f32)
    front_rows = passed_along(projected[row_count - 2 :], "seq", 1)
    extended = jnp.concatenate([front_rows, projected], 0)
    conved = (
        conv_kernel[0] * extended[2:]
        + conv_kernel[1] * extended[1:-1]
        + conv_kernel[2] * extended[:-2]
    )
    conved = conved.reshape(blocks, BLK, head_count, CHAN)
    query_in = conved[..., :F]
    key_in = conved[..., F : 2 * F]
    values = conved[..., 2 * F :].astype(bf16)
    feat_q = features(query_in).astype(bf16)
    feat_k = features(key_in).astype(bf16)
    block_u = jnp.einsum("nshp,nshe->nhpe", feat_k, values, preferred_element_type=f32)
    block_m = jnp.sum(feat_k, axis=1, dtype=f32)
    empty = (jnp.zeros((head_count, FEAT, E), f32), jnp.zeros((head_count, FEAT), f32))
    start_u, start_m = carried_in(
        (jnp.sum(block_u, 0), jnp.sum(block_m, 0)), "seq", add_pair, empty, False
    )
    state_in = start_u[None] + before(block_u)
    key_total = start_m[None] + before(block_m)
    state_b = state_in.astype(bf16)
    causal = lax.broadcasted_iota(jnp.int32, (BLK, BLK), 0) >= lax.broadcasted_iota(
        jnp.int32, (BLK, BLK), 1
    )
    scores = jnp.einsum("nthp,nshp->nhts", feat_q, feat_k, preferred_element_type=f32)
    scores = jnp.where(causal, scores, 0.0)
    scores_b = scores.astype(bf16)
    numerator = jnp.einsum("nthp,nhpe->nthe", feat_q, state_b, preferred_element_type=f32)
    numerator = numerator + jnp.einsum(
        "nhts,nshe->nthe", scores_b, values, preferred_element_type=f32
    )
    denominator = jnp.einsum(
        "nthp,nhp->nth", feat_q, key_total, precision=exact_mode, preferred_element_type=f32
    )
    denominator = denominator + jnp.swapaxes(jnp.sum(scores, -1), 1, 2)
    attended = (numerator / denominator[..., None]).astype(bf16).reshape(row_count, head_count * E)
    cotangent = grad_out.reshape(blocks, BLK, head_count, E).astype(f32)
    grad_num = (cotangent / denominator[..., None]).astype(bf16)
    grad_den = -jnp.sum(cotangent * numerator, -1) / (denominator * denominator)
    block_w = jnp.einsum("nthp,nthe->nhpe", feat_q, grad_num, preferred_element_type=f32)
    block_r = jnp.einsum(
        "nthp,nth->nhp", feat_q, grad_den, precision=exact_mode, preferred_element_type=f32
    )
    end_w, end_r = carried_in(
        (jnp.sum(block_w, 0), jnp.sum(block_r, 0)), "seq", add_pair, empty, True
    )
    later_state = end_w[None] + after(block_w)
    later_total = end_r[None] + after(block_r)
    later_b = later_state.astype(bf16)
    mixing = jnp.einsum("nthe,nshe->nhts", grad_num, values, preferred_element_type=f32)
    mixing = mixing + jnp.swapaxes(grad_den, 1, 2)[..., None]
    mixing_b = jnp.where(causal, mixing, 0.0).astype(bf16)
    grad_fq = jnp.einsum("nthe,nhpe->nthp", grad_num, state_b, preferred_element_type=f32)
    grad_fq = grad_fq + grad_den[..., None] * key_total[:, None]
    grad_fq = grad_fq + jnp.einsum("nhts,nshp->nthp", mixing_b, feat_k, preferred_element_type=f32)
    grad_fk = jnp.einsum("nshe,nhpe->nshp", values, later_b, preferred_element_type=f32)
    grad_fk = grad_fk + later_total[:, None]
    grad_fk = grad_fk + jnp.einsum("nhts,nthp->nshp", mixing_b, feat_q, preferred_element_type=f32)
    grad_values = jnp.einsum("nshp,nhpe->nshe", feat_k, later_b, preferred_element_type=f32)
    grad_values = grad_values + jnp.einsum(
        "nhts,nthe->nshe", scores_b, grad_num, preferred_element_type=f32
    )
    grad_query = feature_grad(query_in, grad_fq)
    grad_key = feature_grad(key_in, grad_fk)
    grad_conved = jnp.concatenate([grad_query, grad_key, grad_values], -1).reshape(
        row_count, head_count, CHAN
    )
    back_rows = passed_along(grad_conved[:2], "seq", -1)
    padded_grad = jnp.concatenate([grad_conved, back_rows], 0)
    grad_proj = (
        conv_kernel[0] * padded_grad[:-2]
        + conv_kernel[1] * padded_grad[1:-1]
        + conv_kernel[2] * padded_grad[2:]
    )
    grad_proj = grad_proj.astype(bf16)
    weight_term = jnp.einsum("td,thc->dhc", gathered, grad_proj, preferred_element_type=f32)
    grad_weight = lax.psum_scatter(weight_term, "seq", scatter_dimension=0, tiled=True)
    partial_value = jnp.einsum("thc,dhc->td", grad_proj, in_weight, preferred_element_type=f32)
    grad_input = lax.psum_scatter(partial_value, "head", scatter_dimension=0, tiled=True).astype(
        bf16
    )
    return (attended, grad_input, grad_weight)


def solution(mesh):
    placed = (
        P(("seq", "head"), None),
        P(None, "head", None),
        P(None, "head", None),
        P("seq", "head"),
    )
    return jax.shard_map(
        local,
        mesh=mesh,
        in_specs=placed,
        out_specs=(P("seq", "head"), P(("seq", "head"), None), P("seq", "head", None)),
        check_vma=False,
    )
```

profile of v0, /device:TPU:0, one launch (start us, length us, event | category | flops | bytes accessed | tf_op | source)
XLA Modules:
  0.0 616.4 jit_solution(16251997606087477909)
XLA Ops:
  8.0 52.4 %all-gather.10.cloned.1.call-done = bf16[1024,2048]{1,0:T(8,128)(2,1)} async-done(((bf16[256,2048]{1,0:T(8,128)(2,1)}), bf16[1024,2048]{1,0:T(8,128)(2,1)}) %all-gather.10.cloned.1.call-update) | async-done | bytes 4194320 | tf_op jit(solution)/shard_map/all_gather | solution.py:75
  60.4 4.7 fusion.53
  68.3 3.2 fusion.14
  71.5 4.2 reshape.51
  76.8 2.0 slice.88
  79.4 3.3 fusion.42
  82.8 2.7 reshape.56
  85.6 2.9 copy.85
  88.5 3.4 convert_reduce_fusion
  94.8 34.6 %all-gather.4 = f32[32,4,273]{2,1,0:T(4,128)} all-gather(f32[1,4,273]{2,1,0:T(4,128)S(1)} %bitcast.162), channel_id=3, replica_groups=mesh['seq'=32,'head'=4] {'seq'}, dimensions={0}, use_global_device_ids=true | all-gather | bytes 144144 | tf_op jit(solution)/shard_map/all_gather | solution.py:28
  132.2 4.2 select_reduce_fusion
  136.4 28.7 %all-gather.12.cloned.1.call-done = f32[128,273,128]{2,1,0:T(8,128)} async-done(((f32[4,273,128]{2,1,0:T(8,128)}), f32[128,273,128]{2,1,0:T(8,128)}) %all-gather.12.cloned.1.call-update) | async-done | bytes 17891344 | tf_op jit(solution)/shard_map/all_gather | solution.py:28
  166.1 3.4 fusion.26
  174.9 3.2 fusion.43
  179.2 2.5 select_convert_fusion
  185.7 2.5 slice.93
  189.3 2.0 fusion.28
  191.4 3.2 rev.14
  198.1 82.9 %all-gather.5 = f32[32,4,273]{2,1,0:T(4,128)} all-gather(f32[1,4,273]{2,1,0:T(4,128)S(1)} %bitcast.163), channel_id=5, replica_groups=mesh['seq'=32,'head'=4] {'seq'}, dimensions={0}, use_global_device_ids=true | all-gather | bytes 144144 | tf_op jit(solution)/shard_map/all_gather | solution.py:28
  281.0 5.0 fusion.7
  287.8 2.2 fusion.21
  290.0 21.7 %all-gather.14.cloned.1.call-done = f32[128,273,128]{2,1,0:T(8,128)} async-done(((f32[4,273,128]{2,1,0:T(8,128)}), f32[128,273,128]{2,1,0:T(8,128)}) %all-gather.14.cloned.1.call-update) | async-done | bytes 17891344 | tf_op jit(solution)/shard_map/all_gather | solution.py:28
  311.8 58.4 %while.27 = (s32[]{:T(128)}, f32[4,273,128]{2,1,0:T(8,128)S(1)}, f32[4,273]{1,0:T(4,128)S(1)}, s32[]{:T(128)}, f32[32,4,273,128]{3,2,1,0:T(8,128)}, /*index=5*/f...) while((s32[]{:T(128)}, f32[4,273,128]{2,1,0:T(8,128)S(1)}, f32[4,273]{1,0:T(4,128)S(1)}, ...), condition=%wide.region_12.13_spmd, body=%wide.region_11.12_spmd.sunk | while | flops 140874 | bytes 1690571 | solution.py:37
  376.5 5.2 fusion.4
  390.4 4.7 fusion.8
  395.1 8.8 %copy.99 = f32[2048,4,160]{2,1,0:T(4,128)} copy(f32[2048,4,160]{0,2,1:T(8,128)} %fusion.8) | data formatting | bytes 10485760 | tf_op jit(solution)/shard_map/td,thc->dhc/dot_general | solution.py:155
  404.0 7.1 %convolution_bitcast_fusion = f32[1024,2048]{1,0:T(8,128)} fusion(bf16[1024,4,160]{0,2,1:T(8,128)(2,1)} %copy-done.28, bf16[2048,4,160]{0,2,1:T(8,128)(2,1)S(1)} %copy-done), kind=kOutput, calls=%fused_computation.9 | convolution fusion | flops 2684354560 | bytes 12320768 | tf_op jit(solution)/shard_map/thc,dhc->td/dot_general | solution.py:157
  413.0 2.4 copy.84
  415.4 2.4 copy.165
  417.7 106.6 %all-reduce.7.cloned.1.call-done = f32[2048,4,160]{2,1,0:T(4,128)} async-done(((f32[2048,4,160]{2,1,0:T(4,128)}), f32[2048,4,160]{2,1,0:T(4,128)}) %all-reduce.7.cloned.1.call-update) | async-done | bytes 5242896
  526.0 80.6 %reduce-scatter.2.cloned.1.call-done = f32[256,2048]{1,0:T(8,128)} async-done(((f32[1024,2048]{1,0:T(8,128)}), f32[256,2048]{1,0:T(8,128)}) %reduce-scatter.2.cloned.1.call-update) | async-done | bytes 2097168 | tf_op jit(solution)/shard_map/reduce_scatter | solution.py:158
  606.6 2.7 convert_element_type.46
  (235 shorter events, 104.7 us)
Async XLA Ops:
  7.2 53.2 %copy-start = (bf16[2048,4,160]{0,2,1:T(8,128)(2,1)S(1)}, bf16[2048,4,160]{0,2,1:T(8,128)(2,1)}, u32[]{:S(2)}) copy-start(bf16[2048,4,160]{0,2,1:T(8,128)(2,1)} %param.9) | copy-start | bytes 7864324
  7.2 53.2 %all-gather.10.cloned.1.call-start = ((), (), s32[]{:S(2)}) async-start(), calls=%async_computation.1 | async-start | bytes 5242880 | tf_op jit(solution)/shard_map/all_gather | solution.py:75
  7.9 157.2 %all-gather.12.cloned.1.call-start = ((), (), s32[]{:S(2)}) async-start(), calls=%async_computation.3 | async-start | bytes 18923520 | tf_op jit(solution)/shard_map/all_gather | solution.py:28
  60.4 6.7 %copy-start.51 = (f32[3,4,160]{2,1,0:T(4,128)S(1)}, f32[3,4,160]{2,1,0:T(4,128)}, u32[]{:S(2)}) copy-start(f32[3,4,160]{2,1,0:T(4,128)} %param.10) | copy-start | bytes 23044
  65.3 3.0 collective-permute-start
  67.2 63.7 %copy-start.47 = (bf16[273]{0:T(512)(128)(2,1)}, bf16[273]{0:T(512)(128)(2,1)S(1)}, u32[]{:S(2)}) copy-start(bf16[273]{0:T(512)(128)(2,1)S(1)} %pad.10.clone) | copy-start | bytes 1642
  78.8 4.0 copy-start.10
  78.8 52.1 %copy-start.29 = (bf16[4,256,4,16]{1,3,2,0:T(8,128)(2,1)}, bf16[4,256,4,16]{1,3,2,0:T(8,128)(2,1)S(1)}, u32[]{:S(2)}) copy-start(bf16[4,256,4,16]{1,3,2,0:T(8,128)(2,1)S(1)} %get-tuple-element.160) | copy-start | bytes 393220
  82.8 228.9 %all-gather.14.cloned.1.call-start = ((), (), s32[]{:S(2)}) async-start(), calls=%async_computation.4 | async-start | bytes 18923520 | tf_op jit(solution)/shard_map/all_gather | solution.py:28
  88.5 4.0 copy-start.26
  93.5 38.7 %copy-start.3 = (bf16[4,256,4,16,16]{1,4,3,2,0:T(8,128)(2,1)S(1)}, bf16[4,256,4,16,16]{1,4,3,2,0:T(8,128)(2,1)}, u32[]{:S(2)}) copy-start(bf16[4,256,4,16,16]{1,4,3,2,0:T(8,128)(2,1)} %copy-done.2) | copy-start | bytes 6291460
  129.5 6.9 %copy-start.33 = (bf16[4,256,4,16]{1,3,2,0:T(8,128)(2,1)}, bf16[4,256,4,16]{1,3,2,0:T(8,128)(2,1)S(1)}, u32[]{:S(2)}) copy-start(bf16[4,256,4,16]{1,3,2,0:T(8,128)(2,1)S(1)} %get-tuple-element.158) | copy-start | bytes 393220
  165.2 4.3 copy-start.19
  165.2 4.3 copy-start.22
  165.2 4.3 copy-start.34
  165.3 4.3 copy-start.48
  178.2 346.1 %all-reduce.7.cloned.1.call-start = ((), (), s32[]{:S(2)}) async-start(), calls=%async_computation.5 | async-start | bytes 16777216
  185.7 3.6 copy-start.1
  185.7 3.6 copy-start.20
  185.7 3.6 copy-start.35
  196.4 84.6 %copy-start.25 = (f32[4,256,4,16]{1,3,2,0:T(8,128)S(1)}, f32[4,256,4,16]{1,3,2,0:T(8,128)}, u32[]{:S(2)}) copy-start(f32[4,256,4,16]{1,3,2,0:T(8,128)} %copy-done.24) | copy-start | bytes 786436
  196.5 84.5 %copy-start.9 = (f32[4,256,4,256]{1,3,2,0:T(8,128)S(1)}, f32[4,256,4,256]{1,3,2,0:T(8,128)}, u32[]{:S(2)}) copy-start(f32[4,256,4,256]{1,3,2,0:T(8,128)} %slice.93) | copy-start | bytes 12582916
  281.0 6.8 %copy-start.15 = (bf16[4,256,4,128]{1,3,2,0:T(8,128)(2,1)S(1)}, bf16[4,256,4,128]{1,3,2,0:T(8,128)(2,1)}, u32[]{:S(2)}) copy-start(bf16[4,256,4,128]{1,3,2,0:T(8,128)(2,1)} %copy-done.13) | copy-start | bytes 3145732
  281.0 6.8 %copy-start.17 = (bf16[4,4,256,256]{2,3,1,0:T(8,128)(2,1)S(1)}, bf16[4,4,256,256]{2,3,1,0:T(8,128)(2,1)}, u32[]{:S(2)}) copy-start(bf16[4,4,256,256]{2,3,1,0:T(8,128)(2,1)} %get-tuple-element.174) | copy-start | bytes 6291460
  376.4 5.3 copy-start.5
  376.4 5.3 copy-start.27
  376.4 5.3 copy-start.31
  383.8 3.6 copy-start.42
  383.8 3.6 copy-start.44
  383.8 3.6 copy-start.46
  383.8 3.5 collective-permute-start.1
  403.9 202.7 %reduce-scatter.2.cloned.1.call-start = ((), (), s32[]{:S(2)}) async-start(), calls=%async_computation.2 | async-start | bytes 10485760 | tf_op jit(solution)/shard_map/reduce_scatter | solution.py:158
  (29 other events, 54.8 us)
Sparse Core Ops, SparseCore 0:
  9.7 50.6 all-gather.9
  82.9 82.2 all-gather.11
  178.3 133.3 all-gather.13
  404.1 120.2 all-reduce.6
  526.8 79.8 reduce-scatter.1
where the time goes:
time: 627 us; the launch traced here: 616 us
  waiting for transfers between devices  294 us (47%)
  blocking collectives  118 us (19%)
  other arithmetic  91.4 us (15%)
  local copies, waits for them, and re-layouts  48.5 us (8%)
  matrix products  45.3 us (7%)
  between operations  15.8 us (3%)
    all_gather x2, blocking collectives, carried_in(): gathered = jax.tree.map(lambda a: lax.all_gather(a, axis), part)  118 us
    unnamed x6, waiting for transfers between devices  107 us
    reduce_scatter x1, waiting for transfers between devices, local(): lax.psum_scatter(partial_value, 'head', scatter_dimension=0, tiled=True)  80.6 us
    add x62, other arithmetic, add_pair(): return (earlier[0] + later_part[0], earlier[1] + later_part[1])  58.1 us
    all_gather x1, waiting for transfers between devices, local(): gathered = lax.all_gather(tokens, 'head', axis=0, tiled=True)  52.4 us
    all_gather x2, waiting for transfers between devices, carried_in(): gathered = jax.tree.map(lambda a: lax.all_gather(a, axis), part)  50.4 us
    unnamed x112, local copies, waits for them, and re-layouts  14 us
  transfers between devices with their start and end apart: 7, of which 7 were waited for; matrix products, arithmetic and copies ran while one was open for 9% of the time, Pallas kernels for 0%

commit v1 on v0

v1 whole, which is shorter than its diff:
```python
import functools
import math

import jax
import jax.numpy as jnp
import numpy as np
from jax import lax
from jax.experimental import pallas as pl
from jax.experimental.pallas import tpu as pltpu
from jax.sharding import PartitionSpec as P

F = 16
E = 128
BLK = 256
CHAN = 160
FS = 160
NF = 1 + F + F * (F + 1) // 2
KAPPA = 32.0 ** -0.25
f32 = jnp.float32
bf16 = jnp.bfloat16
NN = (((1,), (0,)), ((), ()))
NT = (((1,), (1,)), ((), ()))


def dot(a, b, dims=NN):
    return lax.dot_general(a, b, dims, preferred_element_type=f32)


def bf_parts(value, count):
    parts = []
    rest = np.float64(value)
    for _ in range(count):
        part = np.float64(np.asarray(rest, dtype=jnp.bfloat16))
        parts.append(part)
        rest = rest - part
    return parts


def selection(weighted):
    sel = np.zeros((2 * FS, 3 * F), np.float64)
    sel[0, 32] = 1.0
    sel[FS, 32] = 1.0
    for i in range(F):
        row = 1 + i
        sel[row, i] = sel[row, F + i] = 1.0
        for c, part in enumerate(bf_parts(0.5 / KAPPA, 3)):
            sel[FS + row, 32 + c] = part
    row = 1 + F
    for i in range(F):
        for j in range(i, F):
            first = 2.0 if (weighted and j > i) else 1.0
            sel[row, i] = sel[row, F + i] = first
            sel[FS + row, j] = sel[FS + row, F + j] = 1.0
            row += 1
    return sel


def gradient_map(weighted):
    sel = selection(weighted)
    return np.concatenate([sel[:FS, :F].T, sel[FS:, :F].T], 1)


def remote(src, dst, send, recv, **where):
    return pltpu.make_async_remote_copy(
        src_ref=src,
        dst_ref=dst,
        send_sem=send,
        recv_sem=recv,
        device_id=where,
        device_id_type=pl.DeviceIdType.MESH,
    )


def greet(sem, **where):
    pl.semaphore_signal(sem, inc=1, device_id=where, device_id_type=pl.DeviceIdType.MESH)


def gather_kernel(nx, ns, tok, w, gt, p, g, hal, s_own, r_own, s_fwd, r_fwd, s_hal, r_hal):
    x = lax.axis_index("head")
    s = lax.axis_index("seq")
    left, right, opp = (x + nx - 1) % nx, (x + 1) % nx, (x + 2) % nx
    prev, after = (s + ns - 1) % ns, (s + 1) % ns
    rows, depth = tok.shape
    ch = rows // 4
    bar = pltpu.get_barrier_semaphore()
    greet(bar, head=left)
    greet(bar, head=right)
    greet(bar, seq=prev, head=nx - 1)

    @pl.when(x == nx - 1)
    def _():
        for j in range(nx):
            greet(bar, seq=after, head=j)

    pl.semaphore_wait(bar, jnp.where(x == nx - 1, 3 + nx, 3))

    def part(c):
        return pl.ds(c * ch, ch)

    def own(way, c):
        return remote(
            tok.at[part(c)],
            g.at[x, part(c)],
            s_own.at[way, c],
            r_own.at[way, c],
            head=right if way == 0 else left,
        )

    def arrives(way, c):
        slot = left if way == 0 else right
        return remote(
            tok.at[part(c)], g.at[slot, part(c)], s_own.at[way, c], r_own.at[way, c], head=left
        )

    def forward(way, c):
        slot = left if way == 0 else right
        return remote(
            g.at[slot, part(c)],
            g.at[slot, part(c)],
            s_fwd.at[way, c % 2],
            r_fwd.at[way, c % 2],
            head=right if way == 0 else left,
        )

    def arrives_far(way, c):
        return remote(
            tok.at[part(c)], g.at[opp, part(c)], s_fwd.at[way, c % 2], r_fwd.at[way, c % 2], head=left
        )

    def halo(j):
        return remote(tok.at[pl.ds(rows - 16, 16)], hal, s_hal.at[j], r_hal, seq=after, head=j)

    for c in range(4):
        own(0, c).start()
        own(1, (c + 2) % 4).start()
        if c == 0:

            @pl.when(x == nx - 1)
            def _():
                for j in range(nx):
                    halo(j).start()

    def process(slot, src):
        base = pl.multiple_of(slot * rows, rows)
        p[pl.ds(16 + base, rows), :] = dot(src[...], w[...])

        def turn(i, carry):
            at = pl.ds(pl.multiple_of(i * 256, 256), 256)
            gt[at, pl.ds(base, rows)] = src[:, at].T
            return carry

        lax.fori_loop(0, depth // 256, turn, 0)

    process(x, tok)
    for c in range(2):
        arrives(0, c).wait_recv()
        forward(0, c).start()
        arrives(1, c + 2).wait_recv()
        forward(1, c + 2).start()
    halo(0).wait_recv()
    head_rows = dot(hal[...], w[...])
    p[0:16, :] = jnp.where(s == 0, 0.0, head_rows)
    arrives(0, 2).wait_recv()
    arrives(0, 3).wait_recv()
    process(left, g.at[left])
    arrives(1, 0).wait_recv()
    arrives(1, 1).wait_recv()
    process(right, g.at[right])
    for c in range(2):
        arrives_far(0, c).wait_recv()
        arrives_far(1, c + 2).wait_recv()
    process(opp, g.at[opp])
    for c in range(4):
        own(0, c).wait_send()
        own(1, c).wait_send()
    for c in range(2):
        forward(0, c).wait_send()
        forward(1, c + 2).wait_send()

    @pl.when(x == nx - 1)
    def _():
        for j in range(nx):
            halo(j).wait_send()


def gathered_projection(tokens, w, nx, ns):
    rows, depth = tokens.shape
    width = w.shape[1]
    vm = pl.BlockSpec(memory_space=pltpu.VMEM)
    dma = pltpu.SemaphoreType.DMA
    return pl.pallas_call(
        functools.partial(gather_kernel, nx, ns),
        out_shape=(
            jax.ShapeDtypeStruct((depth, nx * rows), bf16),
            jax.ShapeDtypeStruct((16 + nx * rows, width), f32),
        ),
        in_specs=[vm] * 2,
        out_specs=(vm, vm),
        scratch_shapes=[
            pltpu.VMEM((nx, rows, depth), bf16),
            pltpu.VMEM((16, depth), bf16),
            dma((2, 4)),
            dma((2, 4)),
            dma((2, 2)),
            dma((2, 2)),
            dma((nx,)),
            dma(()),
        ],
        compiler_params=pltpu.CompilerParams(
            collective_id=0, has_side_effects=True, vmem_limit_bytes=56 * 2**20
        ),
    )(tokens, w)


def mixer_kernel(
    ga, gb, nh, nb,
    p, taps, go, selq, selk, gmq, gmk,
    att, gp, hc,
    qkt, vaug, fqt, fkt, fq, fk, ub, nin, sco, scot, gna, run, st, pfk, pgv, gc,
    loc, r1, tot, r2, out, res, s1, q1, s2, q2, s3, q3,
):
    s = lax.axis_index("seq")
    me_a, me_b = s % ga, s // ga
    piece = loc.shape[1] // ga
    hb_count = nh * nb
    bar = pltpu.get_barrier_semaphore()
    for k in range(1, ga):
        greet(bar, seq=me_b * ga + (me_a + k) % ga)
    for k in range(1, gb):
        greet(bar, seq=((me_b + k) % gb) * ga + me_a)

    lane = lax.broadcasted_iota(jnp.int32, (BLK, BLK), 1)
    sub = lax.broadcasted_iota(jnp.int32, (BLK, BLK), 0)
    frow = lax.broadcasted_iota(jnp.int32, (FS, E), 0)

    def rows_of(a):
        return pl.ds(pl.multiple_of(a * piece, 16), piece)

    def first(d, k):
        a = (me_a + k) % ga
        return remote(
            loc.at[d, rows_of(a)], r1.at[d, me_a], s1.at[d, k], q1.at[d, k], seq=me_b * ga + a
        )

    def second(d, k):
        b = (me_b + k) % gb
        return remote(tot.at[d], r2.at[d, me_b], s2.at[d, k], q2.at[d, k], seq=b * ga + me_a)

    def third(d, k):
        a = (me_a + k) % ga
        return remote(
            out.at[d, a], res.at[d, rows_of(me_a)], s3.at[d, k], q3.at[d, k], seq=me_b * ga + a
        )

    def exchange_first(d):
        for k in range(1, ga):
            first(d, k).start()
        r1[d, me_a] = loc[d, rows_of(me_a), :]

    def exchange_second(d):
        for k in range(1, ga):
            a = (me_a + ga - k) % ga
            remote(
                loc.at[d, rows_of(a)], r1.at[d, a], s1.at[d, k], q1.at[d, k], seq=s
            ).wait_recv()
        total = jnp.zeros((piece, E), f32)
        for a in range(ga):
            total = total + r1[d, a].astype(f32)
        tot[d] = total
        for k in range(1, gb):
            second(d, k).start()

    def exchange_third(d):
        for k in range(1, gb):
            b = (me_b + gb - k) % gb
            remote(tot.at[d], r2.at[d, b], s2.at[d, k], q2.at[d, k], seq=s).wait_recv()
        r2[d, me_b] = tot[d]
        total = jnp.zeros((piece, E), f32)
        for b in range(gb):
            ahead = b < me_b if d == 0 else b > me_b
            total = total + jnp.where(ahead, r2[d, b], 0.0)
        for step in range(ga):
            a = step if d == 0 else ga - 1 - step
            out[d, a] = total.astype(bf16)
            total = total + r1[d, a].astype(f32)
        for k in range(1, ga):
            third(d, k).start()
        res[d, rows_of(me_a), :] = out[d, me_a]

    def exchange_done(d):
        for k in range(1, ga):
            a = (me_a + ga - k) % ga
            remote(
                out.at[d, a], res.at[d, rows_of(a)], s3.at[d, k], q3.at[d, k], seq=s
            ).wait_recv()

    def pack(d, h, whole):
        column = jnp.concatenate([whole[:, E:], jnp.zeros((2 * E - FS, E), f32)], 0)
        line = column.T[0:1, :]
        body = jnp.where(frow == NF, line[:, :E], jnp.where(frow == NF + 1, line[:, E:], whole[:, :E]))
        loc[d, h * FS : (h + 1) * FS, :] = body.astype(bf16)

    def unpack(d, h):
        body = res[d, h * FS : (h + 1) * FS, :].astype(f32)
        line = jnp.concatenate([body[NF : NF + 1, :], body[NF + 1 : NF + 2, :]], 1)
        column = jnp.broadcast_to(line, (E, 2 * E)).T[:FS, :]
        return jnp.concatenate([jnp.where(frow < NF, body, 0.0), column], 1)

    def factors(u, sel):
        high = u.astype(bf16)
        low = (u - high.astype(f32)).astype(bf16)
        stack = jnp.concatenate([high, low, jnp.ones((F, BLK), bf16)], 0)
        both = dot(sel[...], stack)
        return both[:FS], both[FS:]

    def block_at(b):
        return pl.ds(pl.multiple_of(b * BLK, BLK), BLK)

    def forward_block(b, carry):
        ext = p[pl.ds(pl.multiple_of(b * BLK, BLK), BLK + 16), :]
        conv = taps[0:1, :] * ext[16:] + taps[1:2, :] * ext[15:-1] + taps[2:3, :] * ext[14:-2]
        turned = conv[:, nh * E :].T
        qkt[:, block_at(b)] = turned
        for h in range(nh):
            i = b * nh + h
            va = jnp.concatenate(
                [conv[:, h * E : (h + 1) * E].astype(bf16), jnp.ones((BLK, E), bf16)], 1
            )
            vaug[i] = va
            first_q, second_q = factors(turned[2 * F * h : 2 * F * h + F], selq)
            first_k, second_k = factors(turned[2 * F * h + F : 2 * F * (h + 1)], selk)
            q = (first_q * second_q).astype(bf16)
            k = (first_k * second_k).astype(bf16)
            fqt[i] = q
            fkt[i] = k
            fq[i] = q.T
            fk[i] = k.T
            ub[i] = dot(k, va)
        return carry

    lax.fori_loop(0, nb, forward_block, 0)
    for h in range(nh):
        whole = ub[h]
        for b in range(1, nb):
            whole = whole + ub[b * nh + h]
        pack(0, h, whole)
    pl.semaphore_wait(bar, ga - 1 + gb - 1)
    exchange_first(0)

    def inside(i, carry):
        score = jnp.where(sub >= lane, dot(fq[i], fkt[i]), 0.0).astype(bf16)
        sco[i] = score
        scot[i] = jnp.where(lane >= sub, dot(fk[i], fqt[i]), 0.0).astype(bf16)
        nin[i] = dot(score, vaug[i])
        return carry

    third_of = hb_count // 4
    lax.fori_loop(0, third_of, inside, 0)
    exchange_second(0)
    lax.fori_loop(third_of, 2 * third_of, inside, 0)
    exchange_third(0)
    lax.fori_loop(2 * third_of, hb_count, inside, 0)
    exchange_done(0)
    for h in range(nh):
        run[h] = unpack(0, h)

    ones = jnp.ones((2 * E, E), bf16)

    def attend_block(b, carry):
        for h in range(nh):
            i = b * nh + h
            state = run[h]
            state_b = state.astype(bf16)
            run[h] = state + ub[i]
            both = dot(fq[i], state_b) + nin[i]
            num = both[:, :E]
            inv = 1.0 / both[:, E:]
            mean = num * inv
            at = (block_at(b), slice(h * E, (h + 1) * E))
            att[at] = mean.astype(bf16)
            scaled = go[at].astype(f32) * inv
            product = scaled * mean
            high = product.astype(bf16)
            low = (product - high.astype(f32)).astype(bf16)
            slope = dot(jnp.concatenate([high, low], 1), ones) * (-1.0 / E)
            ga_b = jnp.concatenate([scaled.astype(bf16), slope.astype(bf16)], 1)
            gna[i] = ga_b
            st[i] = state_b
            ub[i] = dot(fqt[i], ga_b)
        return carry

    lax.fori_loop(0, nb, attend_block, 0)
    for h in range(nh):
        whole = ub[h]
        for b in range(1, nb):
            whole = whole + ub[b * nh + h]
        pack(1, h, whole)
    exchange_first(1)

    def feature_gradient(u, sel, gm, grad):
        one, two = factors(u, sel)
        stack = jnp.concatenate([(grad * two).astype(bf16), (grad * one).astype(bf16)], 0)
        return dot(gm[...], stack)

    def inside_back(i, carry):
        b, h = i // nh, i % nh
        ga_b = gna[i]
        va = vaug[i]
        mix = jnp.where(sub >= lane, dot(ga_b, va, NT), 0.0).astype(bf16)
        mixt = jnp.where(lane >= sub, dot(va, ga_b, NT), 0.0).astype(bf16)
        gfq = dot(st[i], ga_b, NT) + dot(fkt[i], mixt)
        at = (pl.ds(pl.multiple_of(h * 2 * F, 2 * F), F), block_at(b))
        gq = feature_gradient(qkt[at], selq, gmq, gfq)
        pfk[i] = dot(fqt[i], mix)
        qkt[at] = gq
        pgv[i] = dot(scot[i], ga_b[:, :E])
        return carry

    lax.fori_loop(0, third_of, inside_back, 0)
    exchange_second(1)
    lax.fori_loop(third_of, 2 * third_of, inside_back, 0)
    exchange_third(1)
    lax.fori_loop(2 * third_of, hb_count, inside_back, 0)
    exchange_done(1)
    for h in range(nh):
        run[h] = unpack(1, h)

    def back_block(step, carry):
        b = nb - 1 - step
        for h in range(nh):
            i = b * nh + h
            state = run[h]
            state_b = state.astype(bf16)
            run[h] = state + ub[i]
            gfk = dot(state_b, vaug[i], NT) + pfk[i]
            at = (slice(2 * F * h + F, 2 * F * (h + 1)), block_at(b))
            qkt[at] = feature_gradient(qkt[at], selk, gmk, gfk)
            gc[block_at(b), h * E : (h + 1) * E] = dot(fk[i], state_b[:, :E]) + pgv[i]
        gc[block_at(b), nh * E :] = qkt[:, block_at(b)].T
        return carry

    gc[nb * BLK :, :] = jnp.zeros((16, gc.shape[1]), f32)
    lax.fori_loop(0, nb, back_block, 0)

    def spread(b, carry):
        ext = gc[pl.ds(pl.multiple_of(b * BLK, BLK), BLK + 16), :]
        grad = taps[0:1, :] * ext[:BLK] + taps[1:2, :] * ext[1 : BLK + 1] + taps[2:3, :] * ext[2 : BLK + 2]
        gp[block_at(b), :] = grad.astype(bf16)
        return carry

    lax.fori_loop(0, nb, spread, 0)
    edge = jnp.concatenate([jnp.zeros((16, gc.shape[1]), f32), gc[0:16, :]], 0)
    hc[...] = (taps[1:2, :] * edge[1:17] + taps[2:3, :] * edge[2:18]).astype(bf16)

    for d in range(2):
        for k in range(1, ga):
            first(d, k).wait_send()
            third(d, k).wait_send()
        for k in range(1, gb):
            second(d, k).wait_send()


def mixer(p, taps, go, ga, gb):
    rows = go.shape[0]
    nh = go.shape[1] // E
    nb = rows // BLK
    n = nh * nb
    width = p.shape[1]
    piece = nh * FS // ga
    vm = pl.BlockSpec(memory_space=pltpu.VMEM)
    dma = pltpu.SemaphoreType.DMA
    consts = [
        jnp.asarray(selection(True), bf16),
        jnp.asarray(selection(False), bf16),
        jnp.asarray(gradient_map(True), bf16),
        jnp.asarray(gradient_map(False), bf16),
    ]
    return pl.pallas_call(
        functools.partial(mixer_kernel, ga, gb, nh, nb),
        out_shape=(
            jax.ShapeDtypeStruct((rows, nh * E), bf16),
            jax.ShapeDtypeStruct((rows, width), bf16),
            jax.ShapeDtypeStruct((16, width), bf16),
        ),
        in_specs=[vm] * 7,
        out_specs=(vm, vm, vm),
        scratch_shapes=[
            pltpu.VMEM((nh * 2 * F, rows), f32),
            pltpu.VMEM((n, BLK, 2 * E), bf16),
            pltpu.VMEM((n, FS, BLK), bf16),
            pltpu.VMEM((n, FS, BLK), bf16),
            pltpu.VMEM((n, BLK, FS), bf16),
            pltpu.VMEM((n, BLK, FS), bf16),
            pltpu.VMEM((n, FS, 2 * E), f32),
            pltpu.VMEM((n, BLK, 2 * E), f32),
            pltpu.VMEM((n, BLK, BLK), bf16),
            pltpu.VMEM((n, BLK, BLK), bf16),
            pltpu.VMEM((n, BLK, 2 * E), bf16),
            pltpu.VMEM((nh, FS, 2 * E), f32),
            pltpu.VMEM((n, FS, 2 * E), bf16),
            pltpu.VMEM((n, FS, BLK), f32),
            pltpu.VMEM((n, BLK, E), f32),
            pltpu.VMEM((rows + 16, width), f32),
            pltpu.VMEM((2, nh * FS, E), bf16),
            pltpu.VMEM((2, ga, piece, E), bf16),
            pltpu.VMEM((2, piece, E), f32),
            pltpu.VMEM((2, gb, piece, E), f32),
            pltpu.VMEM((2, ga, piece, E), bf16),
            pltpu.VMEM((2, nh * FS, E), bf16),
            dma((2, ga)),
            dma((2, ga)),
            dma((2, gb)),
            dma((2, gb)),
            dma((2, ga)),
            dma((2, ga)),
        ],
        compiler_params=pltpu.CompilerParams(
            collective_id=1, has_side_effects=True, vmem_limit_bytes=60 * 2**20
        ),
    )(p, taps, go, *consts)


def tail_kernel(
    nx, ny, nz,
    gp, hc, gt, wf_hbm,
    gi, gw,
    wf, ga, g3, hal, gwb, rp, t, r2a, r2b, ua, ub, r3a, r3b,
    sw, sx, qx, sh, qh, sp, qp, s2a, q2a, s2b, q2b, s3a, q3a, s3b, q3b,
):
    x = lax.axis_index("head")
    s = lax.axis_index("seq")
    ns = ny * nz * 2
    core, z, y = s % 2, (s // 2) % nz, s // (2 * nz)
    rows = ga.shape[1]
    bar = pltpu.get_barrier_semaphore()

    def at_seq(yy, zz, cc):
        return (yy * nz + zz) * 2 + cc

    sibling = at_seq(y, z, 1 - core)
    prev, after = (s + ns - 1) % ns, (s + 1) % ns
    for k in range(1, nx):
        greet(bar, head=(x + k) % nx)
    greet(bar, seq=prev)
    greet(bar, seq=after)
    greet(bar, seq=sibling)
    for k in range(1, nz):
        greet(bar, seq=at_seq(y, (z + k) % nz, core))
    for k in range(1, ny):
        greet(bar, seq=at_seq((y + k) % ny, z, core))
    weights = [pltpu.make_async_copy(wf_hbm.at[j], wf.at[j], sw.at[j]) for j in range(nx)]
    for copy in weights:
        copy.start()
    pl.semaphore_wait(bar, nx - 1 + 3 + nz - 1 + ny - 1)

    edge = remote(hc, hal, sh, qh, seq=prev)
    edge.start()

    def block(j):
        return pl.ds(pl.multiple_of(j * rows, rows), rows)

    def over(k, last):
        j = (x + k) % nx
        src = g3 if last else gp.at[block(j)]
        return remote(src, ga.at[x], sx.at[k], qx.at[k], head=j)

    for k in (1, 3, 2):

        @pl.when((x + k) % nx != nx - 1)
        def _():
            over(k, False).start()

    edge.wait_recv()
    low = gp[(nx - 1) * rows :, :]
    g3[...] = low
    fixed = low[rows - 16 :].astype(f32) + jnp.where(s == ns - 1, 0.0, hal[...].astype(f32))
    g3[rows - 16 :, :] = fixed.astype(bf16)
    for k in (1, 3, 2):

        @pl.when((x + k) % nx == nx - 1)
        def _():
            over(k, True).start()

    @pl.when(x == nx - 1)
    def _():
        ga[x] = g3[...]

    @pl.when(x != nx - 1)
    def _():
        ga[x] = gp[block(x), :]

    pieces = ny * nz
    height = gwb.shape[2]

    def pair(j):
        return remote(gwb.at[j, 1 - core], rp.at[j], sp.at[j], qp.at[j], seq=sibling)

    per = 256 // (2 * height)
    early = (nx - 1) * rows

    def weight_step(i, carry):
        at = pl.ds(pl.multiple_of(i * 256, 256), 256)
        left = gt[at, :]
        whole = dot(left[:, :early], gp[:early, :]) + dot(left[:, early:], g3[...])
        whole = whole.astype(bf16).reshape(per, 2, height, whole.shape[1])
        for q in range(per):
            gwb[i * per + q] = whole[q]
            pair(i * per + q).start()
        return carry

    lax.fori_loop(0, pieces // per, weight_step, 0)

    def pair_sum(j, carry):
        remote(gwb.at[j, core], rp.at[j], sp.at[j], qp.at[j], seq=sibling).wait_recv()
        t[j // nz, j % nz] = (gwb[j, core].astype(f32) + rp[j].astype(f32)).astype(bf16)
        return carry

    lax.fori_loop(0, pieces, pair_sum, 0)
    half = height // 2
    low_half, high_half = pl.ds(0, half), pl.ds(half, half)

    def go_2a(k):
        to = (z + k) % nz
        return remote(
            t.at[:, to, low_half], r2a.at[k], s2a.at[k], q2a.at[k], seq=at_seq(y, to, core)
        )

    def go_2b(k):
        to = (y + k) % ny
        return remote(
            t.at[to, :, high_half], r2b.at[k], s2b.at[k], q2b.at[k], seq=at_seq(to, z, core)
        )

    def go_3a(k):
        to = (y + k) % ny
        return remote(ua.at[to], r3a.at[k], s3a.at[k], q3a.at[k], seq=at_seq(to, z, core))

    def go_3b(k):
        to = (z + k) % nz
        return remote(ub.at[to], r3b.at[k], s3b.at[k], q3b.at[k], seq=at_seq(y, to, core))

    for k in range(1, max(ny, nz)):
        if k < nz:
            go_2a(k).start()
        if k < ny:
            go_2b(k).start()

    for k in (1, 3, 2):
        j = (x + nx - k) % nx
        remote(g3, ga.at[j], sx.at[k], qx.at[k], head=j).wait_recv()
    for copy in weights:
        copy.wait()

    def input_step(i, carry):
        at = pl.ds(pl.multiple_of(i * 256, 256), 256)
        total = dot(ga[0], wf[0, at, :], NT)
        for j in range(1, nx):
            total = total + dot(ga[j], wf[j, at, :], NT)
        gi[:, at] = total.astype(bf16)
        return carry

    steps = gi.shape[1] // 256
    lax.fori_loop(0, steps // 2, input_step, 0)

    for k in range(1, nz):
        go_2a(k).wait_recv()
    for k in range(1, ny):
        go_2b(k).wait_recv()
    for i in range(ny):
        total = t[i, z, 0:half].astype(f32)
        for k in range(1, nz):
            total = total + r2a[k, i].astype(f32)
        ua[i] = total.astype(bf16)
    for i in range(nz):
        total = t[y, i, half:].astype(f32)
        for k in range(1, ny):
            total = total + r2b[k, i].astype(f32)
        ub[i] = total.astype(bf16)
    for k in range(1, max(ny, nz)):
        if k < ny:
            go_3a(k).start()
        if k < nz:
            go_3b(k).start()
    lax.fori_loop(steps // 2, steps, input_step, 0)
    total = ua[y].astype(f32)
    for k in range(1, ny):
        go_3a(k).wait_recv()
        total = total + r3a[k].astype(f32)
    gw[0:half, :] = total
    total = ub[z].astype(f32)
    for k in range(1, nz):
        go_3b(k).wait_recv()
        total = total + r3b[k].astype(f32)
    gw[half:, :] = total

    edge.wait_send()
    for k in range(1, nx):
        over(k, False).wait_send()
    for j in range(pieces):
        pair(j).wait_send()
    for k in range(1, nz):
        go_2a(k).wait_send()
        go_3b(k).wait_send()
    for k in range(1, ny):
        go_2b(k).wait_send()
        go_3a(k).wait_send()


def tail(gp, hc, gt, wf, nx, ny, nz):
    width = gp.shape[1]
    rows = gp.shape[0] // nx
    depth = gt.shape[0]
    ns = ny * nz * 2
    height = depth // ns
    half = height // 2
    vm = pl.BlockSpec(memory_space=pltpu.VMEM)
    dma = pltpu.SemaphoreType.DMA
    return pl.pallas_call(
        functools.partial(tail_kernel, nx, ny, nz),
        out_shape=(
            jax.ShapeDtypeStruct((rows, depth), bf16),
            jax.ShapeDtypeStruct((height, width), f32),
        ),
        in_specs=[vm] * 3 + [pl.BlockSpec(memory_space=pl.ANY)],
        out_specs=(vm, vm),
        scratch_shapes=[
            pltpu.VMEM((nx, depth, width), bf16),
            pltpu.VMEM((nx, rows, width), bf16),
            pltpu.VMEM((rows, width), bf16),
            pltpu.VMEM((16, width), bf16),
            pltpu.VMEM((ny * nz, 2, height, width), bf16),
            pltpu.VMEM((ny * nz, height, width), bf16),
            pltpu.VMEM((ny, nz, height, width), bf16),
            pltpu.VMEM((nz, ny, half, width), bf16),
            pltpu.VMEM((ny, nz, half, width), bf16),
            pltpu.VMEM((ny, half, width), bf16),
            pltpu.VMEM((nz, half, width), bf16),
            pltpu.VMEM((ny, half, width), bf16),
            pltpu.VMEM((nz, half, width), bf16),
            dma((nx,)),
            dma((nx,)),
            dma((nx,)),
            dma(()),
            dma(()),
            dma((ny * nz,)),
            dma((ny * nz,)),
            dma((nz,)),
            dma((nz,)),
            dma((ny,)),
            dma((ny,)),
            dma((ny,)),
            dma((ny,)),
            dma((nz,)),
            dma((nz,)),
        ],
        compiler_params=pltpu.CompilerParams(
            collective_id=2, has_side_effects=True, vmem_limit_bytes=60 * 2**20
        ),
    )(gp, hc, gt, wf)


def ordered(weight):
    lead = weight.shape[0]
    return jnp.concatenate(
        [weight[:, :, 2 * F :].reshape(lead, -1), weight[:, :, : 2 * F].reshape(lead, -1)], 1
    )


def local(nx, ny, nz, tokens, in_weight, conv_kernel, grad_out):
    depth, nh, _ = in_weight.shape
    ns = ny * nz * 2
    w = ordered(in_weight)
    taps = ordered(conv_kernel)
    scale = jnp.where(jnp.arange(taps.shape[1]) < nh * E, 1.0, KAPPA).astype(f32)
    taps = jnp.pad(taps * scale, ((0, 5), (0, 0)))
    height = depth // ns
    own = lax.dynamic_slice_in_dim(w, lax.axis_index("seq") * height, height, 0)
    wf = lax.all_gather(own, ("head", "seq"), axis=0, tiled=True).reshape(nx, depth, -1)
    gt, p = gathered_projection(tokens, w, nx, ns)
    att, gp, hc = mixer(p, taps, grad_out, nz * 2, ny)
    gi, gw = tail(gp, hc, gt, wf, nx, ny, nz)
    gw = jnp.concatenate(
        [gw[:, nh * E :].reshape(height, nh, 2 * F), gw[:, : nh * E].reshape(height, nh, E)], 2
    )
    return att, gi, gw


def solution(mesh):
    nx, ns = mesh.shape["head"], mesh.shape["seq"]
    ny = math.isqrt(ns // 2)
    nz = ns // 2 // ny
    placed = (
        P(("seq", "head"), None),
        P(None, "head", None),
        P(None, "head", None),
        P("seq", "head"),
    )
    return jax.shard_map(
        functools.partial(local, nx, ny, nz),
        mesh=mesh,
        in_specs=placed,
        out_specs=(P("seq", "head"), P(("seq", "head"), None), P("seq", "head", None)),
        check_vma=False,
    )
```

time: 627 us -> 165 us (0.26); the launches traced: 616 us -> 164 us
  waiting for transfers between devices: 294 us -> 0.04 us
  Pallas kernels: 0 us -> 136 us
  blocking collectives: 118 us -> 0 us
  other arithmetic: 91.4 us -> 3.28 us
  matrix products: 45.3 us -> 0 us
  local copies, waits for them, and re-layouts: 48.5 us -> 11.1 us
    pallas_call x0 -> x3, Pallas kernels: none -> 136 us  [the longest x1 52.8 us: gathered_projection(): pl.pallas_call(functools.partial(gather_kernel, nx, ns), out_shape=(jax.S...]
    all_gather x2 -> x0, blocking collectives: 118 us -> none  [carried_in(): gathered = jax.tree.map(lambda a: lax.all_gather(a, axis), part)]
    unnamed x6 -> x1, waiting for transfers between devices: 107 us -> 0.02 us
    all_gather x3 -> x1, waiting for transfers between devices: 103 us -> 0.02 us  [local(): lax.all_gather(own, ('head', 'seq'), axis=0, tiled=True)]
    reduce_scatter x1 -> x0, waiting for transfers between devices: 80.6 us -> none  [local(): lax.psum_scatter(partial_value, 'head', scatter_dimension=0, tiled=True)]
    add x67 -> x0, other arithmetic: 64 us -> none  [the longest x62 58.1 us: add_pair(): return (earlier[0] + later_part[0], earlier[1] + later_part[1])]
    dot_general x16 -> x0, matrix products: 40.6 us -> none  [the longest x1 7.12 us: local(): jnp.einsum('thc,dhc->td', grad_proj, in_weight, preferred_element_type=f32)]
    unnamed x112 -> x10, local copies, waits for them, and re-layouts: 14 us -> 2.03 us
  transfers between devices with their start and end apart: 7 -> 1, of which waited for: 7 -> 0; matrix products, arithmetic and copies ran while one was open for 9% -> 2% of each run, Pallas kernels for 0% -> 64%
where the time goes in v1:
time: 165 us; the launch traced here: 164 us
  Pallas kernels  136 us (82%)
  between operations  14.2 us (9%)
  local copies, waits for them, and re-layouts  11.1 us (7%)
  other arithmetic  3.28 us (2%)
    pallas_call x1, Pallas kernels, gathered_projection(): pl.pallas_call(functools.partial(gather_kernel, nx, ns), out_shape=(jax.S...  52.8 us
    pallas_call x1, Pallas kernels, mixer(): pl.pallas_call(functools.partial(mixer_kernel, ga, gb, nh, nb), out_shape...  52.3 us
    pallas_call x1, Pallas kernels, tail(): pl.pallas_call(functools.partial(tail_kernel, nx, ny, nz), out_shape=(jax...  30.6 us
  transfers between devices with their start and end apart: 1, of which 0 were waited for; matrix products, arithmetic and copies ran while one was open for 2% of the time, Pallas kernels for 64%

profile of v1, /device:TPU:0, one launch (start us, length us, event | category | flops | bytes accessed | tf_op | source)
XLA Modules:
  0.0 164.4 jit_solution(17767757147476858708)
XLA Ops:
  7.2 0.0 slice-start
  7.2 0.0 all-gather.2.cloned.1.call-start
  7.2 3.2 %slice.18 = bf16[2048,4,128]{0,2,1:T(8,128)(2,1)} slice(bf16[2048,4,160]{0,2,1:T(8,128)(2,1)} %param.9), slice={[0:2048], [0:4], [32:160]} | slice | bytes 4194304 | tf_op jit(solution)/shard_map/slice | solution.py:765
  10.4 0.0 slice-done
  10.4 0.3 copy.14
  10.7 0.0 slice-start.1
  10.7 0.0 copy-start.2
  10.7 2.9 %copy.17 = bf16[2048,512]{1,0:T(8,128)(2,1)S(1)} copy(bf16[2048,512]{0,1:T(8,128)(2,1)} %bitcast.10) | data formatting | bytes 4194304 | tf_op jit(solution)/shard_map/reshape | solution.py:765
  13.6 0.6 fusion
  14.3 0.0 all-gather.2.cloned.1.call-update
  14.3 0.0 slice-done.1
  14.3 0.1 reshape.35
  14.4 0.0 copy-done.2
  14.4 0.1 slice_bitcast_fusion
  14.5 1.7 %pad_maximum_fusion.w = bf16[2048,640]{1,0:T(8,128)(2,1)} fusion(bf16[2048,128]{1,0:T(8,128)(2,1)S(1)} %copy.14, bf16[2048,512]{1,0:T(8,128)(2,1)S(1)} %copy.17), kind=kLoop, calls=%fused_computation.1 | loop fusion | flops 5242880 | bytes 5242880 | tf_op jit(solution)/shard_map/concatenate | solution.py:764
  16.2 52.8 %shard_map.103 = (bf16[2048,1024]{1,0:T(8,128)(2,1)}, f32[1040,640]{1,0:T(8,128)}) custom-call(bf16[256,2048]{1,0:T(8,128)(2,1)} %tok.1, bf16[2048,640]{1,0:T(8,128)(2,1)} %pad_maximum_fusion.w), custom_call_target="tpu_custom_call" | custom-call | tf_op jit(solution)/shard_map/pallas_call | solution.py:191
  69.1 0.6 pad.4.taps
  69.7 52.3 %shard_map.104 = (bf16[1024,512]{1,0:T(8,128)(2,1)}, bf16[1024,640]{1,0:T(8,128)(2,1)}, bf16[16,640]{1,0:T(8,128)(2,1)}) custom-call(f32[1040,640]{1,0:T(8,128)} %get-tuple-element.10.p, f32[8,640]{1,0:T(8,128)} %pad.4.taps, bf16[1024,512]{1,0:T(8,128)(2,1)} %go.1, bf16[320,48]{1,0:T(8,128)(2,1)} %constant.28.clone.selq, ...), custom_call_target="tpu_custom_call" | custom-call | tf_op jit(solution)/shard_map/pallas_call | solution.py:478
  122.0 0.0 all-gather.2.cloned.1.call-done
  122.0 0.0 copy-start
  122.0 30.6 %shard_map.105 = (bf16[256,2048]{1,0:T(8,128)(2,1)}, f32[64,640]{1,0:T(8,128)}) custom-call(bf16[1024,640]{1,0:T(8,128)(2,1)} %get-tuple-element.12.gp, bf16[16,640]{1,0:T(8,128)(2,1)} %get-tuple-element.13.hc, bf16[2048,1024]{1,0:T(8,128)(2,1)} %get-tuple-element.14.gt, bf16[4,2048,640]{2,1,0:T(8,128)(2,1)} %bitcast.9), custom_call_target="tpu_custom_call" | custom-call | tf_op jit(solution)/shard_map/pallas_call | solution.py:718
  152.6 0.0 copy-start.1
  152.6 1.0 slice.23
  153.6 0.8 slice.22
  154.4 0.1 copy.15
  154.5 0.1 copy.16
  154.7 0.9 pad_maximum_fusion.1
  155.6 0.0 copy-done
  155.6 1.0 copy.23
  156.5 0.0 copy-done.1
  156.5 1.0 copy.24
  (4 shorter events, 0.1 us)
Async XLA Ops:
  7.2 3.3 %slice-start = ((bf16[2048,4,160]{0,2,1:T(8,128)(2,1)}), bf16[2048,4,32]{0,2,1:T(8,128)(2,1)S(1)}, s32[]{:S(2)}) async-start(bf16[2048,4,160]{0,2,1:T(8,128)(2,1)} %param.9), calls=%async_computation.1 | async-start | bytes 1048576 | tf_op jit(solution)/shard_map/slice | solution.py:765
  7.2 114.8 %all-gather.2.cloned.1.call-start = ((), (), s32[]{:S(2)}) async-start(), calls=%async_computation | async-start | bytes 10567680 | tf_op jit(solution)/shard_map/all_gather | solution.py:778
  10.7 3.6 %slice-start.1 = ((f32[3,4,160]{2,1,0:T(4,128)}), f32[3,4,32]{2,1,0:T(4,128)S(1)}, s32[]{:S(2)}) async-start(f32[3,4,160]{2,1,0:T(4,128)} %param.10), calls=%async_computation.2 | async-start | bytes 12288 | tf_op jit(solution)/shard_map/slice | solution.py:765
  10.7 3.7 %copy-start.2 = (f32[3,4,160]{2,1,0:T(4,128)S(1)}, f32[3,4,160]{2,1,0:T(4,128)}, u32[]{:S(2)}) copy-start(f32[3,4,160]{2,1,0:T(4,128)} %param.10) | copy-start | bytes 23044
  122.0 33.6 %copy-start = (bf16[1024,512]{1,0:T(8,128)(2,1)S(1)}, bf16[1024,512]{1,0:T(8,128)(2,1)}, u32[]{:S(2)}) copy-start(bf16[1024,512]{1,0:T(8,128)(2,1)} %get-tuple-element.20) | copy-start | bytes 3145732
  152.6 3.9 %copy-start.1 = (bf16[256,2048]{1,0:T(8,128)(2,1)S(1)}, bf16[256,2048]{1,0:T(8,128)(2,1)}, u32[]{:S(2)}) copy-start(bf16[256,2048]{1,0:T(8,128)(2,1)} %get-tuple-element.21) | copy-start | bytes 3145732
Sparse Core Ops, SparseCore 0:
  14.4 77.9 all-gather.1

commit v2 on v1

--- a/solution.py
+++ b/solution.py
@@ -75,24 +75,160 @@
     pl.semaphore_signal(sem, inc=1, device_id=where, device_id_type=pl.DeviceIdType.MESH)
 
 
-def gather_kernel(nx, ns, tok, w, gt, p, g, hal, s_own, r_own, s_fwd, r_fwd, s_hal, r_hal):
+def weight_gather(nx, ny, nz, x, y, z, core, w, wf, sems):
+    s1, q1, sa, qa, sb, qb, sc, qc, sd, qd, se, qe, so = sems
+    chan, depth = w.shape
+    half = chan // 2
+    quarter = half // 2
+    col = depth // (ny * nz)
+    rows_c = pl.ds(pl.multiple_of(core * half, 16), half)
+    rows_a = pl.ds(pl.multiple_of(core * half, 16), quarter)
+    rows_b = pl.ds(pl.multiple_of(core * half + quarter, 16), quarter)
+    far = pl.ds(1, nx - 1)
+
+    def cols(yy, zz):
+        return pl.ds(pl.multiple_of((yy * nz + zz) * col, 128), col)
+
+    def row_of(yy):
+        return pl.ds(pl.multiple_of(yy * nz * col, 128), nz * col)
+
+    def at_seq(yy, zz, cc):
+        return (yy * nz + zz) * 2 + cc
+
+    mine = cols(y, z)
+
+    def spread_x(k):
+        return remote(
+            w.at[rows_c, mine], wf.at[nx - k, rows_c, mine], s1.at[k], q1.at[k], head=(x + k) % nx
+        )
+
+    def a_z(k):
+        here = wf.at[far, rows_a, mine]
+        return remote(here, here, sa.at[k], qa.at[k], seq=at_seq(y, (z + k) % nz, core))
+
+    def b_y(k):
+        here = wf.at[far, rows_b, mine]
+        return remote(here, here, sb.at[k], qb.at[k], seq=at_seq((y + k) % ny, z, core))
+
+    def a_y(k):
+        here = wf.at[far, rows_a, row_of(y)]
+        return remote(here, here, sc.at[k], qc.at[k], seq=at_seq((y + k) % ny, z, core))
+
+    def b_z(k, yy):
+        here = wf.at[far, rows_b, cols(yy, z)]
+        return remote(here, here, sd.at[k, yy], qd.at[k, yy], seq=at_seq(y, (z + k) % nz, core))
+
+    def across(part):
+        here = wf.at[far, rows_a if part == 0 else rows_b]
+        return remote(here, here, se.at[part], qe.at[part], seq=at_seq(y, z, 1 - core))
+
+    def own():
+        return pltpu.make_async_copy(w, wf.at[0], so)
+
+    def arrived(src, sem, **where):
+        remote(src, src, sem, sem, **where).wait_recv()
+
+    def step0():
+        for k in range(1, nx):
+            spread_x(k).start()
+        own().start()
+
+    def step1():
+        for k in range(1, nx):
+            spread_x(k).wait_recv()
+        for k in range(1, max(ny, nz)):
+            if k < nz:
+                a_z(k).start()
+            if k < ny:
+                b_y(k).start()
+
+    def step2():
+        for k in range(1, nz):
+            a_z(k).wait_recv()
+        for k in range(1, ny):
+            a_y(k).start()
+        for k in range(1, ny):
+            b_y(k).wait_recv()
+        for k in range(1, nz):
+            for yy in range(ny):
+                b_z(k, yy).start()
+
+    def step3():
+        for k in range(1, ny):
+            a_y(k).wait_recv()
+        across(0).start()
+        for k in range(1, nz):
+            for yy in range(ny):
+                b_z(k, yy).wait_recv()
+        across(1).start()
+
+    def step4():
+        across(0).wait_recv()
+        across(1).wait_recv()
+        own().wait()
+        for k in range(1, nx):
+            spread_x(k).wait_send()
+        for k in range(1, nz):
+            a_z(k).wait_send()
+            for yy in range(ny):
+                b_z(k, yy).wait_send()
+        for k in range(1, ny):
+            b_y(k).wait_send()
+            a_y(k).wait_send()
+        across(0).wait_send()
+        across(1).wait_send()
+
+    return step0, step1, step2, step3, step4
+
+
+def gather_kernel(
+    nx, ny, nz, nh,
+    tok, wt,
+    gt, p, wf,
+    w, g, hal, s_own, r_own, s_fwd, r_fwd, s_hal, r_hal, s_w, *sems,
+):
     x = lax.axis_index("head")
     s = lax.axis_index("seq")
+    ns = 2 * ny * nz
+    core, z, y = s % 2, (s // 2) % nz, s // (2 * nz)
     left, right, opp = (x + nx - 1) % nx, (x + 1) % nx, (x + 2) % nx
     prev, after = (s + ns - 1) % ns, (s + 1) % ns
     rows, depth = tok.shape
     ch = rows // 4
     bar = pltpu.get_barrier_semaphore()
-    greet(bar, head=left)
-    greet(bar, head=right)
+    for k in range(1, nx):
+        greet(bar, head=(x + k) % nx)
     greet(bar, seq=prev, head=nx - 1)
+    greet(bar, seq=s + 1 - 2 * core)
+    for k in range(1, nz):
+        greet(bar, seq=(y * nz + (z + k) % nz) * 2 + core)
+    for k in range(1, ny):
+        greet(bar, seq=(((y + k) % ny) * nz + z) * 2 + core)
 
     @pl.when(x == nx - 1)
     def _():
         for j in range(nx):
             greet(bar, seq=after, head=j)
 
-    pl.semaphore_wait(bar, jnp.where(x == nx - 1, 3 + nx, 3))
+    loads = []
+    for h in range(nh):
+        base = h * CHAN
+        loads.append(
+            pltpu.make_async_copy(
+                wt.at[base + 2 * F : base + CHAN], w.at[h * E : (h + 1) * E], s_w.at[2 * h]
+            )
+        )
+        loads.append(
+            pltpu.make_async_copy(
+                wt.at[base : base + 2 * F],
+                w.at[nh * E + 2 * F * h : nh * E + 2 * F * (h + 1)],
+                s_w.at[2 * h + 1],
+            )
+        )
+    for copy in loads:
+        copy.start()
+    greeted = nx - 1 + 2 + nz - 1 + ny - 1
+    pl.semaphore_wait(bar, jnp.where(x == nx - 1, greeted + nx, greeted))
 
     def part(c):
         return pl.ds(c * ch, ch)
@@ -130,6 +266,7 @@
     def halo(j):
         return remote(tok.at[pl.ds(rows - 16, 16)], hal, s_hal.at[j], r_hal, seq=after, head=j)
 
+    step0, step1, step2, step3, step4 = weight_gather(nx, ny, nz, x, y, z, core, w, wf, sems)
     for c in range(4):
         own(0, c).start()
         own(1, (c + 2) % 4).start()
@@ -140,9 +277,13 @@
                 for j in range(nx):
                     halo(j).start()
 
+            for copy in loads:
+                copy.wait()
+            step0()
+
     def process(slot, src):
         base = pl.multiple_of(slot * rows, rows)
-        p[pl.ds(16 + base, rows), :] = dot(src[...], w[...])
+        p[pl.ds(16 + base, rows), :] = dot(src[...], w[...], NT)
 
         def turn(i, carry):
             at = pl.ds(pl.multiple_of(i * 256, 256), 256)
@@ -151,14 +292,16 @@
 
         lax.fori_loop(0, depth // 256, turn, 0)
 
+    step1()
     process(x, tok)
     for c in range(2):
         arrives(0, c).wait_recv()
         forward(0, c).start()
         arrives(1, c + 2).wait_recv()
         forward(1, c + 2).start()
+    step2()
     halo(0).wait_recv()
-    head_rows = dot(hal[...], w[...])
+    head_rows = dot(hal[...], w[...], NT)
     p[0:16, :] = jnp.where(s == 0, 0.0, head_rows)
     arrives(0, 2).wait_recv()
     arrives(0, 3).wait_recv()
@@ -166,6 +309,7 @@
     arrives(1, 0).wait_recv()
     arrives(1, 1).wait_recv()
     process(right, g.at[right])
+    step3()
     for c in range(2):
         arrives_far(0, c).wait_recv()
         arrives_far(1, c + 2).wait_recv()
@@ -182,21 +326,26 @@
         for j in range(nx):
             halo(j).wait_send()
 
-
-def gathered_projection(tokens, w, nx, ns):
+    step4()
+
+
+def gathered_projection(tokens, wt, nx, ny, nz, nh):
     rows, depth = tokens.shape
-    width = w.shape[1]
+    width = wt.shape[0]
     vm = pl.BlockSpec(memory_space=pltpu.VMEM)
+    hbm = pl.BlockSpec(memory_space=pl.ANY)
     dma = pltpu.SemaphoreType.DMA
     return pl.pallas_call(
-        functools.partial(gather_kernel, nx, ns),
+        functools.partial(gather_kernel, nx, ny, nz, nh),
         out_shape=(
             jax.ShapeDtypeStruct((depth, nx * rows), bf16),
             jax.ShapeDtypeStruct((16 + nx * rows, width), f32),
+            jax.ShapeDtypeStruct((nx, width, depth), bf16),
         ),
-        in_specs=[vm] * 2,
-        out_specs=(vm, vm),
+        in_specs=[vm, hbm],
+        out_specs=(vm, vm, hbm),
         scratch_shapes=[
+            pltpu.VMEM((width, depth), bf16),
             pltpu.VMEM((nx, rows, depth), bf16),
             pltpu.VMEM((16, depth), bf16),
             dma((2, 4)),
@@ -205,24 +354,39 @@
             dma((2, 2)),
             dma((nx,)),
             dma(()),
+            dma((2 * nh,)),
+            dma((nx,)),
+            dma((nx,)),
+            dma((nz,)),
+            dma((nz,)),
+            dma((ny,)),
+            dma((ny,)),
+            dma((ny,)),
+            dma((ny,)),
+            dma((nz, ny)),
+            dma((nz, ny)),
+            dma((2,)),
+            dma((2,)),
+            dma(()),
         ],
         compiler_params=pltpu.CompilerParams(
             collective_id=0, has_side_effects=True, vmem_limit_bytes=56 * 2**20
         ),
-    )(tokens, w)
+    )(tokens, wt)
 
 
 def mixer_kernel(
     ga, gb, nh, nb,
-    p, taps, go, selq, selk, gmq, gmk,
+    p, cv, go, selq, selk, gmq, gmk,
     att, gp, hc,
-    qkt, vaug, fqt, fkt, fq, fk, ub, nin, sco, scot, gna, run, st, pfk, pgv, gc,
+    taps, qkt, vaug, fqt, fkt, fq, fk, ub, nin, scot, gna, run, st, pfk, gc,
     loc, r1, tot, r2, out, res, s1, q1, s2, q2, s3, q3,
 ):
     s = lax.axis_index("seq")
     me_a, me_b = s % ga, s // ga
     piece = loc.shape[1] // ga
-    hb_count = nh * nb
+    gh = nh // 2
+    per = gh * nb
     bar = pltpu.get_barrier_semaphore()
     for k in range(1, ga):
         greet(bar, seq=me_b * ga + (me_a + k) % ga)
@@ -236,75 +400,86 @@
     def rows_of(a):
         return pl.ds(pl.multiple_of(a * piece, 16), piece)
 
-    def first(d, k):
+    def first(e, k):
         a = (me_a + k) % ga
         return remote(
-            loc.at[d, rows_of(a)], r1.at[d, me_a], s1.at[d, k], q1.at[d, k], seq=me_b * ga + a
-        )
-
-    def second(d, k):
+            loc.at[e, rows_of(a)], r1.at[e, me_a], s1.at[e, k], q1.at[e, k], seq=me_b * ga + a
+        )
+
+    def second(e, k):
         b = (me_b + k) % gb
-        return remote(tot.at[d], r2.at[d, me_b], s2.at[d, k], q2.at[d, k], seq=b * ga + me_a)
-
-    def third(d, k):
+        return remote(tot.at[e], r2.at[e, me_b], s2.at[e, k], q2.at[e, k], seq=b * ga + me_a)
+
+    def third(e, k):
         a = (me_a + k) % ga
         return remote(
-            out.at[d, a], res.at[d, rows_of(me_a)], s3.at[d, k], q3.at[d, k], seq=me_b * ga + a
-        )
-
-    def exchange_first(d):
+            out.at[e, a], res.at[e, rows_of(me_a)], s3.at[e, k], q3.at[e, k], seq=me_b * ga + a
+        )
+
+    def exchange_first(e):
         for k in range(1, ga):
-            first(d, k).start()
-        r1[d, me_a] = loc[d, rows_of(me_a), :]
-
-    def exchange_second(d):
+            first(e, k).start()
+        r1[e, me_a] = loc[e, rows_of(me_a), :]
+
+    def exchange_second(e):
         for k in range(1, ga):
             a = (me_a + ga - k) % ga
             remote(
-                loc.at[d, rows_of(a)], r1.at[d, a], s1.at[d, k], q1.at[d, k], seq=s
+                loc.at[e, rows_of(a)], r1.at[e, a], s1.at[e, k], q1.at[e, k], seq=s
             ).wait_recv()
         total = jnp.zeros((piece, E), f32)
         for a in range(ga):
-            total = total + r1[d, a].astype(f32)
-        tot[d] = total
+            total = total + r1[e, a].astype(f32)
+        tot[e] = total.astype(bf16)
         for k in range(1, gb):
-            second(d, k).start()
-
-    def exchange_third(d):
+            second(e, k).start()
+
+    def exchange_third(e):
         for k in range(1, gb):
             b = (me_b + gb - k) % gb
-            remote(tot.at[d], r2.at[d, b], s2.at[d, k], q2.at[d, k], seq=s).wait_recv()
-        r2[d, me_b] = tot[d]
+            remote(tot.at[e], r2.at[e, b], s2.at[e, k], q2.at[e, k], seq=s).wait_recv()
+        r2[e, me_b] = tot[e]
         total = jnp.zeros((piece, E), f32)
         for b in range(gb):
-            ahead = b < me_b if d == 0 else b > me_b
-            total = total + jnp.where(ahead, r2[d, b], 0.0)
+            ahead = b < me_b if e < 2 else b > me_b
+            total = total + jnp.where(ahead, r2[e, b].astype(f32), 0.0)
         for step in range(ga):
-            a = step if d == 0 else ga - 1 - step
-            out[d, a] = total.astype(bf16)
-            total = total + r1[d, a].astype(f32)
+            a = step if e < 2 else ga - 1 - step
+            out[e, a] = total.astype(bf16)
+            total = total + r1[e, a].astype(f32)
         for k in range(1, ga):
-            third(d, k).start()
-        res[d, rows_of(me_a), :] = out[d, me_a]
-
-    def exchange_done(d):
+            third(e, k).start()
+        res[e, rows_of(me_a), :] = out[e, me_a]
+
+    def exchange_done(e):
         for k in range(1, ga):
             a = (me_a + ga - k) % ga
             remote(
-                out.at[d, a], res.at[d, rows_of(a)], s3.at[d, k], q3.at[d, k], seq=s
+                out.at[e, a], res.at[e, rows_of(a)], s3.at[e, k], q3.at[e, k], seq=s
             ).wait_recv()
 
-    def pack(d, h, whole):
+    def pack(e, h, whole):
         column = jnp.concatenate([whole[:, E:], jnp.zeros((2 * E - FS, E), f32)], 0)
         line = column.T[0:1, :]
         body = jnp.where(frow == NF, line[:, :E], jnp.where(frow == NF + 1, line[:, E:], whole[:, :E]))
-        loc[d, h * FS : (h + 1) * FS, :] = body.astype(bf16)
-
-    def unpack(d, h):
-        body = res[d, h * FS : (h + 1) * FS, :].astype(f32)
-        line = jnp.concatenate([body[NF : NF + 1, :], body[NF + 1 : NF + 2, :]], 1)
-        column = jnp.broadcast_to(line, (E, 2 * E)).T[:FS, :]
-        return jnp.concatenate([jnp.where(frow < NF, body, 0.0), column], 1)
+        loc[e, h * FS : (h + 1) * FS, :] = body.astype(bf16)
+
+    def pack_group(e):
+        for j in range(gh):
+            h = (e % 2) * gh + j
+            whole = ub[h * nb]
+            for b in range(1, nb):
+                whole = whole + ub[h * nb + b]
+            pack(e, j, whole)
+        if gh * FS < loc.shape[1]:
+            loc[e, gh * FS :, :] = jnp.zeros((loc.shape[1] - gh * FS, E), bf16)
+
+    def unpack_group(e):
+        for j in range(gh):
+            body = res[e, j * FS : (j + 1) * FS, :].astype(f32)
+            line = jnp.concatenate([body[NF : NF + 1, :], body[NF + 1 : NF + 2, :]], 1)
+            column = jnp.broadcast_to(line, (E, 2 * E)).T[:FS, :]
+            run[(e % 2) * gh + j] = jnp.concatenate([jnp.where(frow < NF, body, 0.0), column], 1)
 
     def factors(u, sel):
         high = u.astype(bf16)
@@ -316,86 +491,103 @@
     def block_at(b):
         return pl.ds(pl.multiple_of(b * BLK, BLK), BLK)
 
-    def forward_block(b, carry):
+    for j in range(3):
+        lines = [cv[j, h : h + 1, :] for h in range(nh)]
+        for h in range(nh):
+            taps[j : j + 1, h * E : (h + 1) * E] = lines[h][:, 2 * F :]
+        taps[j : j + 1, nh * E :] = jnp.concatenate([v[:, : 2 * F] for v in lines], 1) * KAPPA
+
+    def convolve(b, carry):
         ext = p[pl.ds(pl.multiple_of(b * BLK, BLK), BLK + 16), :]
         conv = taps[0:1, :] * ext[16:] + taps[1:2, :] * ext[15:-1] + taps[2:3, :] * ext[14:-2]
-        turned = conv[:, nh * E :].T
-        qkt[:, block_at(b)] = turned
+        qkt[:, block_at(b)] = conv[:, nh * E :].T
         for h in range(nh):
-            i = b * nh + h
-            va = jnp.concatenate(
+            vaug[h * nb + b] = jnp.concatenate(
                 [conv[:, h * E : (h + 1) * E].astype(bf16), jnp.ones((BLK, E), bf16)], 1
             )
-            vaug[i] = va
-            first_q, second_q = factors(turned[2 * F * h : 2 * F * h + F], selq)
-            first_k, second_k = factors(turned[2 * F * h + F : 2 * F * (h + 1)], selk)
-            q = (first_q * second_q).astype(bf16)
-            k = (first_k * second_k).astype(bf16)
-            fqt[i] = q
-            fkt[i] = k
-            fq[i] = q.T
-            fk[i] = k.T
-            ub[i] = dot(k, va)
         return carry
 
-    lax.fori_loop(0, nb, forward_block, 0)
-    for h in range(nh):
-        whole = ub[h]
-        for b in range(1, nb):
-            whole = whole + ub[b * nh + h]
-        pack(0, h, whole)
+    lax.fori_loop(0, nb, convolve, 0)
+
+    def featurize(group):
+        def block(b, carry):
+            for j in range(gh):
+                h = group * gh + j
+                i = h * nb + b
+                at = block_at(b)
+                first_q, second_q = factors(qkt[2 * F * h : 2 * F * h + F, at], selq)
+                first_k, second_k = factors(qkt[2 * F * h + F : 2 * F * (h + 1), at], selk)
+                q = (first_q * second_q).astype(bf16)
+                k = (first_k * second_k).astype(bf16)
+                fqt[i] = q
+                fkt[i] = k
+                fq[i] = q.T
+                fk[i] = k.T
+                ub[i] = dot(k, vaug[i])
+            return carry
+
+        lax.fori_loop(0, nb, block, 0)
+        pack_group(group)
+
+    featurize(0)
     pl.semaphore_wait(bar, ga - 1 + gb - 1)
     exchange_first(0)
+    featurize(1)
+    exchange_first(1)
 
     def inside(i, carry):
         score = jnp.where(sub >= lane, dot(fq[i], fkt[i]), 0.0).astype(bf16)
-        sco[i] = score
         scot[i] = jnp.where(lane >= sub, dot(fk[i], fqt[i]), 0.0).astype(bf16)
         nin[i] = dot(score, vaug[i])
         return carry
 
-    third_of = hb_count // 4
-    lax.fori_loop(0, third_of, inside, 0)
+    def quarter(n, body):
+        lax.fori_loop(n * per // 2, (n + 1) * per // 2, body, 0, unroll=True)
+
+    quarter(0, inside)
     exchange_second(0)
-    lax.fori_loop(third_of, 2 * third_of, inside, 0)
+    quarter(1, inside)
+    exchange_second(1)
+    quarter(2, inside)
     exchange_third(0)
-    lax.fori_loop(2 * third_of, hb_count, inside, 0)
-    exchange_done(0)
-    for h in range(nh):
-        run[h] = unpack(0, h)
+    quarter(3, inside)
+    exchange_third(1)
 
     ones = jnp.ones((2 * E, E), bf16)
 
-    def attend_block(b, carry):
-        for h in range(nh):
-            i = b * nh + h
-            state = run[h]
-            state_b = state.astype(bf16)
-            run[h] = state + ub[i]
-            both = dot(fq[i], state_b) + nin[i]
-            num = both[:, :E]
-            inv = 1.0 / both[:, E:]
-            mean = num * inv
-            at = (block_at(b), slice(h * E, (h + 1) * E))
-            att[at] = mean.astype(bf16)
-            scaled = go[at].astype(f32) * inv
-            product = scaled * mean
-            high = product.astype(bf16)
-            low = (product - high.astype(f32)).astype(bf16)
-            slope = dot(jnp.concatenate([high, low], 1), ones) * (-1.0 / E)
-            ga_b = jnp.concatenate([scaled.astype(bf16), slope.astype(bf16)], 1)
-            gna[i] = ga_b
-            st[i] = state_b
-            ub[i] = dot(fqt[i], ga_b)
-        return carry
-
-    lax.fori_loop(0, nb, attend_block, 0)
-    for h in range(nh):
-        whole = ub[h]
-        for b in range(1, nb):
-            whole = whole + ub[b * nh + h]
-        pack(1, h, whole)
-    exchange_first(1)
+    def attend(group):
+        def block(b, carry):
+            for j in range(gh):
+                h = group * gh + j
+                i = h * nb + b
+                state = run[h]
+                state_b = state.astype(bf16)
+                run[h] = state + ub[i]
+                both = dot(fq[i], state_b) + nin[i]
+                num = both[:, :E]
+                inv = 1.0 / both[:, E:]
+                mean = num * inv
+                at = (block_at(b), slice(h * E, (h + 1) * E))
+                att[at] = mean.astype(bf16)
+                scaled = go[at].astype(f32) * inv
+                product = scaled * mean
+                high = product.astype(bf16)
+                low = (product - high.astype(f32)).astype(bf16)
+                slope = dot(jnp.concatenate([high, low], 1), ones) * (-1.0 / E)
+                ga_b = jnp.concatenate([scaled.astype(bf16), slope.astype(bf16)], 1)
+                gna[i] = ga_b
+                st[i] = state_b
+                ub[i] = dot(fqt[i], ga_b)
+            return carry
+
+        lax.fori_loop(0, nb, block, 0)
+        pack_group(2 + group)
+
+    for group in range(2):
+        exchange_done(group)
+        unpack_group(group)
+        attend(group)
+        exchange_first(2 + group)
 
     def feature_gradient(u, sel, gm, grad):
         one, two = factors(u, sel)
@@ -403,7 +595,7 @@
         return dot(gm[...], stack)
 
     def inside_back(i, carry):
-        b, h = i // nh, i % nh
+        h, b = i // nb, i % nb
         ga_b = gna[i]
         va = vaug[i]
         mix = jnp.where(sub >= lane, dot(ga_b, va, NT), 0.0).astype(bf16)
@@ -413,34 +605,43 @@
         gq = feature_gradient(qkt[at], selq, gmq, gfq)
         pfk[i] = dot(fqt[i], mix)
         qkt[at] = gq
-        pgv[i] = dot(scot[i], ga_b[:, :E])
+        nin[i, :, :E] = dot(scot[i], ga_b[:, :E])
         return carry
 
-    lax.fori_loop(0, third_of, inside_back, 0)
-    exchange_second(1)
-    lax.fori_loop(third_of, 2 * third_of, inside_back, 0)
-    exchange_third(1)
-    lax.fori_loop(2 * third_of, hb_count, inside_back, 0)
-    exchange_done(1)
-    for h in range(nh):
-        run[h] = unpack(1, h)
-
-    def back_block(step, carry):
-        b = nb - 1 - step
-        for h in range(nh):
-            i = b * nh + h
-            state = run[h]
-            state_b = state.astype(bf16)
-            run[h] = state + ub[i]
-            gfk = dot(state_b, vaug[i], NT) + pfk[i]
-            at = (slice(2 * F * h + F, 2 * F * (h + 1)), block_at(b))
-            qkt[at] = feature_gradient(qkt[at], selk, gmk, gfk)
-            gc[block_at(b), h * E : (h + 1) * E] = dot(fk[i], state_b[:, :E]) + pgv[i]
-        gc[block_at(b), nh * E :] = qkt[:, block_at(b)].T
-        return carry
+    quarter(0, inside_back)
+    exchange_second(2)
+    quarter(1, inside_back)
+    exchange_second(3)
+    quarter(2, inside_back)
+    exchange_third(2)
+    quarter(3, inside_back)
+    exchange_third(3)
+
+    def finish(group):
+        def block(step, carry):
+            b = nb - 1 - step
+            for j in range(gh):
+                h = group * gh + j
+                i = h * nb + b
+                state = run[h]
+                state_b = state.astype(bf16)
+                run[h] = state + ub[i]
+                gfk = dot(state_b, vaug[i], NT) + pfk[i]
+                at = (slice(2 * F * h + F, 2 * F * (h + 1)), block_at(b))
+                qkt[at] = feature_gradient(qkt[at], selk, gmk, gfk)
+                gc[block_at(b), h * E : (h + 1) * E] = dot(fk[i], state_b[:, :E]) + nin[i, :, :E]
+            return carry
+
+        lax.fori_loop(0, nb, block, 0)
+
+    for group in range(2):
+        exchange_done(2 + group)
+        unpack_group(2 + group)
+        finish(group)
 
     gc[nb * BLK :, :] = jnp.zeros((16, gc.shape[1]), f32)
-    lax.fori_loop(0, nb, back_block, 0)
+    for b in range(nb):
+        gc[b * BLK : (b + 1) * BLK, nh * E :] = qkt[:, b * BLK : (b + 1) * BLK].T
 
     def spread(b, carry):
         ext = gc[pl.ds(pl.multiple_of(b * BLK, BLK), BLK + 16), :]
@@ -452,21 +653,21 @@
     edge = jnp.concatenate([jnp.zeros((16, gc.shape[1]), f32), gc[0:16, :]], 0)
     hc[...] = (taps[1:2, :] * edge[1:17] + taps[2:3, :] * edge[2:18]).astype(bf16)
 
-    for d in range(2):
+    for e in range(4):
         for k in range(1, ga):
-            first(d, k).wait_send()
-            third(d, k).wait_send()
+            first(e, k).wait_send()
+            third(e, k).wait_send()
         for k in range(1, gb):
-            second(d, k).wait_send()
-
-
-def mixer(p, taps, go, ga, gb):
+            second(e, k).wait_send()
+
+
+def mixer(p, cv, go, ga, gb):
     rows = go.shape[0]
     nh = go.shape[1] // E
     nb = rows // BLK
     n = nh * nb
     width = p.shape[1]
-    piece = nh * FS // ga
+    piece = -(-(nh // 2) * FS // (16 * ga)) * 16
     vm = pl.BlockSpec(memory_space=pltpu.VMEM)
     dma = pltpu.SemaphoreType.DMA
     consts = [
@@ -485,6 +686,7 @@
         in_specs=[vm] * 7,
         out_specs=(vm, vm, vm),
         scratch_shapes=[
+            pltpu.VMEM((8, width), f32),
             pltpu.VMEM((nh * 2 * F, rows), f32),
             pltpu.VMEM((n, BLK, 2 * E), bf16),
             pltpu.VMEM((n, FS, BLK), bf16),
@@ -494,30 +696,28 @@
             pltpu.VMEM((n, FS, 2 * E), f32),
             pltpu.VMEM((n, BLK, 2 * E), f32),
             pltpu.VMEM((n, BLK, BLK), bf16),
-            pltpu.VMEM((n, BLK, BLK), bf16),
             pltpu.VMEM((n, BLK, 2 * E), bf16),
             pltpu.VMEM((nh, FS, 2 * E), f32),
             pltpu.VMEM((n, FS, 2 * E), bf16),
             pltpu.VMEM((n, FS, BLK), f32),
-            pltpu.VMEM((n, BLK, E), f32),
             pltpu.VMEM((rows + 16, width), f32),
-            pltpu.VMEM((2, nh * FS, E), bf16),
-            pltpu.VMEM((2, ga, piece, E), bf16),
-            pltpu.VMEM((2, piece, E), f32),
-            pltpu.VMEM((2, gb, piece, E), f32),
-            pltpu.VMEM((2, ga, piece, E), bf16),
-            pltpu.VMEM((2, nh * FS, E), bf16),
-            dma((2, ga)),
-            dma((2, ga)),
-            dma((2, gb)),
-            dma((2, gb)),
-            dma((2, ga)),
-            dma((2, ga)),
+            pltpu.VMEM((4, ga * piece, E), bf16),
+            pltpu.VMEM((4, ga, piece, E), bf16),
+            pltpu.VMEM((4, piece, E), bf16),
+            pltpu.VMEM((4, gb, piece, E), bf16),
+            pltpu.VMEM((4, ga, piece, E), bf16),
+            pltpu.VMEM((4, ga * piece, E), bf16),
+            dma((4, ga)),
+            dma((4, ga)),
+            dma((4, gb)),
+            dma((4, gb)),
+            dma((4, ga)),
+            dma((4, ga)),
         ],
         compiler_params=pltpu.CompilerParams(
             collective_id=1, has_side_effects=True, vmem_limit_bytes=60 * 2**20
         ),
-    )(p, taps, go, *consts)
+    )(p, cv, go, *consts)
 
 
 def tail_kernel(
@@ -562,7 +762,7 @@
     def over(k, last):
         j = (x + k) % nx
         src = g3 if last else gp.at[block(j)]
-        return remote(src, ga.at[x], sx.at[k], qx.at[k], head=j)
+        return remote(src, ga.at[nx - k], sx.at[k], qx.at[nx - k], head=j)
 
     for k in (1, 3, 2):
 
@@ -583,11 +783,11 @@
 
     @pl.when(x == nx - 1)
     def _():
-        ga[x] = g3[...]
+        ga[0] = g3[...]
 
     @pl.when(x != nx - 1)
     def _():
-        ga[x] = gp[block(x), :]
+        ga[0] = gp[block(x), :]
 
     pieces = ny * nz
     height = gwb.shape[2]
@@ -646,16 +846,15 @@
             go_2b(k).start()
 
     for k in (1, 3, 2):
-        j = (x + nx - k) % nx
-        remote(g3, ga.at[j], sx.at[k], qx.at[k], head=j).wait_recv()
+        remote(g3, ga.at[k], sx.at[k], qx.at[k], head=(x + k) % nx).wait_recv()
     for copy in weights:
         copy.wait()
 
     def input_step(i, carry):
         at = pl.ds(pl.multiple_of(i * 256, 256), 256)
-        total = dot(ga[0], wf[0, at, :], NT)
+        total = dot(ga[0], wf[0, :, at])
         for j in range(1, nx):
-            total = total + dot(ga[j], wf[j, at, :], NT)
+            total = total + dot(ga[j], wf[j, :, at])
         gi[:, at] = total.astype(bf16)
         return carry
 
@@ -682,16 +881,23 @@
         if k < nz:
             go_3b(k).start()
     lax.fori_loop(steps // 2, steps, input_step, 0)
+    nh = gw.shape[1]
+
+    def put(at, total):
+        for h in range(nh):
+            narrow = total[:, nh * E + 2 * F * h : nh * E + 2 * F * (h + 1)]
+            gw[at, h, :] = jnp.concatenate([narrow, total[:, h * E : (h + 1) * E]], 1)
+
     total = ua[y].astype(f32)
     for k in range(1, ny):
         go_3a(k).wait_recv()
         total = total + r3a[k].astype(f32)
-    gw[0:half, :] = total
+    put(slice(0, half), total)
     total = ub[z].astype(f32)
     for k in range(1, nz):
         go_3b(k).wait_recv()
         total = total + r3b[k].astype(f32)
-    gw[half:, :] = total
+    put(slice(half, height), total)
 
     edge.wait_send()
     for k in range(1, nx):
@@ -719,12 +925,12 @@
         functools.partial(tail_kernel, nx, ny, nz),
         out_shape=(
             jax.ShapeDtypeStruct((rows, depth), bf16),
-            jax.ShapeDtypeStruct((height, width), f32),
+            jax.ShapeDtypeStruct((height, width // CHAN, CHAN), f32),
         ),
         in_specs=[vm] * 3 + [pl.BlockSpec(memory_space=pl.ANY)],
         out_specs=(vm, vm),
         scratch_shapes=[
-            pltpu.VMEM((nx, depth, width), bf16),
+            pltpu.VMEM((nx, width, depth), bf16),
             pltpu.VMEM((nx, rows, width), bf16),
             pltpu.VMEM((rows, width), bf16),
             pltpu.VMEM((16, width), bf16),
@@ -759,29 +965,12 @@
     )(gp, hc, gt, wf)
 
 
-def ordered(weight):
-    lead = weight.shape[0]
-    return jnp.concatenate(
-        [weight[:, :, 2 * F :].reshape(lead, -1), weight[:, :, : 2 * F].reshape(lead, -1)], 1
-    )
-
-
 def local(nx, ny, nz, tokens, in_weight, conv_kernel, grad_out):
     depth, nh, _ = in_weight.shape
-    ns = ny * nz * 2
-    w = ordered(in_weight)
-    taps = ordered(conv_kernel)
-    scale = jnp.where(jnp.arange(taps.shape[1]) < nh * E, 1.0, KAPPA).astype(f32)
-    taps = jnp.pad(taps * scale, ((0, 5), (0, 0)))
-    height = depth // ns
-    own = lax.dynamic_slice_in_dim(w, lax.axis_index("seq") * height, height, 0)
-    wf = lax.all_gather(own, ("head", "seq"), axis=0, tiled=True).reshape(nx, depth, -1)
-    gt, p = gathered_projection(tokens, w, nx, ns)
-    att, gp, hc = mixer(p, taps, grad_out, nz * 2, ny)
+    wt = jnp.transpose(in_weight, (1, 2, 0)).reshape(nh * CHAN, depth)
+    gt, p, wf = gathered_projection(tokens, wt, nx, ny, nz, nh)
+    att, gp, hc = mixer(p, conv_kernel, grad_out, nz * 2, ny)
     gi, gw = tail(gp, hc, gt, wf, nx, ny, nz)
-    gw = jnp.concatenate(
-        [gw[:, nh * E :].reshape(height, nh, 2 * F), gw[:, : nh * E].reshape(height, nh, E)], 2
-    )
     return att, gi, gw
 
 

time: 165 us -> 144 us (0.87)
  between operations: 14.2 us -> 0.69 us
  local copies, waits for them, and re-layouts: 11.1 us -> 3.26 us
  Pallas kernels: 136 us -> 140 us
  other arithmetic: 3.28 us -> 0 us
    pallas_call x1, Pallas kernels: 52.8 us -> 64.3 us  [gathered_projection(): pl.pallas_call(functools.partial(gather_kernel, nx, ny, nz, nh), out_shap...]
    pallas_call x1, Pallas kernels: 52.3 us -> 44 us  [mixer(): pl.pallas_call(functools.partial(mixer_kernel, ga, gb, nh, nb), out_shape...]
    slice x8 -> x0, local copies, waits for them, and re-layouts: 5.09 us -> none  [the longest x1 3.22 us: ordered(): weight[:, :, 2 * F:].reshape(lead, -1)]
    reshape x5 -> x0, local copies, waits for them, and re-layouts: 3.38 us -> none  [the longest x1 2.87 us: ordered(): weight[:, :, 2 * F:].reshape(lead, -1)]
    concatenate x3 -> x0, other arithmetic: 3.27 us -> none  [the longest x2 2.36 us: ordered(): jnp.concatenate([weight[:, :, 2 * F:].reshape(lead, -1), weight[:, :, :2...]
  transfers between devices with their start and end apart: 1 -> 0, of which waited for: 0 -> 0; matrix products, arithmetic and copies ran while one was open for 2% -> 0% of each run, Pallas kernels for 64% -> 0%
where the time goes in v2:
time: 144 us
  Pallas kernels  140 us (97%)
  local copies, waits for them, and re-layouts  3.26 us (2%)
    pallas_call x1, Pallas kernels, gathered_projection(): pl.pallas_call(functools.partial(gather_kernel, nx, ny, nz, nh), out_shap...  64.3 us
    pallas_call x1, Pallas kernels, mixer(): pl.pallas_call(functools.partial(mixer_kernel, ga, gb, nh, nb), out_shape...  44 us
    pallas_call x1, Pallas kernels, tail(): pl.pallas_call(functools.partial(tail_kernel, nx, ny, nz), out_shape=(jax...  31.3 us
    unnamed x9, local copies, waits for them, and re-layouts  3.26 us

profile of v2, /device:TPU:0, one launch (start us, length us, event | category | flops | bytes accessed | tf_op | source)
XLA Modules:
  0.0 143.5 jit_solution(10035698630958223913)
XLA Ops:
  0.6 64.3 %shard_map.103 = (bf16[2048,1024]{1,0:T(8,128)(2,1)}, f32[1040,640]{1,0:T(8,128)}, bf16[4,640,2048]{2,1,0:T(8,128)(2,1)}) custom-call(bf16[256,2048]{1,0:T(8,128)(2,1)} %tok.1, bf16[640,2048]{1,0:T(8,128)(2,1)} %bitcast.3), custom_call_target="tpu_custom_call" | custom-call | tf_op jit(solution)/shard_map/pallas_call | solution.py:338
  65.0 44.0 %shard_map.104 = (bf16[1024,512]{1,0:T(8,128)(2,1)}, bf16[1024,640]{1,0:T(8,128)(2,1)}, bf16[16,640]{1,0:T(8,128)(2,1)}) custom-call(f32[1040,640]{1,0:T(8,128)} %get-tuple-element.11.p, f32[3,4,160]{2,1,0:T(4,128)} %cv.1, bf16[1024,512]{1,0:T(8,128)(2,1)} %go.1, bf16[320,48]{1,0:T(8,128)(2,1)} %constant.8.clone.selq, bf16[320,48]{1,0:T(8,128)(2,1)} %constant.9.clone.selk, ...), custom_call_target="tpu_custom_call" | custom-call | tf_op jit(solution)/shard_map/pallas_call | solution.py:679
  108.9 0.0 copy-start
  109.0 31.3 %shard_map.105 = (bf16[256,2048]{1,0:T(8,128)(2,1)}, f32[64,4,160]{2,1,0:T(4,128)}) custom-call(bf16[1024,640]{1,0:T(8,128)(2,1)} %get-tuple-element.13.gp, bf16[16,640]{1,0:T(8,128)(2,1)} %get-tuple-element.14.hc, bf16[2048,1024]{1,0:T(8,128)(2,1)} %get-tuple-element.15.gt, bf16[4,640,2048]{2,1,0:T(8,128)(2,1)} %get-tuple-element.16.wf_hbm), custom_call_target="tpu_custom_call" | custom-call | tf_op jit(solution)/shard_map/pallas_call | solution.py:924
  140.2 0.0 copy-start.1
  140.2 0.0 copy-start.2
  140.3 0.0 copy-done
  140.3 1.0 copy.14
  141.2 0.6 copy-done.1
  141.8 1.0 copy.15
  142.8 0.0 copy-done.2
  142.8 0.7 copy.16
Async XLA Ops:
  108.9 31.3 %copy-start = (bf16[1024,512]{1,0:T(8,128)(2,1)S(1)}, bf16[1024,512]{1,0:T(8,128)(2,1)}, u32[]{:S(2)}) copy-start(bf16[1024,512]{1,0:T(8,128)(2,1)} %get-tuple-element.22) | copy-start | bytes 3145732
  140.2 1.6 %copy-start.1 = (bf16[256,2048]{1,0:T(8,128)(2,1)S(1)}, bf16[256,2048]{1,0:T(8,128)(2,1)}, u32[]{:S(2)}) copy-start(bf16[256,2048]{1,0:T(8,128)(2,1)} %get-tuple-element.23) | copy-start | bytes 3145732
  140.2 2.6 %copy-start.2 = (f32[64,4,160]{2,1,0:T(4,128)S(1)}, f32[64,4,160]{2,1,0:T(4,128)}, u32[]{:S(2)}) copy-start(f32[64,4,160]{2,1,0:T(4,128)} %get-tuple-element.24) | copy-start | bytes 491524

commit v3 on v2

v3 whole, which is shorter than its diff:
```python
import functools
import math

import jax
import jax.numpy as jnp
import numpy as np
from jax import lax
from jax.experimental import pallas as pl
from jax.experimental.pallas import tpu as pltpu
from jax.sharding import PartitionSpec as P

F = 16
E = 128
BLK = 256
CHAN = 160
FS = 160
NF = 1 + F + F * (F + 1) // 2
KAPPA = 32.0 ** -0.25
f32 = jnp.float32
bf16 = jnp.bfloat16
NN = (((1,), (0,)), ((), ()))
NT = (((1,), (1,)), ((), ()))


def dot(a, b, dims=NN):
    return lax.dot_general(a, b, dims, preferred_element_type=f32)


def bf_parts(value, count):
    parts = []
    rest = np.float64(value)
    for _ in range(count):
        part = np.float64(np.asarray(rest, dtype=jnp.bfloat16))
        parts.append(part)
        rest = rest - part
    return parts


def selection(weighted):
    sel = np.zeros((2 * FS, 3 * F), np.float64)
    sel[0, 32] = 1.0
    sel[FS, 32] = 1.0
    for i in range(F):
        row = 1 + i
        sel[row, i] = sel[row, F + i] = 1.0
        for c, part in enumerate(bf_parts(0.5 / KAPPA, 3)):
            sel[FS + row, 32 + c] = part
    row = 1 + F
    for i in range(F):
        for j in range(i, F):
            first = 2.0 if (weighted and j > i) else 1.0
            sel[row, i] = sel[row, F + i] = first
            sel[FS + row, j] = sel[FS + row, F + j] = 1.0
            row += 1
    return sel


def gradient_map(weighted):
    sel = selection(weighted)
    return np.concatenate([sel[:FS, :F].T, sel[FS:, :F].T], 1)


def remote(src, dst, send, recv, **where):
    return pltpu.make_async_remote_copy(
        src_ref=src,
        dst_ref=dst,
        send_sem=send,
        recv_sem=recv,
        device_id=where,
        device_id_type=pl.DeviceIdType.MESH,
    )


def greet(sem, **where):
    pl.semaphore_signal(sem, inc=1, device_id=where, device_id_type=pl.DeviceIdType.MESH)


def weight_gather(nx, ny, nz, x, y, z, core, w, wf, sems):
    s1, q1, sa, qa, sb, qb, sc, qc, sd, qd, se, qe = sems
    chan, depth = w.shape
    half = chan // 2
    quarter = half // 2
    col = depth // (ny * nz)
    rows_c = pl.ds(pl.multiple_of(core * half, 16), half)
    rows_a = pl.ds(pl.multiple_of(core * half, 16), quarter)
    rows_b = pl.ds(pl.multiple_of(core * half + quarter, 16), quarter)
    far = pl.ds(0, nx - 1)

    def cols(yy, zz):
        return pl.ds(pl.multiple_of((yy * nz + zz) * col, 128), col)

    def row_of(yy):
        return pl.ds(pl.multiple_of(yy * nz * col, 128), nz * col)

    def at_seq(yy, zz, cc):
        return (yy * nz + zz) * 2 + cc

    mine = cols(y, z)

    def spread_x(k):
        return remote(
            w.at[rows_c, mine], wf.at[nx - k - 1, rows_c, mine], s1.at[k], q1.at[k], head=(x + k) % nx
        )

    def a_z(k):
        here = wf.at[far, rows_a, mine]
        return remote(here, here, sa.at[k], qa.at[k], seq=at_seq(y, (z + k) % nz, core))

    def b_y(k):
        here = wf.at[far, rows_b, mine]
        return remote(here, here, sb.at[k], qb.at[k], seq=at_seq((y + k) % ny, z, core))

    def a_y(k):
        here = wf.at[far, rows_a, row_of(y)]
        return remote(here, here, sc.at[k], qc.at[k], seq=at_seq((y + k) % ny, z, core))

    def b_z(k, yy):
        here = wf.at[far, rows_b, cols(yy, z)]
        return remote(here, here, sd.at[k, yy], qd.at[k, yy], seq=at_seq(y, (z + k) % nz, core))

    def across(part):
        here = wf.at[far, rows_a if part == 0 else rows_b]
        return remote(here, here, se.at[part], qe.at[part], seq=at_seq(y, z, 1 - core))

    def arrived(src, sem, **where):
        remote(src, src, sem, sem, **where).wait_recv()

    def step0():
        for k in range(1, nx):
            spread_x(k).start()

    def step1():
        for k in range(1, nx):
            spread_x(k).wait_recv()
        for k in range(1, max(ny, nz)):
            if k < nz:
                a_z(k).start()
            if k < ny:
                b_y(k).start()

    def step2():
        for k in range(1, nz):
            a_z(k).wait_recv()
        for k in range(1, ny):
            a_y(k).start()
        for k in range(1, ny):
            b_y(k).wait_recv()
        for k in range(1, nz):
            for yy in range(ny):
                b_z(k, yy).start()

    def step3():
        for k in range(1, ny):
            a_y(k).wait_recv()
        across(0).start()
        for k in range(1, nz):
            for yy in range(ny):
                b_z(k, yy).wait_recv()
        across(1).start()

    def step4():
        across(0).wait_recv()
        across(1).wait_recv()
        for k in range(1, nx):
            spread_x(k).wait_send()
        for k in range(1, nz):
            a_z(k).wait_send()
            for yy in range(ny):
                b_z(k, yy).wait_send()
        for k in range(1, ny):
            b_y(k).wait_send()
            a_y(k).wait_send()
        across(0).wait_send()
        across(1).wait_send()

    return step0, step1, step2, step3, step4


def kernel(
    nx, ny, nz, nh,
    tok, wt, cv, go, selq, selk, gmq, gmk,
    att, gi, gw, wf,
    w, g, gt, p, hal, taps, qkt, vaug, fqt, fkt, fq, fk, ub, nin, scot, gna, run, st, pfk, gp, hc,
    loc, r1, tot, r2, out, res,
    wbuf, gin, g3, hal2, gwb, rp, t, r2a, r2b, va, vb, r3a, r3b,
    s_own, r_own, s_fwd, r_fwd, s_hal, r_hal, s_w, s_tok,
    s1, q1, s2, q2, s3, q3,
    sw, sx, qx, sh, qh, sp, qp, s2a, q2a, s2b, q2b, s3a, q3a, s3b, q3b,
    *sems,
):
    x = lax.axis_index("head")
    s = lax.axis_index("seq")
    ns = 2 * ny * nz
    core, z, y = s % 2, (s // 2) % nz, s // (2 * nz)
    left, right, opp = (x + nx - 1) % nx, (x + 1) % nx, (x + 2) % nx
    prev, after = (s + ns - 1) % ns, (s + 1) % ns
    ga, gb = 2 * nz, ny
    me_a, me_b = s % ga, s // ga
    rows, depth = tok.shape
    nb = go.shape[0] // BLK
    ch = rows // 4
    piece = loc.shape[1] // ga
    gh = nh // 2
    per = gh * nb

    def at_seq(yy, zz, cc):
        return (yy * nz + zz) * 2 + cc

    sibling = at_seq(y, z, 1 - core)
    bar = pltpu.get_barrier_semaphore()
    for k in range(1, nx):
        greet(bar, head=(x + k) % nx)
    for k in range(1, ga):
        greet(bar, seq=me_b * ga + (me_a + k) % ga)
    for k in range(1, gb):
        greet(bar, seq=((me_b + k) % gb) * ga + me_a)
    greet(bar, seq=prev)
    greet(bar, seq=after)
    greet(bar, seq=prev, head=nx - 1)

    @pl.when(x == nx - 1)
    def _():
        for j in range(nx):
            greet(bar, seq=after, head=j)

    local_tok = pltpu.make_async_copy(tok, g.at[x], s_tok)
    local_tok.start()
    loads = []
    for h in range(nh):
        base = h * CHAN
        loads.append(
            pltpu.make_async_copy(
                wt.at[base + 2 * F : base + CHAN], w.at[h * E : (h + 1) * E], s_w.at[2 * h]
            )
        )
        loads.append(
            pltpu.make_async_copy(
                wt.at[base : base + 2 * F],
                w.at[nh * E + 2 * F * h : nh * E + 2 * F * (h + 1)],
                s_w.at[2 * h + 1],
            )
        )
    for copy in loads:
        copy.start()
    greeted = nx - 1 + ga - 1 + gb - 1 + 3
    pl.semaphore_wait(bar, jnp.where(x == nx - 1, greeted + nx, greeted))

    def part(c):
        return pl.ds(c * ch, ch)

    def own(way, c):
        return remote(
            tok.at[part(c)],
            g.at[x, part(c)],
            s_own.at[way, c],
            r_own.at[way, c],
            head=right if way == 0 else left,
        )

    def arrives(way, c):
        slot = left if way == 0 else right
        return remote(
            tok.at[part(c)], g.at[slot, part(c)], s_own.at[way, c], r_own.at[way, c], head=left
        )

    def forward(way, c):
        slot = left if way == 0 else right
        return remote(
            g.at[slot, part(c)],
            g.at[slot, part(c)],
            s_fwd.at[way, c % 2],
            r_fwd.at[way, c % 2],
            head=right if way == 0 else left,
        )

    def arrives_far(way, c):
        return remote(
            tok.at[part(c)], g.at[opp, part(c)], s_fwd.at[way, c % 2], r_fwd.at[way, c % 2], head=left
        )

    def halo(j):
        return remote(tok.at[pl.ds(rows - 16, 16)], hal, s_hal.at[j], r_hal, seq=after, head=j)

    step0, step1, step2, step3, step4 = weight_gather(nx, ny, nz, x, y, z, core, w, wf, sems)
    for c in range(2):
        own(0, c).start()
        own(1, c + 2).start()

    @pl.when(x == nx - 1)
    def _():
        for j in range(nx):
            halo(j).start()

    for copy in loads:
        copy.wait()
    step0()

    lane = lax.broadcasted_iota(jnp.int32, (BLK, BLK), 1)
    sub = lax.broadcasted_iota(jnp.int32, (BLK, BLK), 0)
    frow = lax.broadcasted_iota(jnp.int32, (FS, E), 0)

    for j in range(3):
        lines = [cv[j, h : h + 1, :] for h in range(nh)]
        for h in range(nh):
            taps[j : j + 1, h * E : (h + 1) * E] = lines[h][:, 2 * F :]
        taps[j : j + 1, nh * E :] = jnp.concatenate([v[:, : 2 * F] for v in lines], 1) * KAPPA

    def rows_of(a):
        return pl.ds(pl.multiple_of(a * piece, 16), piece)

    def first(e, k):
        a = (me_a + k) % ga
        return remote(
            loc.at[e, rows_of(a)], r1.at[e, me_a], s1.at[e, k], q1.at[e, k], seq=me_b * ga + a
        )

    def second(e, k):
        b = (me_b + k) % gb
        return remote(tot.at[e], r2.at[e, me_b], s2.at[e, k], q2.at[e, k], seq=b * ga + me_a)

    def third(e, k):
        a = (me_a + k) % ga
        return remote(
            out.at[e, a], res.at[e, rows_of(me_a)], s3.at[e, k], q3.at[e, k], seq=me_b * ga + a
        )

    def exchange_first(e):
        for k in range(1, ga):
            first(e, k).start()
        r1[e, me_a] = loc[e, rows_of(me_a), :]

    def exchange_second(e):
        for k in range(1, ga):
            a = (me_a + ga - k) % ga
            remote(
                loc.at[e, rows_of(a)], r1.at[e, a], s1.at[e, k], q1.at[e, k], seq=s
            ).wait_recv()
        total = jnp.zeros((piece, E), f32)
        for a in range(ga):
            total = total + r1[e, a].astype(f32)
        tot[e] = total.astype(bf16)
        for k in range(1, gb):
            second(e, k).start()

    def exchange_third(e):
        for k in range(1, gb):
            b = (me_b + gb - k) % gb
            remote(tot.at[e], r2.at[e, b], s2.at[e, k], q2.at[e, k], seq=s).wait_recv()
        r2[e, me_b] = tot[e]
        total = jnp.zeros((piece, E), f32)
        for b in range(gb):
            ahead = b < me_b if e < 2 else b > me_b
            total = total + jnp.where(ahead, r2[e, b].astype(f32), 0.0)
        for step in range(ga):
            a = step if e < 2 else ga - 1 - step
            out[e, a] = total.astype(bf16)
            total = total + r1[e, a].astype(f32)
        for k in range(1, ga):
            third(e, k).start()
        res[e, rows_of(me_a), :] = out[e, me_a]

    def exchange_done(e):
        for k in range(1, ga):
            a = (me_a + ga - k) % ga
            remote(
                out.at[e, a], res.at[e, rows_of(a)], s3.at[e, k], q3.at[e, k], seq=s
            ).wait_recv()

    def pack(e, h, whole):
        column = jnp.concatenate([whole[:, E:], jnp.zeros((2 * E - FS, E), f32)], 0)
        line = column.T[0:1, :]
        body = jnp.where(frow == NF, line[:, :E], jnp.where(frow == NF + 1, line[:, E:], whole[:, :E]))
        loc[e, h * FS : (h + 1) * FS, :] = body.astype(bf16)

    def pack_group(e):
        for j in range(gh):
            h = (e % 2) * gh + j
            whole = ub[h * nb]
            for b in range(1, nb):
                whole = whole + ub[h * nb + b]
            pack(e, j, whole)
        if gh * FS < loc.shape[1]:
            loc[e, gh * FS :, :] = jnp.zeros((loc.shape[1] - gh * FS, E), bf16)

    def unpack_group(e):
        for j in range(gh):
            body = res[e, j * FS : (j + 1) * FS, :].astype(f32)
            line = jnp.concatenate([body[NF : NF + 1, :], body[NF + 1 : NF + 2, :]], 1)
            column = jnp.broadcast_to(line, (E, 2 * E)).T[:FS, :]
            run[(e % 2) * gh + j] = jnp.concatenate([jnp.where(frow < NF, body, 0.0), column], 1)

    def factors(u, sel):
        high = u.astype(bf16)
        low = (u - high.astype(f32)).astype(bf16)
        stack = jnp.concatenate([high, low, jnp.ones((F, BLK), bf16)], 0)
        both = dot(sel[...], stack)
        return both[:FS], both[FS:]

    def block_at(b):
        return pl.ds(pl.multiple_of(b * BLK, BLK), BLK)

    def convolve(b):
        ext = p[pl.ds(pl.multiple_of(b * BLK, BLK), BLK + 16), :]
        conv = taps[0:1, :] * ext[16:] + taps[1:2, :] * ext[15:-1] + taps[2:3, :] * ext[14:-2]
        qkt[:, block_at(b)] = conv[:, nh * E :].T
        for h in range(nh):
            vaug[h * nb + b] = jnp.concatenate(
                [conv[:, h * E : (h + 1) * E].astype(bf16), jnp.ones((BLK, E), bf16)], 1
            )

    def featurize(b, group):
        for j in range(gh):
            h = group * gh + j
            i = h * nb + b
            at = block_at(b)
            first_q, second_q = factors(qkt[2 * F * h : 2 * F * h + F, at], selq)
            first_k, second_k = factors(qkt[2 * F * h + F : 2 * F * (h + 1), at], selk)
            q = (first_q * second_q).astype(bf16)
            k = (first_k * second_k).astype(bf16)
            fqt[i] = q
            fkt[i] = k
            fq[i] = q.T
            fk[i] = k.T
            ub[i] = dot(k, vaug[i])

    def project(slot):
        base = pl.multiple_of(slot * rows, rows)
        p[pl.ds(16 + base, rows), :] = dot(g[slot], w[...], NT)

    def turn(slot):
        base = pl.multiple_of(slot * rows, rows)

        def piece_of(i, carry):
            at = pl.ds(pl.multiple_of(i * 256, 256), 256)
            gt[at, pl.ds(base, rows)] = g[slot, :, at].T
            return carry

        lax.fori_loop(0, depth // 256, piece_of, 0)

    local_tok.wait()
    project(x)
    for c in range(2):
        own(0, c).wait_send()
        own(1, c + 2).wait_send()
        own(0, c + 2).start()
        own(1, c).start()
    step1()
    for c in range(2):
        arrives(0, c).wait_recv()
        forward(0, c).start()
        arrives(1, c + 2).wait_recv()
        forward(1, c + 2).start()
    turn(x)
    halo(0).wait_recv()
    head_rows = dot(hal[...], w[...], NT)
    p[0:16, :] = jnp.where(s == 0, 0.0, head_rows)
    step2()
    arrives(0, 2).wait_recv()
    arrives(0, 3).wait_recv()
    project(left)
    arrives(1, 0).wait_recv()
    arrives(1, 1).wait_recv()
    project(right)
    for b in (x, right):
        convolve(b)
        featurize(b, 0)
        featurize(b, 1)
    turn(left)
    turn(right)
    for c in range(2):
        arrives_far(0, c).wait_recv()
        arrives_far(1, c + 2).wait_recv()
    project(opp)
    for b in (opp, left):
        convolve(b)
        featurize(b, 0)
    pack_group(0)
    exchange_first(0)
    for b in (opp, left):
        featurize(b, 1)
    pack_group(1)
    exchange_first(1)

    def inside(i, carry):
        score = jnp.where(sub >= lane, dot(fq[i], fkt[i]), 0.0).astype(bf16)
        scot[i] = jnp.where(lane >= sub, dot(fk[i], fqt[i]), 0.0).astype(bf16)
        nin[i] = dot(score, vaug[i])
        return carry

    def quarter(n, body):
        lax.fori_loop(n * per // 2, (n + 1) * per // 2, body, 0, unroll=True)

    turn(opp)
    quarter(0, inside)
    exchange_second(0)
    quarter(1, inside)
    exchange_second(1)
    quarter(2, inside)
    exchange_third(0)
    quarter(3, inside)
    exchange_third(1)

    ones = jnp.ones((2 * E, E), bf16)

    def attend(group):
        def block(b, carry):
            for j in range(gh):
                h = group * gh + j
                i = h * nb + b
                state = run[h]
                state_b = state.astype(bf16)
                run[h] = state + ub[i]
                both = dot(fq[i], state_b) + nin[i]
                num = both[:, :E]
                inv = 1.0 / both[:, E:]
                mean = num * inv
                at = (block_at(b), slice(h * E, (h + 1) * E))
                att[at] = mean.astype(bf16)
                scaled = go[at].astype(f32) * inv
                product = scaled * mean
                high = product.astype(bf16)
                low = (product - high.astype(f32)).astype(bf16)
                slope = dot(jnp.concatenate([high, low], 1), ones) * (-1.0 / E)
                ga_b = jnp.concatenate([scaled.astype(bf16), slope.astype(bf16)], 1)
                gna[i] = ga_b
                st[i] = state_b
                ub[i] = dot(fqt[i], ga_b)
            return carry

        lax.fori_loop(0, nb, block, 0)
        pack_group(2 + group)

    for group in range(2):
        exchange_done(group)
        unpack_group(group)
        attend(group)
        exchange_first(2 + group)

    def feature_gradient(u, sel, gm, grad):
        one, two = factors(u, sel)
        stack = jnp.concatenate([(grad * two).astype(bf16), (grad * one).astype(bf16)], 0)
        return dot(gm[...], stack)

    def inside_back(i, carry):
        h, b = i // nb, i % nb
        ga_b = gna[i]
        va = vaug[i]
        mix = jnp.where(sub >= lane, dot(ga_b, va, NT), 0.0).astype(bf16)
        mixt = jnp.where(lane >= sub, dot(va, ga_b, NT), 0.0).astype(bf16)
        gfq = dot(st[i], ga_b, NT) + dot(fkt[i], mixt)
        at = (pl.ds(pl.multiple_of(h * 2 * F, 2 * F), F), block_at(b))
        gq = feature_gradient(qkt[at], selq, gmq, gfq)
        pfk[i] = dot(fqt[i], mix)
        qkt[at] = gq
        nin[i, :, :E] = dot(scot[i], ga_b[:, :E])
        return carry

    step3()
    quarter(0, inside_back)
    exchange_second(2)
    quarter(1, inside_back)
    exchange_second(3)
    quarter(2, inside_back)
    exchange_third(2)
    quarter(3, inside_back)
    exchange_third(3)

    def finish(group):
        def block(step, carry):
            b = nb - 1 - step
            for j in range(gh):
                h = group * gh + j
                i = h * nb + b
                state = run[h]
                state_b = state.astype(bf16)
                run[h] = state + ub[i]
                gfk = dot(state_b, vaug[i], NT) + pfk[i]
                at = (slice(2 * F * h + F, 2 * F * (h + 1)), block_at(b))
                qkt[at] = feature_gradient(qkt[at], selk, gmk, gfk)
                p[block_at(b), h * E : (h + 1) * E] = dot(fk[i], state_b[:, :E]) + nin[i, :, :E]
            return carry

        lax.fori_loop(0, nb, block, 0)

    for group in range(2):
        exchange_done(2 + group)
        unpack_group(2 + group)
        finish(group)

    p[nb * BLK :, :] = jnp.zeros((16, p.shape[1]), f32)
    for b in range(nb):
        p[b * BLK : (b + 1) * BLK, nh * E :] = qkt[:, b * BLK : (b + 1) * BLK].T

    def spread(b, carry):
        ext = p[pl.ds(pl.multiple_of(b * BLK, BLK), BLK + 16), :]
        grad = taps[0:1, :] * ext[:BLK] + taps[1:2, :] * ext[1 : BLK + 1] + taps[2:3, :] * ext[2 : BLK + 2]
        gp[block_at(b), :] = grad.astype(bf16)
        return carry

    lax.fori_loop(0, nb, spread, 0)
    edge = jnp.concatenate([jnp.zeros((16, p.shape[1]), f32), p[0:16, :]], 0)
    hc[...] = (taps[1:2, :] * edge[1:17] + taps[2:3, :] * edge[2:18]).astype(bf16)


    rows = gin.shape[1]
    steps = gi.shape[1] // 256

    def load(i, slot):
        return pltpu.make_async_copy(
            wf.at[:, :, pl.ds(pl.multiple_of(i * 256, 256), 256)], wbuf.at[slot], sw.at[slot]
        )

    back = remote(hc, hal2, sh, qh, seq=prev)
    back.start()

    def rows_at(j):
        return pl.ds(pl.multiple_of(j * rows, rows), rows)

    def over(k, last):
        j = (x + k) % nx
        src = g3 if last else gp.at[rows_at(j)]
        return remote(src, gin.at[nx - k], sx.at[k], qx.at[nx - k], head=j)

    for k in (2, 1, 3):

        @pl.when((x + k) % nx != nx - 1)
        def _():
            over(k, False).start()

    back.wait_recv()
    low = gp[(nx - 1) * rows :, :]
    g3[...] = low
    fixed = low[rows - 16 :].astype(f32) + jnp.where(s == ns - 1, 0.0, hal2[...].astype(f32))
    g3[rows - 16 :, :] = fixed.astype(bf16)
    for k in (2, 1, 3):

        @pl.when((x + k) % nx == nx - 1)
        def _():
            over(k, True).start()

    @pl.when(x == nx - 1)
    def _():
        gin[0] = g3[...]

    @pl.when(x != nx - 1)
    def _():
        gin[0] = gp[rows_at(x), :]

    pieces = ny * nz
    height = gwb.shape[2]

    def pair(j):
        return remote(gwb.at[j, 1 - core], rp.at[j], sp.at[j], qp.at[j], seq=sibling)

    per_step = 256 // (2 * height)
    early = (nx - 1) * rows

    def weight_step(i, carry):
        at = pl.ds(pl.multiple_of(i * 256, 256), 256)
        left = gt[at, :]
        whole = dot(left[:, :early], gp[:early, :]) + dot(left[:, early:], g3[...])
        whole = whole.astype(bf16).reshape(per_step, 2, height, whole.shape[1])
        for q in range(per_step):
            gwb[i * per_step + q] = whole[q]
            pair(i * per_step + q).start()
        return carry

    lax.fori_loop(0, pieces // per_step, weight_step, 0)

    step4()
    load(0, 0).start()
    load(1, 1).start()

    def pair_sum(j, carry):
        remote(gwb.at[j, core], rp.at[j], sp.at[j], qp.at[j], seq=sibling).wait_recv()
        t[j // nz, j % nz] = (gwb[j, core].astype(f32) + rp[j].astype(f32)).astype(bf16)
        return carry

    lax.fori_loop(0, pieces, pair_sum, 0)
    half = height // 2
    low_half, high_half = pl.ds(0, half), pl.ds(half, half)

    def go_2a(k):
        to = (z + k) % nz
        return remote(
            t.at[:, to, low_half], r2a.at[k], s2a.at[k], q2a.at[k], seq=at_seq(y, to, core)
        )

    def go_2b(k):
        to = (y + k) % ny
        return remote(
            t.at[to, :, high_half], r2b.at[k], s2b.at[k], q2b.at[k], seq=at_seq(to, z, core)
        )

    def go_3a(k):
        to = (y + k) % ny
        return remote(va.at[to], r3a.at[k], s3a.at[k], q3a.at[k], seq=at_seq(to, z, core))

    def go_3b(k):
        to = (z + k) % nz
        return remote(vb.at[to], r3b.at[k], s3b.at[k], q3b.at[k], seq=at_seq(y, to, core))

    for k in range(1, max(ny, nz)):
        if k < nz:
            go_2a(k).start()
        if k < ny:
            go_2b(k).start()

    for k in (2, 1, 3):
        remote(g3, gin.at[k], sx.at[k], qx.at[k], head=(x + k) % nx).wait_recv()

    def input_step(i, carry):
        at = pl.ds(pl.multiple_of(i * 256, 256), 256)
        slot = i % 2
        total = dot(gin[0], w[:, at])
        load(i, slot).wait()
        for j in range(1, nx):
            total = total + dot(gin[j], wbuf[slot, j - 1])
        gi[:, at] = total.astype(bf16)

        @pl.when(i + 2 < steps)
        def _():
            load(i + 2, slot).start()

        return carry

    lax.fori_loop(0, steps // 2, input_step, 0)

    for k in range(1, nz):
        go_2a(k).wait_recv()
    for k in range(1, ny):
        go_2b(k).wait_recv()
    for i in range(ny):
        total = t[i, z, 0:half].astype(f32)
        for k in range(1, nz):
            total = total + r2a[k, i].astype(f32)
        va[i] = total.astype(bf16)
    for i in range(nz):
        total = t[y, i, half:].astype(f32)
        for k in range(1, ny):
            total = total + r2b[k, i].astype(f32)
        vb[i] = total.astype(bf16)
    for k in range(1, max(ny, nz)):
        if k < ny:
            go_3a(k).start()
        if k < nz:
            go_3b(k).start()
    lax.fori_loop(steps // 2, steps, input_step, 0)
    def put(at, total):
        for h in range(nh):
            narrow = total[:, nh * E + 2 * F * h : nh * E + 2 * F * (h + 1)]
            gw[at, h, :] = jnp.concatenate([narrow, total[:, h * E : (h + 1) * E]], 1)

    total = va[y].astype(f32)
    for k in range(1, ny):
        go_3a(k).wait_recv()
        total = total + r3a[k].astype(f32)
    put(slice(0, half), total)
    total = vb[z].astype(f32)
    for k in range(1, nz):
        go_3b(k).wait_recv()
        total = total + r3b[k].astype(f32)
    put(slice(half, height), total)

    back.wait_send()
    for k in range(1, nx):
        over(k, False).wait_send()
    for j in range(pieces):
        pair(j).wait_send()
    for k in range(1, nz):
        go_2a(k).wait_send()
        go_3b(k).wait_send()
    for k in range(1, ny):
        go_2b(k).wait_send()
        go_3a(k).wait_send()
    for e in range(4):
        for k in range(1, ga):
            first(e, k).wait_send()
            third(e, k).wait_send()
        for k in range(1, gb):
            second(e, k).wait_send()
    for c in range(2):
        own(0, c + 2).wait_send()
        own(1, c).wait_send()
        forward(0, c).wait_send()
        forward(1, c + 2).wait_send()

    @pl.when(x == nx - 1)
    def _():
        for j in range(nx):
            halo(j).wait_send()


def local(nx, ny, nz, tokens, in_weight, conv_kernel, grad_out):
    depth, nh, _ = in_weight.shape
    wt = jnp.transpose(in_weight, (1, 2, 0)).reshape(nh * CHAN, depth)
    rows = tokens.shape[0]
    every = grad_out.shape[0]
    width = nh * CHAN
    nb = every // BLK
    n = nh * nb
    ga, gb, ns = 2 * nz, ny, 2 * ny * nz
    piece = -(-(nh // 2) * FS // (16 * ga)) * 16
    height = depth // ns
    half = height // 2
    vm = pl.BlockSpec(memory_space=pltpu.VMEM)
    hbm = pl.BlockSpec(memory_space=pl.ANY)
    dma = pltpu.SemaphoreType.DMA
    consts = [
        jnp.asarray(selection(True), bf16),
        jnp.asarray(selection(False), bf16),
        jnp.asarray(gradient_map(True), bf16),
        jnp.asarray(gradient_map(False), bf16),
    ]
    att, gi, gw, _ = pl.pallas_call(
        functools.partial(kernel, nx, ny, nz, nh),
        out_shape=(
            jax.ShapeDtypeStruct((every, nh * E), bf16),
            jax.ShapeDtypeStruct((rows, depth), bf16),
            jax.ShapeDtypeStruct((height, nh, CHAN), f32),
            jax.ShapeDtypeStruct((nx - 1, width, depth), bf16),
        ),
        in_specs=[hbm, hbm] + [vm] * 6,
        out_specs=(vm, vm, vm, hbm),
        scratch_shapes=[
            pltpu.VMEM((width, depth), bf16),
            pltpu.VMEM((nx, rows, depth), bf16),
            pltpu.VMEM((depth, every), bf16),
            pltpu.VMEM((16 + every, width), f32),
            pltpu.VMEM((16, depth), bf16),
            pltpu.VMEM((8, width), f32),
            pltpu.VMEM((nh * 2 * F, every), f32),
            pltpu.VMEM((n, BLK, 2 * E), bf16),
            pltpu.VMEM((n, FS, BLK), bf16),
            pltpu.VMEM((n, FS, BLK), bf16),
            pltpu.VMEM((n, BLK, FS), bf16),
            pltpu.VMEM((n, BLK, FS), bf16),
            pltpu.VMEM((n, FS, 2 * E), f32),
            pltpu.VMEM((n, BLK, 2 * E), f32),
            pltpu.VMEM((n, BLK, BLK), bf16),
            pltpu.VMEM((n, BLK, 2 * E), bf16),
            pltpu.VMEM((nh, FS, 2 * E), f32),
            pltpu.VMEM((n, FS, 2 * E), bf16),
            pltpu.VMEM((n, FS, BLK), f32),
            pltpu.VMEM((every, width), bf16),
            pltpu.VMEM((16, width), bf16),
            pltpu.VMEM((4, ga * piece, E), bf16),
            pltpu.VMEM((4, ga, piece, E), bf16),
            pltpu.VMEM((4, piece, E), bf16),
            pltpu.VMEM((4, gb, piece, E), bf16),
            pltpu.VMEM((4, ga, piece, E), bf16),
            pltpu.VMEM((4, ga * piece, E), bf16),
            pltpu.VMEM((2, nx - 1, width, 256), bf16),
            pltpu.VMEM((nx, rows, width), bf16),
            pltpu.VMEM((rows, width), bf16),
            pltpu.VMEM((16, width), bf16),
            pltpu.VMEM((ny * nz, 2, height, width), bf16),
            pltpu.VMEM((ny * nz, height, width), bf16),
            pltpu.VMEM((ny, nz, height, width), bf16),
            pltpu.VMEM((nz, ny, half, width), bf16),
            pltpu.VMEM((ny, nz, half, width), bf16),
            pltpu.VMEM((ny, half, width), bf16),
            pltpu.VMEM((nz, half, width), bf16),
            pltpu.VMEM((ny, half, width), bf16),
            pltpu.VMEM((nz, half, width), bf16),
            dma((2, 4)),
            dma((2, 4)),
            dma((2, 2)),
            dma((2, 2)),
            dma((nx,)),
            dma(()),
            dma((2 * nh,)),
            dma(()),
            dma((4, ga)),
            dma((4, ga)),
            dma((4, gb)),
            dma((4, gb)),
            dma((4, ga)),
            dma((4, ga)),
            dma((2,)),
            dma((nx,)),
            dma((nx,)),
            dma(()),
            dma(()),
            dma((ny * nz,)),
            dma((ny * nz,)),
            dma((nz,)),
            dma((nz,)),
            dma((ny,)),
            dma((ny,)),
            dma((ny,)),
            dma((ny,)),
            dma((nz,)),
            dma((nz,)),
            dma((nx,)),
            dma((nx,)),
            dma((nz,)),
            dma((nz,)),
            dma((ny,)),
            dma((ny,)),
            dma((ny,)),
            dma((ny,)),
            dma((nz, ny)),
            dma((nz, ny)),
            dma((2,)),
            dma((2,)),
        ],
        compiler_params=pltpu.CompilerParams(
            collective_id=0, has_side_effects=True, vmem_limit_bytes=62 * 2**20
        ),
    )(tokens, wt, conv_kernel, grad_out, *consts)
    return att, gi, gw


def solution(mesh):
    nx, ns = mesh.shape["head"], mesh.shape["seq"]
    ny = math.isqrt(ns // 2)
    nz = ns // 2 // ny
    placed = (
        P(("seq", "head"), None),
        P(None, "head", None),
        P(None, "head", None),
        P("seq", "head"),
    )
    return jax.shard_map(
        functools.partial(local, nx, ny, nz),
        mesh=mesh,
        in_specs=placed,
        out_specs=(P("seq", "head"), P(("seq", "head"), None), P("seq", "head", None)),
        check_vma=False,
    )
```

time: 144 us -> 130 us (0.903)
  Pallas kernels: 140 us -> 121 us
  local copies, waits for them, and re-layouts: 3.26 us -> 6.23 us
    pallas_call x3 -> x1, Pallas kernels: 140 us -> 121 us  [local(): pl.pallas_call(functools.partial(kernel, nx, ny, nz, nh), out_shape=(jax....]
    unnamed x9 -> x3, local copies, waits for them, and re-layouts: 3.26 us -> 6.23 us
where the time goes in v3:
time: 130 us; the launch traced here: 128 us
  Pallas kernels  121 us (93%)
  local copies, waits for them, and re-layouts  6.23 us (5%)
    pallas_call x1, Pallas kernels, local(): pl.pallas_call(functools.partial(kernel, nx, ny, nz, nh), out_shape=(jax....  121 us
    unnamed x3, local copies, waits for them, and re-layouts  6.23 us

profile of v3, /device:TPU:0, one launch (start us, length us, event | category | flops | bytes accessed | tf_op | source)
XLA Modules:
  0.0 128.2 jit_solution(2695125949180225379)
XLA Ops:
  0.6 121.3 %shard_map.103 = (bf16[1024,512]{1,0:T(8,128)(2,1)}, bf16[256,2048]{1,0:T(8,128)(2,1)}, f32[64,4,160]{2,1,0:T(4,128)}, bf16[3,640,2048]{2,1,0:T(8,128)(2,1)}) custom-call(bf16[256,2048]{1,0:T(8,128)(2,1)} %tok.1, bf16[640,2048]{1,0:T(8,128)(2,1)} %bitcast.3, f32[3,4,160]{2,1,0:T(4,128)} %cv.1, bf16[1024,512]{1,0:T(8,128)(2,1)} %go.1, ...), custom_call_target="tpu_custom_call" | custom-call | tf_op jit(solution)/shard_map/pallas_call | solution.py:815
  121.9 2.3 %copy.14 = bf16[1024,512]{1,0:T(8,128)(2,1)} copy(bf16[1024,512]{1,0:T(8,128)(2,1)} %get-tuple-element.12) | data formatting | bytes 2097152
  124.2 2.3 %copy.15 = bf16[256,2048]{1,0:T(8,128)(2,1)} copy(bf16[256,2048]{1,0:T(8,128)(2,1)} %get-tuple-element.13) | data formatting | bytes 2097152
  126.5 1.7 %copy.16 = f32[64,4,160]{2,1,0:T(4,128)} copy(f32[64,4,160]{2,1,0:T(4,128)} %get-tuple-element.14) | data formatting | bytes 327680

commit v4 on v3

v4 whole, which is shorter than its diff:
```python
import functools
import math

import jax
import jax.numpy as jnp
import numpy as np
from jax import lax
from jax.experimental import pallas as pl
from jax.experimental.pallas import tpu as pltpu
from jax.sharding import PartitionSpec as P

F = 16
E = 128
BLK = 256
CHAN = 160
FS = 160
NF = 1 + F + F * (F + 1) // 2
KAPPA = 32.0 ** -0.25
f32 = jnp.float32
bf16 = jnp.bfloat16
NN = (((1,), (0,)), ((), ()))
NT = (((1,), (1,)), ((), ()))


def dot(a, b, dims=NN):
    return lax.dot_general(a, b, dims, preferred_element_type=f32)


def bf_parts(value, count):
    parts = []
    rest = np.float64(value)
    for _ in range(count):
        part = np.float64(np.asarray(rest, dtype=jnp.bfloat16))
        parts.append(part)
        rest = rest - part
    return parts


def selection(weighted):
    sel = np.zeros((2 * FS, 3 * F), np.float64)
    sel[0, 32] = 1.0
    sel[FS, 32] = 1.0
    for i in range(F):
        row = 1 + i
        sel[row, i] = sel[row, F + i] = 1.0
        for c, part in enumerate(bf_parts(0.5 / KAPPA, 3)):
            sel[FS + row, 32 + c] = part
    row = 1 + F
    for i in range(F):
        for j in range(i, F):
            first = 2.0 if (weighted and j > i) else 1.0
            sel[row, i] = sel[row, F + i] = first
            sel[FS + row, j] = sel[FS + row, F + j] = 1.0
            row += 1
    return sel


def gradient_map(weighted):
    sel = selection(weighted)
    return np.concatenate([sel[:FS, :F].T, sel[FS:, :F].T], 1)


def remote(src, dst, send, recv, **where):
    return pltpu.make_async_remote_copy(
        src_ref=src,
        dst_ref=dst,
        send_sem=send,
        recv_sem=recv,
        device_id=where,
        device_id_type=pl.DeviceIdType.MESH,
    )


def arrived(ref, sem):
    remote(ref, ref, sem, sem, seq=lax.axis_index("seq")).wait_recv()


def sent(ref, sem):
    remote(ref, ref, sem, sem, seq=lax.axis_index("seq")).wait_send()


def greet(sem, **where):
    pl.semaphore_signal(sem, inc=1, device_id=where, device_id_type=pl.DeviceIdType.MESH)


def weight_gather(nx, ny, nz, x, y, z, core, w, wf, sems):
    s1, q1, sr, qr, sa, qa, sb, qb, sc, qc, sd, qd, sf, qf, sg, qg, se, qe = sems
    chan, depth = w.shape
    half = chan // 2
    quarter = half // 2
    eighth = quarter // 2
    col = depth // (ny * nz)
    base = core * half
    rows_c = pl.ds(pl.multiple_of(base, 16), half)
    rows_a = pl.ds(pl.multiple_of(base, 16), quarter)
    rows_b = pl.ds(pl.multiple_of(base + quarter, 16), quarter)
    far = pl.ds(0, nx - 1)

    def piece_a(n):
        return pl.ds(pl.multiple_of(base + n * eighth, 16), eighth)

    def piece_b(n):
        return pl.ds(pl.multiple_of(base + quarter + n * eighth, 16), eighth)

    def cols(yy, zz):
        return pl.ds(pl.multiple_of((yy * nz + zz) * col, 128), col)

    def row_of(yy):
        return pl.ds(pl.multiple_of(yy * nz * col, 128), nz * col)

    def at_seq(yy, zz, cc):
        return (yy * nz + zz) * 2 + cc

    mine = cols(y, z)
    ring_y = (1, ny - 1) if ny > 2 else (1,)
    ring_z = (1, nz - 1) if nz > 2 else (1,)

    def spread_x(k):
        return remote(w.at[rows_c, mine], wf.at[nx - k - 1, rows_c, mine], s1, q1, head=(x + k) % nx)

    def spread_on(k):
        here = wf.at[nx - k - 1, rows_a if k == 1 else rows_b, mine]
        there = wf.at[nx // 2 - 1, rows_a if k == 1 else rows_b, mine]
        return remote(here, there, sr, qr, head=(x + k) % nx)

    def a_z(k):
        here = wf.at[far, rows_a, mine]
        return remote(here, here, sa, qa, seq=at_seq(y, (z + k) % nz, core))

    def b_y(k):
        here = wf.at[far, rows_b, mine]
        return remote(here, here, sb, qb, seq=at_seq((y + k) % ny, z, core))

    def a_y(k):
        here = wf.at[far, rows_a, row_of(y)]
        return remote(here, here, sc.at[k], qc.at[k], seq=at_seq((y + k) % ny, z, core))

    def b_z(k, yy):
        here = wf.at[far, rows_b, cols(yy, z)]
        return remote(here, here, sd.at[k], qd.at[k], seq=at_seq(y, (z + k) % nz, core))

    def a_y_on(k):
        here = wf.at[far, piece_a(0 if k == 1 else 1), row_of((y - k) % ny)]
        return remote(here, here, sf, qf, seq=at_seq((y + k) % ny, z, core))

    def b_z_on(k, yy):
        here = wf.at[far, piece_b(0 if k == 1 else 1), cols(yy, (z - k) % nz)]
        return remote(here, here, sg, qg, seq=at_seq(y, (z + k) % nz, core))

    def across(part):
        here = wf.at[far, rows_a if part == 0 else rows_b]
        return remote(here, here, se.at[part], qe.at[part], seq=at_seq(y, z, 1 - core))

    def lanes(rows, count):
        return wf.at[far, rows, pl.ds(0, count * col)]

    def step0():
        for k in (1, nx - 1):
            spread_x(k).start()

    def step1():
        arrived(wf.at[pl.ds(0, 2), rows_c, mine], q1)
        for k in (1, nx - 1):
            spread_on(k).start()

    def step2():
        arrived(wf.at[0, rows_c, mine], qr)
        for k in range(1, max(ny, nz)):
            if k < nz:
                a_z(k).start()
            if k < ny:
                b_y(k).start()

    def step3():
        arrived(lanes(rows_a, nz - 1), qa)
        for k in ring_y:
            a_y(k).start()
        arrived(lanes(rows_b, ny - 1), qb)
        for k in ring_z:
            for yy in range(ny):
                b_z(k, yy).start()

    def step4():
        for k in ring_y:
            arrived(lanes(rows_a, nz), qc.at[ny - k])
            if ny > 2:
                a_y_on(ny - k).start()
        for k in ring_z:
            arrived(lanes(rows_b, ny), qd.at[nz - k])
            if nz > 2:
                for yy in range(ny):
                    b_z_on(nz - k, yy).start()

    def step5():
        if ny > 2:
            arrived(lanes(rows_a, nz), qf)
        across(0).start()
        if nz > 2:
            arrived(lanes(rows_b, ny), qg)
        across(1).start()

    def step6():
        across(0).wait_recv()
        across(1).wait_recv()

    def step7():
        sent(wf.at[pl.ds(0, 2), rows_c, mine], s1)
        sent(wf.at[0, rows_c, mine], sr)
        sent(lanes(rows_a, nz - 1), sa)
        sent(lanes(rows_b, ny - 1), sb)
        for k in ring_y:
            sent(lanes(rows_a, nz), sc.at[k])
        for k in ring_z:
            sent(lanes(rows_b, ny), sd.at[k])
        if ny > 2:
            sent(lanes(rows_a, nz), sf)
        if nz > 2:
            sent(lanes(rows_b, ny), sg)
        across(0).wait_send()
        across(1).wait_send()

    return step0, step1, step2, step3, step4, step5, step6, step7


def kernel(
    nx, ny, nz, nh,
    tok, wt, cv_hbm, go, selq_hbm, selk_hbm, gmq_hbm, gmk_hbm,
    att, gi, gw, wf,
    cv, selq, selk, gmq, gmk, go_v, att_v, gi_v, gw_v, w, g, gt, p, hal, taps, qkt, vaug, fqt, fkt, fq, fk, ub, nin, scot, gna, run, st, pfk, gp,
    loc, r1, tot, r2, out, res,
    wbuf, gin, hi, gwb, rp, t, r2a, r2b, va, vb, r3a, r3b,
    s_own, r_own, r_rest, s_fwd, r_fwd, s_hal, r_hal, s_w, s_tok,
    s1, q1, s2, q2, s3, q3,
    sw, sx, qx, sh, qh, sp, qp, s2a, q2a, s2b, q2b, s3a, q3a, s3b, q3b, s_att, s_gi, s_gw, s_go, s_const,
    *sems,
):
    x = lax.axis_index("head")
    s = lax.axis_index("seq")
    ns = 2 * ny * nz
    core, z, y = s % 2, (s // 2) % nz, s // (2 * nz)
    left, right, opp = (x + nx - 1) % nx, (x + 1) % nx, (x + 2) % nx
    prev, after = (s + ns - 1) % ns, (s + 1) % ns
    ga, gb = 2 * nz, ny
    me_a, me_b = s % ga, s // ga
    rows, depth = tok.shape
    nb = go.shape[0] // BLK
    ch = rows // 4
    piece = loc.shape[1] // ga
    gh = nh // 2
    per = gh * nb

    def at_seq(yy, zz, cc):
        return (yy * nz + zz) * 2 + cc

    sibling = at_seq(y, z, 1 - core)
    bar = pltpu.get_barrier_semaphore()
    for k in range(1, nx):
        greet(bar, head=(x + k) % nx)
    for k in range(1, ga):
        greet(bar, seq=me_b * ga + (me_a + k) % ga)
    for k in range(1, gb):
        greet(bar, seq=((me_b + k) % gb) * ga + me_a)
    greet(bar, seq=prev)
    greet(bar, seq=after)
    greet(bar, seq=prev, head=nx - 1)

    @pl.when(x == nx - 1)
    def _():
        for j in range(nx):
            greet(bar, seq=after, head=j)

    local_tok = pltpu.make_async_copy(tok, g.at[x], s_tok)
    local_tok.start()
    local_go = pltpu.make_async_copy(go, go_v, s_go)
    local_go.start()
    small = [
        pltpu.make_async_copy(src, dst, s_const.at[i])
        for i, (src, dst) in enumerate(
            ((cv_hbm, cv), (selq_hbm, selq), (selk_hbm, selk), (gmq_hbm, gmq), (gmk_hbm, gmk))
        )
    ]
    for copy in small:
        copy.start()
    loads = []
    for h in range(nh):
        base = h * CHAN
        loads.append(
            pltpu.make_async_copy(
                wt.at[base + 2 * F : base + CHAN], w.at[h * E : (h + 1) * E], s_w
            )
        )
        loads.append(
            pltpu.make_async_copy(
                wt.at[base : base + 2 * F],
                w.at[nh * E + 2 * F * h : nh * E + 2 * F * (h + 1)],
                s_w,
            )
        )
    for copy in loads:
        copy.start()
    greeted = nx - 1 + ga - 1 + gb - 1 + 3
    pl.semaphore_wait(bar, jnp.where(x == nx - 1, greeted + nx, greeted))

    def chunk(c):
        return pl.ds(c * ch, ch)

    def own(way, c, first):
        return remote(
            tok.at[chunk(c)],
            g.at[x, chunk(c)],
            s_own.at[0 if first else 1],
            r_own.at[way, c % 2] if first else r_rest.at[way],
            head=right if way == 0 else left,
        )

    def forward(way, c):
        slot = left if way == 0 else right
        return remote(
            g.at[slot, chunk(c)],
            g.at[slot, chunk(c)],
            s_fwd,
            r_fwd,
            head=right if way == 0 else left,
        )

    def halo(j):
        return remote(tok.at[pl.ds(rows - 16, 16)], hal, s_hal, r_hal, seq=after, head=j)

    step0, step1, step2, step3, step4, step5, step6, step7 = weight_gather(
        nx, ny, nz, x, y, z, core, w, wf, sems
    )
    pltpu.make_async_copy(w, w, s_w).wait()
    step0()
    own(0, 0, True).start()
    own(1, 2, True).start()
    @pl.when(x == nx - 1)
    def _():
        for j in range(nx):
            halo(j).start()

    lane = lax.broadcasted_iota(jnp.int32, (BLK, BLK), 1)
    sub = lax.broadcasted_iota(jnp.int32, (BLK, BLK), 0)
    frow = lax.broadcasted_iota(jnp.int32, (FS, E), 0)

    for copy in small:
        copy.wait()

    for j in range(3):
        lines = [cv[j, h : h + 1, :] for h in range(nh)]
        for h in range(nh):
            taps[j : j + 1, h * E : (h + 1) * E] = lines[h][:, 2 * F :]
        taps[j : j + 1, nh * E :] = jnp.concatenate([v[:, : 2 * F] for v in lines], 1) * KAPPA

    def rows_of(a):
        return pl.ds(pl.multiple_of(a * piece, 16), piece)

    def first(e, k):
        a = (me_a + k) % ga
        return remote(
            loc.at[e, rows_of(a)], r1.at[e, me_a], s1.at[e], q1.at[e], seq=me_b * ga + a
        )

    def second(e, k):
        b = (me_b + k) % gb
        return remote(tot.at[e], r2.at[e, me_b], s2.at[e], q2.at[e], seq=b * ga + me_a)

    def third(e, k):
        a = (me_a + k) % ga
        return remote(
            out.at[e, a], res.at[e, rows_of(me_a)], s3.at[e], q3.at[e], seq=me_b * ga + a
        )

    def exchange_first(e):
        for k in range(1, ga):
            first(e, k).start()
        r1[e, me_a] = loc[e, rows_of(me_a), :]

    def exchange_second(e):
        arrived(r1.at[e, pl.ds(0, ga - 1)], q1.at[e])
        total = jnp.zeros((piece, E), f32)
        for a in range(ga):
            total = total + r1[e, a].astype(f32)
        tot[e] = total.astype(bf16)
        for k in range(1, gb):
            second(e, k).start()

    def exchange_third(e):
        arrived(r2.at[e, pl.ds(0, gb - 1)], q2.at[e])
        r2[e, me_b] = tot[e]
        total = jnp.zeros((piece, E), f32)
        for b in range(gb):
            ahead = b < me_b if e < 2 else b > me_b
            total = total + jnp.where(ahead, r2[e, b].astype(f32), 0.0)
        for step in range(ga):
            a = step if e < 2 else ga - 1 - step
            out[e, a] = total.astype(bf16)
            total = total + r1[e, a].astype(f32)
        for k in range(1, ga):
            third(e, k).start()
        res[e, rows_of(me_a), :] = out[e, me_a]

    def exchange_done(e):
        arrived(res.at[e, pl.ds(0, (ga - 1) * piece)], q3.at[e])

    def pack(e, h, whole):
        column = jnp.concatenate([whole[:, E:], jnp.zeros((2 * E - FS, E), f32)], 0)
        line = column.T[0:1, :]
        body = jnp.where(frow == NF, line[:, :E], jnp.where(frow == NF + 1, line[:, E:], whole[:, :E]))
        loc[e, h * FS : (h + 1) * FS, :] = body.astype(bf16)

    def pack_group(e):
        for j in range(gh):
            h = (e % 2) * gh + j
            whole = ub[h * nb]
            for b in range(1, nb):
                whole = whole + ub[h * nb + b]
            pack(e, j, whole)
        if gh * FS < loc.shape[1]:
            loc[e, gh * FS :, :] = jnp.zeros((loc.shape[1] - gh * FS, E), bf16)

    def unpack_group(e):
        for j in range(gh):
            body = res[e, j * FS : (j + 1) * FS, :].astype(f32)
            line = jnp.concatenate([body[NF : NF + 1, :], body[NF + 1 : NF + 2, :]], 1)
            column = jnp.broadcast_to(line, (E, 2 * E)).T[:FS, :]
            run[(e % 2) * gh + j] = jnp.concatenate([jnp.where(frow < NF, body, 0.0), column], 1)

    def factors(u, sel):
        high = u.astype(bf16)
        low = (u - high.astype(f32)).astype(bf16)
        stack = jnp.concatenate([high, low, jnp.ones((F, BLK), bf16)], 0)
        both = dot(sel[...], stack)
        return both[:FS], both[FS:]

    def block_at(b):
        return pl.ds(pl.multiple_of(b * BLK, BLK), BLK)

    def convolve(b):
        ext = p[pl.ds(pl.multiple_of(b * BLK, BLK), BLK + 16), :]
        conv = taps[0:1, :] * ext[16:] + taps[1:2, :] * ext[15:-1] + taps[2:3, :] * ext[14:-2]
        qkt[:, block_at(b)] = conv[:, nh * E :].T
        for h in range(nh):
            vaug[h * nb + b] = jnp.concatenate(
                [conv[:, h * E : (h + 1) * E].astype(bf16), jnp.ones((BLK, E), bf16)], 1
            )

    def featurize(b, group):
        for j in range(gh):
            h = group * gh + j
            i = h * nb + b
            at = block_at(b)
            first_q, second_q = factors(qkt[2 * F * h : 2 * F * h + F, at], selq)
            first_k, second_k = factors(qkt[2 * F * h + F : 2 * F * (h + 1), at], selk)
            q = (first_q * second_q).astype(bf16)
            k = (first_k * second_k).astype(bf16)
            fqt[i] = q
            fkt[i] = k
            fq[i] = q.T
            fk[i] = k.T
            ub[i] = dot(k, vaug[i])

    def project(slot):
        base = pl.multiple_of(slot * rows, rows)
        p[pl.ds(16 + base, rows), :] = dot(g[slot], w[...], NT)

    def turn(slot):
        base = pl.multiple_of(slot * rows, rows)

        def piece_of(i, carry):
            at = pl.ds(pl.multiple_of(i * 256, 256), 256)
            gt[at, pl.ds(base, rows)] = g[slot, :, at].T
            return carry

        lax.fori_loop(0, depth // 256, piece_of, 0)

    local_tok.wait()
    project(x)
    turn(x)
    step1()
    own(0, 1, True).start()
    own(1, 3, True).start()
    own(0, 2, False).start()
    own(1, 0, False).start()
    step2()
    sent(tok, s_own.at[0])
    own(0, 3, False).start()
    own(1, 1, False).start()
    for c in range(2):
        arrived(g.at[left, chunk(c)], r_own.at[0, c])
        forward(0, c).start()
        arrived(g.at[right, chunk(c + 2)], r_own.at[1, c])
        forward(1, c + 2).start()
    step3()
    arrived(hal, r_hal)
    head_rows = dot(hal[...], w[...], NT)
    p[0:16, :] = jnp.where(s == 0, 0.0, head_rows)

    def turn_halo(i, carry):
        at = pl.ds(pl.multiple_of(i * 256, 256), 256)
        tail_rows = jnp.concatenate([hal[:, at], jnp.zeros((E - 16, 256), bf16)], 0)
        gt[at, nb * BLK :] = tail_rows.T
        return carry

    lax.fori_loop(0, depth // 256, turn_halo, 0)
    arrived(g.at[left, pl.ds(0, 2 * ch)], r_rest.at[0])
    project(left)
    arrived(g.at[right, pl.ds(0, 2 * ch)], r_rest.at[1])
    project(right)
    step4()
    for b in (x, right):
        convolve(b)
        featurize(b, 0)
        featurize(b, 1)
    arrived(g.at[opp], r_fwd)
    project(opp)
    for b in (opp, left):
        convolve(b)
        featurize(b, 0)
    pack_group(0)
    exchange_first(0)
    for b in (opp, left):
        featurize(b, 1)
    pack_group(1)
    exchange_first(1)

    def inside(i, carry):
        score = jnp.where(sub >= lane, dot(fq[i], fkt[i]), 0.0).astype(bf16)
        scot[i] = jnp.where(lane >= sub, dot(fk[i], fqt[i]), 0.0).astype(bf16)
        nin[i] = dot(score, vaug[i])
        return carry

    def quarter(n, body):
        lax.fori_loop(n * per // 2, (n + 1) * per // 2, body, 0, unroll=True)

    for slot in (opp, left, right):
        turn(slot)
    quarter(0, inside)
    exchange_second(0)
    quarter(1, inside)
    exchange_second(1)
    quarter(2, inside)
    exchange_third(0)
    quarter(3, inside)
    exchange_third(1)

    ones = jnp.ones((2 * E, E), bf16)

    def attend(group):
        for b in range(nb):
            for j in range(gh):
                h = group * gh + j
                i = h * nb + b
                state = run[h]
                state_b = state.astype(bf16)
                run[h] = state + ub[i]
                both = dot(fq[i], state_b) + nin[i]
                num = both[:, :E]
                inv = 1.0 / both[:, E:]
                mean = num * inv
                at = (slice(b * BLK, (b + 1) * BLK), slice(h * E, (h + 1) * E))
                att_v[at] = mean.astype(bf16)
                scaled = go_v[at].astype(f32) * inv
                product = scaled * mean
                high = product.astype(bf16)
                low = (product - high.astype(f32)).astype(bf16)
                slope = dot(jnp.concatenate([high, low], 1), ones) * (-1.0 / E)
                ga_b = jnp.concatenate([scaled.astype(bf16), slope.astype(bf16)], 1)
                gna[i] = ga_b
                st[i] = state_b
                ub[i] = dot(fqt[i], ga_b)
        pack_group(2 + group)

    def att_out(group):
        at = pl.ds(group * gh * E, gh * E)
        return pltpu.make_async_copy(att_v.at[:, at], att.at[:, at], s_att)

    local_go.wait()
    for group in range(2):
        exchange_done(group)
        unpack_group(group)
        attend(group)
        exchange_first(2 + group)
        att_out(group).start()

    def feature_gradient(u, sel, gm, grad):
        one, two = factors(u, sel)
        stack = jnp.concatenate([(grad * two).astype(bf16), (grad * one).astype(bf16)], 0)
        return dot(gm[...], stack)

    def inside_back(i, carry):
        h, b = i // nb, i % nb
        ga_b = gna[i]
        va = vaug[i]
        mix = jnp.where(sub >= lane, dot(ga_b, va, NT), 0.0).astype(bf16)
        mixt = mix.T
        gfq = dot(st[i], ga_b, NT) + dot(fkt[i], mixt)
        at = (pl.ds(pl.multiple_of(h * 2 * F, 2 * F), F), block_at(b))
        gq = feature_gradient(qkt[at], selq, gmq, gfq)
        pfk[i] = dot(fqt[i], mix)
        qkt[at] = gq
        nin[i, :, :E] = dot(scot[i], ga_b[:, :E])
        return carry

    step5()
    quarter(0, inside_back)
    exchange_second(2)
    quarter(1, inside_back)
    exchange_second(3)
    quarter(2, inside_back)
    exchange_third(2)
    quarter(3, inside_back)
    exchange_third(3)

    def value_gradient(group):
        for b in reversed(range(nb)):
            for j in range(gh):
                h = group * gh + j
                i = h * nb + b
                state = run[h]
                state_b = state.astype(bf16)
                st[i] = state_b
                run[h] = state + ub[i]
                rows_b = slice(b * BLK, (b + 1) * BLK)
                p[rows_b, h * E : (h + 1) * E] = dot(fk[i], state_b[:, :E]) + nin[i, :, :E]

    def key_gradient(b):
        rows_b = slice(b * BLK, (b + 1) * BLK)
        for h in range(nh):
            i = h * nb + b
            gfk = dot(st[i], vaug[i], NT) + pfk[i]
            at = (slice(2 * F * h + F, 2 * F * (h + 1)), rows_b)
            qkt[at] = feature_gradient(qkt[at], selk, gmk, gfk)
        p[rows_b, nh * E :] = qkt[:, rows_b].T

    total_rows = nb * BLK
    width = gp.shape[1]
    lanes = ((0, gh * E), (gh * E, nh * E), (nh * E, width))

    def spread(part):
        lo, up = lanes[part]
        one, two, three = taps[0:1, lo:up], taps[1:2, lo:up], taps[2:3, lo:up]
        p[total_rows:, lo:up] = jnp.zeros((16, up - lo), f32)
        for b in range(nb):
            ext = p[b * BLK : (b + 1) * BLK + 16, lo:up]
            grad = one * ext[:BLK] + two * ext[1 : BLK + 1] + three * ext[2 : BLK + 2]
            gp[b * BLK : (b + 1) * BLK, lo:up] = grad.astype(bf16)
        edge = jnp.concatenate([jnp.zeros((16, up - lo), f32), p[0:16, lo:up]], 0)
        edge = jnp.where(s == 0, 0.0, two * edge[1:17] + three * edge[2:18])
        gp[total_rows : total_rows + 16, lo:up] = edge.astype(bf16)
        gp[total_rows + 16 :, lo:up] = jnp.zeros((E - 16, up - lo), bf16)

    def rows_at(j):
        return pl.ds(pl.multiple_of(j * rows, rows), rows)

    def part_of(part):
        return pl.ds(lanes[part][0], lanes[part][1] - lanes[part][0])

    def back(part):
        return remote(
            gp.at[pl.ds(total_rows, 16), part_of(part)],
            hi.at[(x + 1) % nx, :, part_of(part)],
            sh.at[part],
            qh.at[part],
            seq=prev,
            head=nx - 1,
        )

    def over(part, k):
        j = (x + k) % nx
        return remote(
            gp.at[rows_at(j), part_of(part)],
            gin.at[:, pl.ds((nx - k) * width + lanes[part][0], lanes[part][1] - lanes[part][0])],
            sx.at[part],
            qx.at[part],
            head=j,
        )

    def send_rows(part):
        for k in (2, 1, 3):
            over(part, k).start()
        back(part).start()

    pieces = ny * nz
    height = gwb.shape[2]
    half = height // 2
    per_step = 512 // (2 * height)
    low_half, high_half = pl.ds(0, half), pl.ds(half, half)

    def pair(part, j):
        at = part_of(part)
        return remote(
            gwb.at[j, 1 - core, :, at], rp.at[j, :, at], sp.at[part], qp.at[part], seq=sibling
        )

    def weight_part(part):
        lo, up = lanes[part]

        def weight_step(i, carry):
            at = pl.ds(pl.multiple_of(i * 512, 512), 512)
            whole = dot(gt[at, :], gp[:, lo:up]).astype(bf16)
            whole = whole.reshape(per_step, 2, height, up - lo)
            for q in range(per_step):
                gwb[i * per_step + q, :, :, lo:up] = whole[q]
                pair(part, i * per_step + q).start()
            return carry

        lax.fori_loop(0, pieces // per_step, weight_step, 0)

    def go_2a(part, k):
        to, at = (z + k) % nz, part_of(part)
        return remote(
            t.at[:, to, low_half, at],
            r2a.at[k, :, :, at],
            s2a.at[part],
            q2a.at[part],
            seq=at_seq(y, to, core),
        )

    def go_2b(part, k):
        to, at = (y + k) % ny, part_of(part)
        return remote(
            t.at[to, :, high_half, at],
            r2b.at[k, :, :, at],
            s2b.at[part],
            q2b.at[part],
            seq=at_seq(to, z, core),
        )

    def go_3a(part, k):
        to, at = (y + k) % ny, part_of(part)
        return remote(
            va.at[to, :, at],
            r3a.at[k, :, at],
            s3a.at[part],
            q3a.at[part],
            seq=at_seq(to, z, core),
        )

    def go_3b(part, k):
        to, at = (z + k) % nz, part_of(part)
        return remote(
            vb.at[to, :, at],
            r3b.at[k, :, at],
            s3b.at[part],
            q3b.at[part],
            seq=at_seq(y, to, core),
        )

    def weight_second(part):
        lo, up = lanes[part]

        def pair_sum(j, carry):
            both = gwb[j, core, :, lo:up].astype(f32) + rp[j, :, lo:up].astype(f32)
            t[j // nz, j % nz, :, lo:up] = both.astype(bf16)
            return carry

        arrived(rp.at[:, :, part_of(part)], qp.at[part])
        lax.fori_loop(0, pieces, pair_sum, 0)
        for k in range(1, max(ny, nz)):
            if k < nz:
                go_2a(part, k).start()
            if k < ny:
                go_2b(part, k).start()

    def weight_third(part):
        lo, up = lanes[part]
        at = part_of(part)
        arrived(r2a.at[pl.ds(1, nz - 1), :, :, at], q2a.at[part])
        arrived(r2b.at[pl.ds(1, ny - 1), :, :, at], q2b.at[part])
        for i in range(ny):
            total = t[i, z, 0:half, lo:up].astype(f32)
            for k in range(1, nz):
                total = total + r2a[k, i, :, lo:up].astype(f32)
            va[i, :, lo:up] = total.astype(bf16)
        for i in range(nz):
            total = t[y, i, half:, lo:up].astype(f32)
            for k in range(1, ny):
                total = total + r2b[k, i, :, lo:up].astype(f32)
            vb[i, :, lo:up] = total.astype(bf16)
        for k in range(1, max(ny, nz)):
            if k < ny:
                go_3a(part, k).start()
            if k < nz:
                go_3b(part, k).start()

    exchange_done(2)
    unpack_group(2)
    value_gradient(0)
    spread(0)
    send_rows(0)
    weight_part(0)
    exchange_done(3)
    unpack_group(3)
    value_gradient(1)
    spread(1)
    send_rows(1)
    weight_second(0)
    for b in range(nb):
        key_gradient(b)
    spread(2)
    send_rows(2)
    weight_part(1)
    weight_second(1)
    weight_part(2)
    weight_third(0)

    steps = depth // 256

    def load(i, slot):
        at = pl.ds(pl.multiple_of(i * 256, 256), 256)
        for j in range(nx):
            src = w.at[:, at] if j == 0 else wf.at[j - 1, :, at]
            dst = wbuf.at[slot, pl.ds(j * width, width)]
            pltpu.make_async_copy(src, dst, sw.at[slot]).start()

    def three(part):
        return gin.at[:, pl.ds(0, (nx - 1) * (lanes[part][1] - lanes[part][0]))]

    def gi_out(i):
        at = pl.ds(pl.multiple_of(i * 256, 256), 256)
        return pltpu.make_async_copy(gi_v.at[:, at], gi.at[:, at], s_gi)

    step6()
    load(0, 0)
    load(1, 1)
    weight_second(2)
    gin[:, :width] = gp[rows_at(x), :]
    for part in range(3):
        arrived(three(part), qx.at[part])

    @pl.when(x == nx - 1)
    def _():
        for part in range(3):
            arrived(hi.at[:, :, part_of(part)], qh.at[part])
        for k in range(nx):
            at = slice(k * width, (k + 1) * width)
            last = gin[rows - 16 :, at].astype(f32) + hi[k].astype(f32)
            gin[rows - 16 :, at] = last.astype(bf16)

    def input_step(i, carry):
        at = pl.ds(pl.multiple_of(i * 256, 256), 256)
        slot = i % 2
        pltpu.make_async_copy(wbuf.at[slot], wbuf.at[slot], sw.at[slot]).wait()
        gi_v[:, at] = dot(gin[...], wbuf[slot]).astype(bf16)
        gi_out(i).start()

        @pl.when(i + 2 < steps)
        def _():
            load(i + 2, slot)

        return carry

    lax.fori_loop(0, steps // 4, input_step, 0)
    weight_third(1)
    lax.fori_loop(steps // 4, 5 * steps // 8, input_step, 0)
    weight_third(2)
    lax.fori_loop(5 * steps // 8, steps, input_step, 0)

    for part in range(3):
        at = part_of(part)
        arrived(r3a.at[pl.ds(1, ny - 1), :, at], q3a.at[part])
        arrived(r3b.at[pl.ds(1, nz - 1), :, at], q3b.at[part])

    def put(at, total):
        for h in range(nh):
            narrow = total[:, nh * E + 2 * F * h : nh * E + 2 * F * (h + 1)]
            gw_v[at, h, :] = jnp.concatenate([narrow, total[:, h * E : (h + 1) * E]], 1)

    total = va[y].astype(f32)
    for k in range(1, ny):
        total = total + r3a[k].astype(f32)
    put(slice(0, half), total)
    total = vb[z].astype(f32)
    for k in range(1, nz):
        total = total + r3b[k].astype(f32)
    put(slice(half, height), total)
    gw_out = pltpu.make_async_copy(gw_v, gw, s_gw)
    gw_out.start()

    for part in range(3):
        at = part_of(part)
        back(part).wait_send()
        sent(three(part), sx.at[part])
        sent(rp.at[:, :, at], sp.at[part])
        sent(r2a.at[pl.ds(1, nz - 1), :, :, at], s2a.at[part])
        sent(r2b.at[pl.ds(1, ny - 1), :, :, at], s2b.at[part])
        sent(r3a.at[pl.ds(1, ny - 1), :, at], s3a.at[part])
        sent(r3b.at[pl.ds(1, nz - 1), :, at], s3b.at[part])
    for e in range(4):
        sent(r1.at[e, pl.ds(0, ga - 1)], s1.at[e])
        sent(r2.at[e, pl.ds(0, gb - 1)], s2.at[e])
        sent(res.at[e, pl.ds(0, (ga - 1) * piece)], s3.at[e])
    sent(tok, s_own.at[1])
    sent(g.at[opp], s_fwd)

    @pl.when(x == nx - 1)
    def _():
        sent(tok.at[pl.ds(0, 16 * nx)], s_hal)

    step7()
    pltpu.make_async_copy(att_v, att, s_att).wait()
    pltpu.make_async_copy(gi_v, gi, s_gi).wait()
    gw_out.wait()


def hand_on_kernel(count, *refs):
    srcs, dsts, held = refs[:count], refs[count : 2 * count], refs[2 * count : 3 * count]
    come, leave = refs[3 * count :]
    cuts = come.shape[1]

    def slices(i, c):
        size = srcs[i].shape[0] // cuts
        at = pl.ds(c * size, size)
        return (
            pltpu.make_async_copy(srcs[i].at[at], held[i].at[at], come.at[i, c]),
            pltpu.make_async_copy(held[i].at[at], dsts[i].at[at], leave.at[i, c]),
        )

    every = [slices(i, c) for c in range(cuts) for i in range(count)]
    for first, _ in every:
        first.start()
    for first, second in every:
        first.wait()
        second.start()
    for _, second in every:
        second.wait()


def hand_on(*arrays):
    hbm = pl.BlockSpec(memory_space=pl.ANY)
    count = len(arrays)
    return pl.pallas_call(
        functools.partial(hand_on_kernel, count),
        out_shape=tuple(jax.ShapeDtypeStruct(a.shape, a.dtype) for a in arrays),
        in_specs=[hbm] * count,
        out_specs=(hbm,) * count,
        scratch_shapes=[pltpu.VMEM(a.shape, a.dtype) for a in arrays]
        + [pltpu.SemaphoreType.DMA((count, 4))] * 2,
        compiler_params=pltpu.CompilerParams(vmem_limit_bytes=60 * 2**20),
    )(*arrays)


def local(nx, ny, nz, tokens, in_weight, conv_kernel, grad_out):
    depth, nh, _ = in_weight.shape
    wt = jnp.transpose(in_weight, (1, 2, 0)).reshape(nh * CHAN, depth)
    rows = tokens.shape[0]
    every = grad_out.shape[0]
    width = nh * CHAN
    nb = every // BLK
    n = nh * nb
    ga, gb, ns = 2 * nz, ny, 2 * ny * nz
    piece = -(-(nh // 2) * FS // (16 * ga)) * 16
    height = depth // ns
    half = height // 2
    hbm = pl.BlockSpec(memory_space=pl.ANY)
    dma = pltpu.SemaphoreType.DMA
    consts = [
        jnp.asarray(selection(True), bf16),
        jnp.asarray(selection(False), bf16),
        jnp.asarray(gradient_map(True), bf16),
        jnp.asarray(gradient_map(False), bf16),
    ]
    att, gi, gw, _ = pl.pallas_call(
        functools.partial(kernel, nx, ny, nz, nh),
        out_shape=(
            jax.ShapeDtypeStruct((every, nh * E), bf16),
            jax.ShapeDtypeStruct((rows, depth), bf16),
            jax.ShapeDtypeStruct((height, nh, CHAN), f32),
            jax.ShapeDtypeStruct((nx - 1, width, depth), bf16),
        ),
        in_specs=[hbm] * 8,
        out_specs=(hbm, hbm, hbm, hbm),
        scratch_shapes=[
            pltpu.VMEM(conv_kernel.shape, f32),
            pltpu.VMEM((2 * FS, 3 * F), bf16),
            pltpu.VMEM((2 * FS, 3 * F), bf16),
            pltpu.VMEM((F, 2 * FS), bf16),
            pltpu.VMEM((F, 2 * FS), bf16),
            pltpu.VMEM((every, nh * E), bf16),
            pltpu.VMEM((every, nh * E), bf16),
            pltpu.VMEM((rows, depth), bf16),
            pltpu.VMEM((height, nh, CHAN), f32),
            pltpu.VMEM((width, depth), bf16),
            pltpu.VMEM((nx, rows, depth), bf16),
            pltpu.VMEM((depth, every + E), bf16),
            pltpu.VMEM((16 + every, width), f32),
            pltpu.VMEM((16, depth), bf16),
            pltpu.VMEM((8, width), f32),
            pltpu.VMEM((nh * 2 * F, every), f32),
            pltpu.VMEM((n, BLK, 2 * E), bf16),
            pltpu.VMEM((n, FS, BLK), bf16),
            pltpu.VMEM((n, FS, BLK), bf16),
            pltpu.VMEM((n, BLK, FS), bf16),
            pltpu.VMEM((n, BLK, FS), bf16),
            pltpu.VMEM((n, FS, 2 * E), f32),
            pltpu.VMEM((n, BLK, 2 * E), f32),
            pltpu.VMEM((n, BLK, BLK), bf16),
            pltpu.VMEM((n, BLK, 2 * E), bf16),
            pltpu.VMEM((nh, FS, 2 * E), f32),
            pltpu.VMEM((n, FS, 2 * E), bf16),
            pltpu.VMEM((n, FS, BLK), f32),
            pltpu.VMEM((every + E, width), bf16),
            pltpu.VMEM((4, ga * piece, E), bf16),
            pltpu.VMEM((4, ga, piece, E), bf16),
            pltpu.VMEM((4, piece, E), bf16),
            pltpu.VMEM((4, gb, piece, E), bf16),
            pltpu.VMEM((4, ga, piece, E), bf16),
            pltpu.VMEM((4, ga * piece, E), bf16),
            pltpu.VMEM((2, nx * width, 256), bf16),
            pltpu.VMEM((rows, nx * width), bf16),
            pltpu.VMEM((nx, 16, width), bf16),
            pltpu.VMEM((ny * nz, 2, height, width), bf16),
            pltpu.VMEM((ny * nz, height, width), bf16),
            pltpu.VMEM((ny, nz, height, width), bf16),
            pltpu.VMEM((nz, ny, half, width), bf16),
            pltpu.VMEM((ny, nz, half, width), bf16),
            pltpu.VMEM((ny, half, width), bf16),
            pltpu.VMEM((nz, half, width), bf16),
            pltpu.VMEM((ny, half, width), bf16),
            pltpu.VMEM((nz, half, width), bf16),
            dma((2,)),
            dma((2, 2)),
            dma((2,)),
            dma(()),
            dma(()),
            dma(()),
            dma(()),
            dma(()),
            dma(()),
            dma((4,)),
            dma((4,)),
            dma((4,)),
            dma((4,)),
            dma((4,)),
            dma((4,)),
            dma((2,)),
            dma((3,)),
            dma((3,)),
            dma((3,)),
            dma((3,)),
            dma((3,)),
            dma((3,)),
            dma((3,)),
            dma((3,)),
            dma((3,)),
            dma((3,)),
            dma((3,)),
            dma((3,)),
            dma((3,)),
            dma((3,)),
            dma(()),
            dma(()),
            dma(()),
            dma(()),
            dma((5,)),
            dma(()),
            dma(()),
            dma(()),
            dma(()),
            dma(()),
            dma(()),
            dma(()),
            dma(()),
            dma((ny,)),
            dma((ny,)),
            dma((nz,)),
            dma((nz,)),
            dma(()),
            dma(()),
            dma(()),
            dma(()),
            dma((2,)),
            dma((2,)),
        ],
        compiler_params=pltpu.CompilerParams(
            collective_id=0, has_side_effects=True, vmem_limit_bytes=62 * 2**20
        ),
    )(tokens, wt, conv_kernel, grad_out, *consts)
    return hand_on(att, gi, gw)


def solution(mesh):
    nx, ns = mesh.shape["head"], mesh.shape["seq"]
    ny = math.isqrt(ns // 2)
    nz = ns // 2 // ny
    placed = (
        P(("seq", "head"), None),
        P(None, "head", None),
        P(None, "head", None),
        P("seq", "head"),
    )
    return jax.shard_map(
        functools.partial(local, nx, ny, nz),
        mesh=mesh,
        in_specs=placed,
        out_specs=(P("seq", "head"), P(("seq", "head"), None), P("seq", "head", None)),
        check_vma=False,
    )
```

time: 130 us -> 110 us (0.85)
  Pallas kernels: 121 us -> 109 us
  local copies, waits for them, and re-layouts: 6.23 us -> 0 us
    pallas_call x1, Pallas kernels: 121 us -> 106 us  [local(): pl.pallas_call(functools.partial(kernel, nx, ny, nz, nh), out_shape=(jax....]
    unnamed x3 -> x0, local copies, waits for them, and re-layouts: 6.23 us -> none
    pallas_call x0 -> x1, Pallas kernels: none -> 2.54 us  [hand_on(): pl.pallas_call(functools.partial(hand_on_kernel, count), out_shape=tuple(...]
where the time goes in v4:
time: 110 us; the launch traced here: 109 us
  Pallas kernels  109 us (99%)
    pallas_call x1, Pallas kernels, local(): pl.pallas_call(functools.partial(kernel, nx, ny, nz, nh), out_shape=(jax....  106 us
    pallas_call x1, Pallas kernels, hand_on(): pl.pallas_call(functools.partial(hand_on_kernel, count), out_shape=tuple(...  2.54 us

profile of v4, /device:TPU:0, one launch (start us, length us, event | category | flops | bytes accessed | tf_op | source)
XLA Modules:
  0.0 109.4 jit_solution(17427498418143576314)
XLA Ops:
  0.6 106.1 %shard_map.103 = (bf16[1024,512]{1,0:T(8,128)(2,1)}, bf16[256,2048]{1,0:T(8,128)(2,1)}, f32[64,4,160]{2,1,0:T(4,128)}, bf16[3,640,2048]{2,1,0:T(8,128)(2,1)}) custom-call(bf16[256,2048]{1,0:T(8,128)(2,1)} %tok.1, bf16[640,2048]{1,0:T(8,128)(2,1)} %bitcast.3, f32[3,4,160]{2,1,0:T(4,128)} %cv_hbm.1, bf16[1024,512]{1,0:T(8,128)(2,1)} %go.1, ...), custom_call_target="tpu_custom_call" | custom-call | tf_op jit(solution)/shard_map/pallas_call | solution.py:963
  106.7 2.5 %shard_map.104 = (bf16[1024,512]{1,0:T(8,128)(2,1)}, bf16[256,2048]{1,0:T(8,128)(2,1)}, f32[64,4,160]{2,1,0:T(4,128)}) custom-call(bf16[1024,512]{1,0:T(8,128)(2,1)} %get-tuple-element.6.refs_0_, bf16[256,2048]{1,0:T(8,128)(2,1)} %get-tuple-element.7.refs_1_, f32[64,4,160]{2,1,0:T(4,128)} %get-tuple-element.8.refs_2_), custom_call_target="tpu_custom_call" | custom-call | tf_op jit(solution)/shard_map/pallas_call | solution.py:932

commit v5 on v4

--- a/solution.py
+++ b/solution.py
@@ -228,10 +228,10 @@
     att, gi, gw, wf,
     cv, selq, selk, gmq, gmk, go_v, att_v, gi_v, gw_v, w, g, gt, p, hal, taps, qkt, vaug, fqt, fkt, fq, fk, ub, nin, scot, gna, run, st, pfk, gp,
     loc, r1, tot, r2, out, res,
-    wbuf, gin, hi, gwb, rp, t, r2a, r2b, va, vb, r3a, r3b,
+    wbuf, gin, relay, hi, gwb, rp, t, r2a, r2b, va, vb, r3a, r3b,
     s_own, r_own, r_rest, s_fwd, r_fwd, s_hal, r_hal, s_w, s_tok,
     s1, q1, s2, q2, s3, q3,
-    sw, sx, qx, sh, qh, sp, qp, s2a, q2a, s2b, q2b, s3a, q3a, s3b, q3b, s_att, s_gi, s_gw, s_go, s_const,
+    sw, sr1, qr1, sr2, qr2, sx, qx, sh, qh, sp, qp, s2a, q2a, s2b, q2b, s3a, q3a, s3b, q3b, s_att, s_gi, s_gw, s_go, s_const,
     *sems,
 ):
     x = lax.axis_index("head")
@@ -511,6 +511,8 @@
         convolve(b)
         featurize(b, 0)
         featurize(b, 1)
+    turn(left)
+    turn(right)
     arrived(g.at[opp], r_fwd)
     project(opp)
     for b in (opp, left):
@@ -523,25 +525,38 @@
     pack_group(1)
     exchange_first(1)
 
-    def inside(i, carry):
+    def inside(i):
         score = jnp.where(sub >= lane, dot(fq[i], fkt[i]), 0.0).astype(bf16)
         scot[i] = jnp.where(lane >= sub, dot(fk[i], fqt[i]), 0.0).astype(bf16)
         nin[i] = dot(score, vaug[i])
-        return carry
+
+    fold = g.shape[2] // BLK
+
+    def raw_at(i):
+        return (i // fold, slice(None), slice(i % fold * BLK, (i % fold + 1) * BLK))
+
+    def inside_raw(i):
+        h, b = i // nb, i % nb
+        cot = go_v[b * BLK : (b + 1) * BLK, h * E : (h + 1) * E]
+        g[raw_at(i)] = dot(cot, vaug[i, :, :E], NT).astype(bf16)
 
     def quarter(n, body):
-        lax.fori_loop(n * per // 2, (n + 1) * per // 2, body, 0, unroll=True)
-
-    for slot in (opp, left, right):
-        turn(slot)
+        for i in range(n * per // 2, (n + 1) * per // 2):
+            body(i)
+
+    turn(opp)
+    local_go.wait()
     quarter(0, inside)
     exchange_second(0)
     quarter(1, inside)
     exchange_second(1)
     quarter(2, inside)
     exchange_third(0)
+    exchange_third(1)
     quarter(3, inside)
-    exchange_third(1)
+    sent(g.at[opp], s_fwd)
+    for n in range(4):
+        quarter(n, inside_raw)
 
     ones = jnp.ones((2 * E, E), bf16)
 
@@ -566,6 +581,7 @@
                 slope = dot(jnp.concatenate([high, low], 1), ones) * (-1.0 / E)
                 ga_b = jnp.concatenate([scaled.astype(bf16), slope.astype(bf16)], 1)
                 gna[i] = ga_b
+                nin[i, :, E:] = inv
                 st[i] = state_b
                 ub[i] = dot(fqt[i], ga_b)
         pack_group(2 + group)
@@ -574,7 +590,6 @@
         at = pl.ds(group * gh * E, gh * E)
         return pltpu.make_async_copy(att_v.at[:, at], att.at[:, at], s_att)
 
-    local_go.wait()
     for group in range(2):
         exchange_done(group)
         unpack_group(group)
@@ -587,27 +602,29 @@
         stack = jnp.concatenate([(grad * two).astype(bf16), (grad * one).astype(bf16)], 0)
         return dot(gm[...], stack)
 
-    def inside_back(i, carry):
+    def inside_back(i):
         h, b = i // nb, i % nb
         ga_b = gna[i]
-        va = vaug[i]
-        mix = jnp.where(sub >= lane, dot(ga_b, va, NT), 0.0).astype(bf16)
+        inv = nin[i, :, E:]
+        slope = ga_b[:, E:].astype(f32) * float(E)
+        scaled = g[raw_at(i)].astype(f32) * jnp.concatenate([inv, inv], 1)
+        mix = scaled + jnp.concatenate([slope, slope], 1)
+        mix = jnp.where(sub >= lane, mix, 0.0).astype(bf16)
         mixt = mix.T
         gfq = dot(st[i], ga_b, NT) + dot(fkt[i], mixt)
-        at = (pl.ds(pl.multiple_of(h * 2 * F, 2 * F), F), block_at(b))
+        at = (slice(h * 2 * F, h * 2 * F + F), slice(b * BLK, (b + 1) * BLK))
         gq = feature_gradient(qkt[at], selq, gmq, gfq)
         pfk[i] = dot(fqt[i], mix)
         qkt[at] = gq
         nin[i, :, :E] = dot(scot[i], ga_b[:, :E])
-        return carry
 
     step5()
+    exchange_second(2)
     quarter(0, inside_back)
-    exchange_second(2)
     quarter(1, inside_back)
     exchange_second(3)
+    exchange_third(2)
     quarter(2, inside_back)
-    exchange_third(2)
     quarter(3, inside_back)
     exchange_third(3)
 
@@ -665,6 +682,34 @@
             head=nx - 1,
         )
 
+    near = rows // 2
+
+    def out_far(part, way):
+        j = (x + 2) % nx
+        src = pl.ds(pl.multiple_of(j * rows + way * near, near), near)
+        return remote(
+            gp.at[src, part_of(part)],
+            relay.at[way, :, part_of(part)],
+            sr1.at[part],
+            qr1.at[part, way],
+            head=right if way == 0 else left,
+        )
+
+    def on_far(part, way):
+        lo, up = lanes[part]
+        return remote(
+            relay.at[way, :, part_of(part)],
+            gin.at[pl.ds(way * near, near), pl.ds(2 * width + lo, up - lo)],
+            sr2.at[part],
+            qr2.at[part],
+            head=right if way == 0 else left,
+        )
+
+    def pass_on(part):
+        for way in range(2):
+            arrived(relay.at[way, :, part_of(part)], qr1.at[part, way])
+            on_far(part, way).start()
+
     def over(part, k):
         j = (x + k) % nx
         return remote(
@@ -676,8 +721,13 @@
         )
 
     def send_rows(part):
-        for k in (2, 1, 3):
-            over(part, k).start()
+        if part < 2:
+            out_far(part, 0).start()
+            out_far(part, 1).start()
+        else:
+            over(part, 2).start()
+        over(part, 1).start()
+        over(part, 3).start()
         back(part).start()
 
     pieces = ny * nz
@@ -797,9 +847,12 @@
     weight_second(0)
     for b in range(nb):
         key_gradient(b)
+        if b == nb // 2:
+            pass_on(0)
     spread(2)
     send_rows(2)
     weight_part(1)
+    pass_on(1)
     weight_second(1)
     weight_part(2)
     weight_third(0)
@@ -813,8 +866,8 @@
             dst = wbuf.at[slot, pl.ds(j * width, width)]
             pltpu.make_async_copy(src, dst, sw.at[slot]).start()
 
-    def three(part):
-        return gin.at[:, pl.ds(0, (nx - 1) * (lanes[part][1] - lanes[part][0]))]
+    def as_many(part, count):
+        return gin.at[:, pl.ds(0, count * (lanes[part][1] - lanes[part][0]))]
 
     def gi_out(i):
         at = pl.ds(pl.multiple_of(i * 256, 256), 256)
@@ -826,7 +879,9 @@
     weight_second(2)
     gin[:, :width] = gp[rows_at(x), :]
     for part in range(3):
-        arrived(three(part), qx.at[part])
+        if part < 2:
+            arrived(as_many(part, 1), qr2.at[part])
+        arrived(as_many(part, 2 if part < 2 else 3), qx.at[part])
 
     @pl.when(x == nx - 1)
     def _():
@@ -880,7 +935,10 @@
     for part in range(3):
         at = part_of(part)
         back(part).wait_send()
-        sent(three(part), sx.at[part])
+        if part < 2:
+            sent(as_many(part, 1), sr1.at[part])
+            sent(as_many(part, 1), sr2.at[part])
+        sent(as_many(part, 2 if part < 2 else 3), sx.at[part])
         sent(rp.at[:, :, at], sp.at[part])
         sent(r2a.at[pl.ds(1, nz - 1), :, :, at], s2a.at[part])
         sent(r2b.at[pl.ds(1, ny - 1), :, :, at], s2b.at[part])
@@ -891,7 +949,6 @@
         sent(r2.at[e, pl.ds(0, gb - 1)], s2.at[e])
         sent(res.at[e, pl.ds(0, (ga - 1) * piece)], s3.at[e])
     sent(tok, s_own.at[1])
-    sent(g.at[opp], s_fwd)
 
     @pl.when(x == nx - 1)
     def _():
@@ -1008,6 +1065,7 @@
             pltpu.VMEM((4, ga * piece, E), bf16),
             pltpu.VMEM((2, nx * width, 256), bf16),
             pltpu.VMEM((rows, nx * width), bf16),
+            pltpu.VMEM((2, rows // 2, nh * E), bf16),
             pltpu.VMEM((nx, 16, width), bf16),
             pltpu.VMEM((ny * nz, 2, height, width), bf16),
             pltpu.VMEM((ny * nz, height, width), bf16),
@@ -1033,6 +1091,10 @@
             dma((4,)),
             dma((4,)),
             dma((4,)),
+            dma((2,)),
+            dma((2,)),
+            dma((2, 2)),
+            dma((2,)),
             dma((2,)),
             dma((3,)),
             dma((3,)),

time: 110 us -> 106 us (0.964)
  Pallas kernels: 109 us -> 104 us
    pallas_call x1, Pallas kernels: 106 us -> 102 us  [local(): pl.pallas_call(functools.partial(kernel, nx, ny, nz, nh), out_shape=(jax....]
where the time goes in v5:
time: 106 us; the launch traced here: 105 us
  Pallas kernels  104 us (98%)
    pallas_call x1, Pallas kernels, local(): pl.pallas_call(functools.partial(kernel, nx, ny, nz, nh), out_shape=(jax....  102 us
    pallas_call x1, Pallas kernels, hand_on(): pl.pallas_call(functools.partial(hand_on_kernel, count), out_shape=tuple(...  2.54 us

profile of v5, /device:TPU:0, one launch (start us, length us, event | category | flops | bytes accessed | tf_op | source)
XLA Modules:
  0.0 105.0 jit_solution(14514584846946744927)
XLA Ops:
  0.6 101.6 %shard_map.103 = (bf16[1024,512]{1,0:T(8,128)(2,1)}, bf16[256,2048]{1,0:T(8,128)(2,1)}, f32[64,4,160]{2,1,0:T(4,128)}, bf16[3,640,2048]{2,1,0:T(8,128)(2,1)}) custom-call(bf16[256,2048]{1,0:T(8,128)(2,1)} %tok.1, bf16[640,2048]{1,0:T(8,128)(2,1)} %bitcast.3, f32[3,4,160]{2,1,0:T(4,128)} %cv_hbm.1, bf16[1024,512]{1,0:T(8,128)(2,1)} %go.1, ...), custom_call_target="tpu_custom_call" | custom-call | tf_op jit(solution)/shard_map/pallas_call | solution.py:1020
  102.2 2.5 %shard_map.104 = (bf16[1024,512]{1,0:T(8,128)(2,1)}, bf16[256,2048]{1,0:T(8,128)(2,1)}, f32[64,4,160]{2,1,0:T(4,128)}) custom-call(bf16[1024,512]{1,0:T(8,128)(2,1)} %get-tuple-element.6.refs_0_, bf16[256,2048]{1,0:T(8,128)(2,1)} %get-tuple-element.7.refs_1_, f32[64,4,160]{2,1,0:T(4,128)} %get-tuple-element.8.refs_2_), custom_call_target="tpu_custom_call" | custom-call | tf_op jit(solution)/shard_map/pallas_call | solution.py:989

commit v6 on v5

--- a/solution.py
+++ b/solution.py
@@ -481,10 +481,9 @@
     own(1, 3, True).start()
     own(0, 2, False).start()
     own(1, 0, False).start()
-    step2()
-    sent(tok, s_own.at[0])
     own(0, 3, False).start()
     own(1, 1, False).start()
+    step2()
     for c in range(2):
         arrived(g.at[left, chunk(c)], r_own.at[0, c])
         forward(0, c).start()
@@ -733,7 +732,7 @@
     pieces = ny * nz
     height = gwb.shape[2]
     half = height // 2
-    per_step = 512 // (2 * height)
+    per_step = 1024 // (2 * height)
     low_half, high_half = pl.ds(0, half), pl.ds(half, half)
 
     def pair(part, j):
@@ -746,7 +745,7 @@
         lo, up = lanes[part]
 
         def weight_step(i, carry):
-            at = pl.ds(pl.multiple_of(i * 512, 512), 512)
+            at = pl.ds(pl.multiple_of(i * 1024, 1024), 1024)
             whole = dot(gt[at, :], gp[:, lo:up]).astype(bf16)
             whole = whole.reshape(per_step, 2, height, up - lo)
             for q in range(per_step):
@@ -948,6 +947,7 @@
         sent(r1.at[e, pl.ds(0, ga - 1)], s1.at[e])
         sent(r2.at[e, pl.ds(0, gb - 1)], s2.at[e])
         sent(res.at[e, pl.ds(0, (ga - 1) * piece)], s3.at[e])
+    sent(tok, s_own.at[0])
     sent(tok, s_own.at[1])
 
     @pl.when(x == nx - 1)
@@ -961,26 +961,12 @@
 
 
 def hand_on_kernel(count, *refs):
-    srcs, dsts, held = refs[:count], refs[count : 2 * count], refs[2 * count : 3 * count]
-    come, leave = refs[3 * count :]
-    cuts = come.shape[1]
-
-    def slices(i, c):
-        size = srcs[i].shape[0] // cuts
-        at = pl.ds(c * size, size)
-        return (
-            pltpu.make_async_copy(srcs[i].at[at], held[i].at[at], come.at[i, c]),
-            pltpu.make_async_copy(held[i].at[at], dsts[i].at[at], leave.at[i, c]),
-        )
-
-    every = [slices(i, c) for c in range(cuts) for i in range(count)]
-    for first, _ in every:
-        first.start()
-    for first, second in every:
-        first.wait()
-        second.start()
-    for _, second in every:
-        second.wait()
+    srcs, dsts, sems = refs[:count], refs[count : 2 * count], refs[2 * count]
+    copies = [pltpu.make_async_copy(srcs[i], dsts[i], sems.at[i]) for i in range(count)]
+    for copy in copies:
+        copy.start()
+    for copy in copies:
+        copy.wait()
 
 
 def hand_on(*arrays):
@@ -991,9 +977,8 @@
         out_shape=tuple(jax.ShapeDtypeStruct(a.shape, a.dtype) for a in arrays),
         in_specs=[hbm] * count,
         out_specs=(hbm,) * count,
-        scratch_shapes=[pltpu.VMEM(a.shape, a.dtype) for a in arrays]
-        + [pltpu.SemaphoreType.DMA((count, 4))] * 2,
-        compiler_params=pltpu.CompilerParams(vmem_limit_bytes=60 * 2**20),
+        scratch_shapes=[pltpu.SemaphoreType.DMA((count,))],
+        compiler_params=pltpu.CompilerParams(vmem_limit_bytes=2**20),
     )(*arrays)
 
 
@@ -1020,9 +1005,9 @@
     att, gi, gw, _ = pl.pallas_call(
         functools.partial(kernel, nx, ny, nz, nh),
         out_shape=(
-            jax.ShapeDtypeStruct((every, nh * E), bf16),
-            jax.ShapeDtypeStruct((rows, depth), bf16),
-            jax.ShapeDtypeStruct((height, nh, CHAN), f32),
+            pltpu.VMEM((every, nh * E), bf16),
+            pltpu.VMEM((rows, depth), bf16),
+            pltpu.VMEM((height, nh, CHAN), f32),
             jax.ShapeDtypeStruct((nx - 1, width, depth), bf16),
         ),
         in_specs=[hbm] * 8,
@@ -1135,7 +1120,7 @@
             dma((2,)),
         ],
         compiler_params=pltpu.CompilerParams(
-            collective_id=0, has_side_effects=True, vmem_limit_bytes=62 * 2**20
+            collective_id=0, has_side_effects=True, vmem_limit_bytes=60 * 2**20
         ),
     )(tokens, wt, conv_kernel, grad_out, *consts)
     return hand_on(att, gi, gw)

time: 106 us -> 104 us (0.981)
  Pallas kernels: 104 us -> 102 us
    pallas_call x1, Pallas kernels: 2.54 us -> 1.42 us  [hand_on(): pl.pallas_call(functools.partial(hand_on_kernel, count), out_shape=tuple(...]
where the time goes in v6:
time: 104 us; the launch traced here: 103 us
  Pallas kernels  102 us (98%)
    pallas_call x1, Pallas kernels, local(): pl.pallas_call(functools.partial(kernel, nx, ny, nz, nh), out_shape=(pltp...  101 us

profile of v6, /device:TPU:0, one launch (start us, length us, event | category | flops | bytes accessed | tf_op | source)
XLA Modules:
  0.0 103.3 jit_solution(9279768128757419820)
XLA Ops:
  0.6 101.0 %shard_map.103 = (bf16[1024,512]{1,0:T(8,128)(2,1)S(1)}, bf16[256,2048]{1,0:T(8,128)(2,1)S(1)}, f32[64,4,160]{2,1,0:T(4,128)S(1)}, bf16[3,640,2048]{2,1,0:T(8,128)(2,1)}) custom-call(bf16[256,2048]{1,0:T(8,128)(2,1)} %tok.1, bf16[640,2048]{1,0:T(8,128)(2,1)} %bitcast.3, f32[3,4,160]{2,1,0:T(4,128)} %cv_hbm.1, bf16[1024,512]{1,0:T(8,128)(2,1)} %go.1, ...), custom_call_target="tpu_custom_call" | custom-call | tf_op jit(solution)/shard_map/pallas_call | solution.py:1005
  101.7 1.4 %shard_map.104 = (bf16[1024,512]{1,0:T(8,128)(2,1)}, bf16[256,2048]{1,0:T(8,128)(2,1)}, f32[64,4,160]{2,1,0:T(4,128)}) custom-call(bf16[1024,512]{1,0:T(8,128)(2,1)S(1)} %get-tuple-element.6.refs_0_, bf16[256,2048]{1,0:T(8,128)(2,1)S(1)} %get-tuple-element.7.refs_1_, f32[64,4,160]{2,1,0:T(4,128)S(1)} %get-tuple-element.8.refs_2_), custom_call_target="tpu_custom_call" | custom-call | tf_op jit(solution)/shard_map/pallas_call | solution.py:975

commit v7 on v6

--- a/solution.py
+++ b/solution.py
@@ -557,7 +557,7 @@
     for n in range(4):
         quarter(n, inside_raw)
 
-    ones = jnp.ones((2 * E, E), bf16)
+    ones = jnp.ones((E, E), bf16)
 
     def attend(group):
         for b in range(nb):
@@ -575,9 +575,7 @@
                 att_v[at] = mean.astype(bf16)
                 scaled = go_v[at].astype(f32) * inv
                 product = scaled * mean
-                high = product.astype(bf16)
-                low = (product - high.astype(f32)).astype(bf16)
-                slope = dot(jnp.concatenate([high, low], 1), ones) * (-1.0 / E)
+                slope = dot(product.astype(bf16), ones) * (-1.0 / E)
                 ga_b = jnp.concatenate([scaled.astype(bf16), slope.astype(bf16)], 1)
                 gna[i] = ga_b
                 nin[i, :, E:] = inv
@@ -857,13 +855,13 @@
     weight_third(0)
 
     steps = depth // 256
+    slots = wbuf.shape[0]
 
     def load(i, slot):
         at = pl.ds(pl.multiple_of(i * 256, 256), 256)
-        for j in range(nx):
-            src = w.at[:, at] if j == 0 else wf.at[j - 1, :, at]
+        for j in range(nx - 1):
             dst = wbuf.at[slot, pl.ds(j * width, width)]
-            pltpu.make_async_copy(src, dst, sw.at[slot]).start()
+            pltpu.make_async_copy(wf.at[j, :, at], dst, sw.at[slot]).start()
 
     def as_many(part, count):
         return gin.at[:, pl.ds(0, count * (lanes[part][1] - lanes[part][0]))]
@@ -873,8 +871,8 @@
         return pltpu.make_async_copy(gi_v.at[:, at], gi.at[:, at], s_gi)
 
     step6()
-    load(0, 0)
-    load(1, 1)
+    for slot in range(slots):
+        load(slot, slot)
     weight_second(2)
     gin[:, :width] = gp[rows_at(x), :]
     for part in range(3):
@@ -893,14 +891,15 @@
 
     def input_step(i, carry):
         at = pl.ds(pl.multiple_of(i * 256, 256), 256)
-        slot = i % 2
+        slot = i % slots
+        total = dot(gin[:, :width], w[:, at])
         pltpu.make_async_copy(wbuf.at[slot], wbuf.at[slot], sw.at[slot]).wait()
-        gi_v[:, at] = dot(gin[...], wbuf[slot]).astype(bf16)
+        gi_v[:, at] = (total + dot(gin[:, width:], wbuf[slot])).astype(bf16)
         gi_out(i).start()
 
-        @pl.when(i + 2 < steps)
+        @pl.when(i + slots < steps)
         def _():
-            load(i + 2, slot)
+            load(i + slots, slot)
 
         return carry
 
@@ -1048,7 +1047,7 @@
             pltpu.VMEM((4, gb, piece, E), bf16),
             pltpu.VMEM((4, ga, piece, E), bf16),
             pltpu.VMEM((4, ga * piece, E), bf16),
-            pltpu.VMEM((2, nx * width, 256), bf16),
+            pltpu.VMEM((3, (nx - 1) * width, 256), bf16),
             pltpu.VMEM((rows, nx * width), bf16),
             pltpu.VMEM((2, rows // 2, nh * E), bf16),
             pltpu.VMEM((nx, 16, width), bf16),
@@ -1076,7 +1075,7 @@
             dma((4,)),
             dma((4,)),
             dma((4,)),
-            dma((2,)),
+            dma((3,)),
             dma((2,)),
             dma((2, 2)),
             dma((2,)),

time: 104 us -> 103 us (level)
    pallas_call x1, Pallas kernels: 101 us -> 99.9 us  [local(): pl.pallas_call(functools.partial(kernel, nx, ny, nz, nh), out_shape=(pltp...]
where the time goes in v7:
time: 103 us; the launch traced here: 102 us
  Pallas kernels  101 us (98%)
    pallas_call x1, Pallas kernels, local(): pl.pallas_call(functools.partial(kernel, nx, ny, nz, nh), out_shape=(pltp...  99.9 us

profile of v7, /device:TPU:0, one launch (start us, length us, event | category | flops | bytes accessed | tf_op | source)
XLA Modules:
  0.0 102.1 jit_solution(14061186585395288197)
XLA Ops:
  0.6 99.9 %shard_map.103 = (bf16[1024,512]{1,0:T(8,128)(2,1)S(1)}, bf16[256,2048]{1,0:T(8,128)(2,1)S(1)}, f32[64,4,160]{2,1,0:T(4,128)S(1)}, bf16[3,640,2048]{2,1,0:T(8,128)(2,1)}) custom-call(bf16[256,2048]{1,0:T(8,128)(2,1)} %tok.1, bf16[640,2048]{1,0:T(8,128)(2,1)} %bitcast.3, f32[3,4,160]{2,1,0:T(4,128)} %cv_hbm.1, bf16[1024,512]{1,0:T(8,128)(2,1)} %go.1, ...), custom_call_target="tpu_custom_call" | custom-call | tf_op jit(solution)/shard_map/pallas_call | solution.py:1004
  100.5 1.4 %shard_map.104 = (bf16[1024,512]{1,0:T(8,128)(2,1)}, bf16[256,2048]{1,0:T(8,128)(2,1)}, f32[64,4,160]{2,1,0:T(4,128)}) custom-call(bf16[1024,512]{1,0:T(8,128)(2,1)S(1)} %get-tuple-element.6.refs_0_, bf16[256,2048]{1,0:T(8,128)(2,1)S(1)} %get-tuple-element.7.refs_1_, f32[64,4,160]{2,1,0:T(4,128)S(1)} %get-tuple-element.8.refs_2_), custom_call_target="tpu_custom_call" | custom-call | tf_op jit(solution)/shard_map/pallas_call | solution.py:974

commit v8 on v7

--- a/solution.py
+++ b/solution.py
@@ -1047,7 +1047,7 @@
             pltpu.VMEM((4, gb, piece, E), bf16),
             pltpu.VMEM((4, ga, piece, E), bf16),
             pltpu.VMEM((4, ga * piece, E), bf16),
-            pltpu.VMEM((3, (nx - 1) * width, 256), bf16),
+            pltpu.VMEM((4, (nx - 1) * width, 256), bf16),
             pltpu.VMEM((rows, nx * width), bf16),
             pltpu.VMEM((2, rows // 2, nh * E), bf16),
             pltpu.VMEM((nx, 16, width), bf16),
@@ -1075,7 +1075,7 @@
             dma((4,)),
             dma((4,)),
             dma((4,)),
-            dma((3,)),
+            dma((4,)),
             dma((2,)),
             dma((2, 2)),
             dma((2,)),

time: 103 us -> 103 us (level)
  no operation moved by 1% of the time
where the time goes in v8:
time: 103 us; the launch traced here: 102 us
  Pallas kernels  101 us (98%)
    pallas_call x1, Pallas kernels, local(): pl.pallas_call(functools.partial(kernel, nx, ny, nz, nh), out_shape=(pltp...  99.9 us

profile of v8, /device:TPU:0, one launch (start us, length us, event | category | flops | bytes accessed | tf_op | source)
XLA Modules:
  0.0 102.1 jit_solution(17096843981043362020)
XLA Ops:
  0.6 99.9 %shard_map.103 = (bf16[1024,512]{1,0:T(8,128)(2,1)S(1)}, bf16[256,2048]{1,0:T(8,128)(2,1)S(1)}, f32[64,4,160]{2,1,0:T(4,128)S(1)}, bf16[3,640,2048]{2,1,0:T(8,128)(2,1)}) custom-call(bf16[256,2048]{1,0:T(8,128)(2,1)} %tok.1, bf16[640,2048]{1,0:T(8,128)(2,1)} %bitcast.3, f32[3,4,160]{2,1,0:T(4,128)} %cv_hbm.1, bf16[1024,512]{1,0:T(8,128)(2,1)} %go.1, ...), custom_call_target="tpu_custom_call" | custom-call | tf_op jit(solution)/shard_map/pallas_call | solution.py:1004
  100.5 1.4 %shard_map.104 = (bf16[1024,512]{1,0:T(8,128)(2,1)}, bf16[256,2048]{1,0:T(8,128)(2,1)}, f32[64,4,160]{2,1,0:T(4,128)}) custom-call(bf16[1024,512]{1,0:T(8,128)(2,1)S(1)} %get-tuple-element.6.refs_0_, bf16[256,2048]{1,0:T(8,128)(2,1)S(1)} %get-tuple-element.7.refs_1_, f32[64,4,160]{2,1,0:T(4,128)S(1)} %get-tuple-element.8.refs_2_), custom_call_target="tpu_custom_call" | custom-call | tf_op jit(solution)/shard_map/pallas_call | solution.py:974
